TPU v7x, 32 devices: a whole 2x2x4 slice. The times are simulated.
32 devices in a mesh: section: 2 (over core), dp: 4 (over z), tensor: 4 (over y, x).
Axes of the slice: x: 2, y: 2, z: 4, core: 2. Of those that a mesh axis runs over, the one named last changes fastest.
Arguments:
- token_ids: int32 [8, 1024], P('dp'), may hold values from 0 to 30719
- targets: int32 [8, 1024], P('dp'), may hold values from 0 to 30719
- lengths: int32 [8, 4], P('dp'), may hold values from 1 to 4, 8 in all within a row
- embedding: bfloat16 [30720, 768], P('tensor'), may hold values from -0.25259074 to 0.25259074
- w_qkv: bfloat16 [2, 768, 3, 768], P('section', None, None, 'tensor'), may hold values from -0.21875 to 0.21875
- b_qv: float32 [2, 2, 768], P('section', None, 'tensor'), may hold values from -1.8 to 1.8
- w_out: bfloat16 [2, 768, 768], P('section', 'tensor'), may hold values from -3.5 to 3.5
- w_in: bfloat16 [2, 768, 3072], P('section', None, 'tensor'), may hold values from -0.21875 to 0.21875
- b_in: float32 [2, 3072], P('section', 'tensor'), may hold values from -1.8 to 1.8
- w_down: bfloat16 [2, 3072, 768], P('section', 'tensor'), may hold values from -0.109375 to 0.109375
- norm_gains: float32 [2, 2, 768], P('section'), may hold values from 0.5 to 1.5
- shifts: float32 [2, 4, 768], P('section'), may hold values from -1.8 to 1.8
- mask_logits: float32 [2, 12, 512, 512], P('section', 'tensor'), may hold values from -6 to 6
- mask_noise: float32 [2, 12, 512, 512], P('section', 'tensor'), may hold values from -6 to 6
Outputs:
- hidden_states: float32 [2, 8, 1024, 768], P('section', 'dp', 'tensor')
- grads_in: float32 [2, 8, 1024, 768], P('section', 'dp', 'tensor')
- d_embedding: float32 [30720, 768], P(('tensor', 'section', 'dp'))
- d_w_qkv: float32 [2, 768, 3, 768], P('section', None, None, 'tensor')
- d_b_qv: float32 [2, 2, 768], P('section', None, 'tensor')
- d_w_out: float32 [2, 768, 768], P('section', 'tensor')
- d_w_in: float32 [2, 768, 3072], P('section', None, 'tensor')
- d_b_in: float32 [2, 3072], P('section', 'tensor')
- d_w_down: float32 [2, 3072, 768], P('section', 'tensor')
- d_norm_gains: float32 [2, 2, 768], P('section')
- d_shifts: float32 [2, 4, 768], P('section')
- d_mask_logits: float32 [2, 12, 512, 512], P('section', 'tensor')
Inputs may be any that keep to these rules, and one draw needn't show every extreme that they name: Each row gives the lengths, in buckets of 128 tokens, of the 4 sequences of one micro-batch in order; each row sums to 8.
All inputs are finite; a program needn't handle non-finite values.
Results may differ from a plain program's by a relative error of at most 0.02.
The roundings to bfloat16 on the way count: a program that leaves them out, or rounds other values in their place, can miss the bound.
Values may be sent and summed in bfloat16 or wider, within the bound.
No kernel may reach another device: no remote copies, remote signals or barrier semaphores. Data moves between devices by JAX's collectives and lax.ppermute only.
A program may use at most 448 MiB of HBM per device.

v0:
```python
import jax
import jax.numpy as jnp
from jax import lax
from jax.sharding import PartitionSpec as P

MAXLEN = 512
BUCKET = 128
MB_TOK = 1024


EPSILON = 1e-12
LOSS_SCALE = 16.0


def joined(array, axis, combine):
    everything = jax.tree.map(lambda part: lax.all_gather(part, axis), array)
    first = jax.tree.map(lambda part: part[0], everything)

    def lap(k, so_far):
        return combine(so_far, jax.tree.map(lambda part: part[k], everything))

    return lax.fori_loop(1, lax.axis_size(axis), lap, first)


def passed_along(block, axis, distance):
    devices = range(lax.axis_size(axis))
    route = [(i - distance, i) for i in devices if i - distance in devices]
    return lax.ppermute(block, axis, route)


def times(left, right):
    return jnp.dot(left, right, preferred_element_type=jnp.float32)


def times_left(left, right):
    return lax.dot_general(
        left, right, (((0,), (0,)), ((), ())), preferred_element_type=jnp.float32
    )


def times_right(left, right):
    return lax.dot_general(
        left, right, (((1,), (1,)), ((), ())), preferred_element_type=jnp.float32
    )


def gather_rows(shard):
    return lax.all_gather(shard, "tensor", axis=0, tiled=True)


def sum_rows(work, shard_rows):
    return lax.psum_scatter(
        work(jnp.int32(0), shard_rows * lax.axis_size("tensor")),
        "tensor",
        scatter_dimension=0,
        tiled=True,
    )


def merge_stats(first_pair, second_pair):
    row_max = jnp.maximum(first_pair[0], second_pair[0])
    row_total = first_pair[1] * jnp.exp(first_pair[0] - row_max) + second_pair[1] * jnp.exp(
        second_pair[0] - row_max
    )
    return (row_max, row_total)


def norm_forward(value_in, gain, shift):
    row_mean = jnp.mean(value_in, axis=-1, keepdims=True)
    centered = value_in - row_mean
    row_scale = lax.rsqrt(jnp.mean(centered * centered, axis=-1, keepdims=True) + EPSILON)
    normed = centered * row_scale
    return (normed * gain + shift, normed, row_scale)


def norm_backward(grad_out, normed, row_scale, gain):
    scaled_grad = grad_out * gain
    grad_in = row_scale * (
        scaled_grad
        - jnp.mean(scaled_grad, axis=-1, keepdims=True)
        - normed * jnp.mean(scaled_grad * normed, axis=-1, keepdims=True)
    )
    return (grad_in, jnp.sum(grad_out * normed, axis=0), jnp.sum(grad_out, axis=0))


def slot_layout(seq_units):
    seq_lens = seq_units * BUCKET
    starts = jnp.cumsum(seq_lens) - seq_lens
    position = jnp.arange(MAXLEN, dtype=jnp.int32)
    gather_index = jnp.minimum(starts[:, None] + position[None, :], MB_TOK - 1)
    valid_keys = position[None, :] < seq_lens[:, None]
    token_pos = jnp.arange(MB_TOK, dtype=jnp.int32)
    owner = jnp.sum((token_pos[:, None] >= starts[None, :]).astype(jnp.int32), axis=1) - 1
    owner_hit = owner[:, None] == jnp.arange(seq_units.shape[0], dtype=jnp.int32)[None, :]
    offset = token_pos - jnp.sum(jnp.where(owner_hit, starts[None, :], 0), axis=1)
    return (gather_index, valid_keys, owner * MAXLEN + offset)


def split_heads(projected, gather_index, valid_keys, head_count):
    padded = jnp.where(
        valid_keys[:, :, None, None], projected[gather_index], jnp.zeros((), projected.dtype)
    )
    padded = padded.reshape(gather_index.shape[0], MAXLEN, 3, head_count, -1)
    return (padded[:, :, 0], padded[:, :, 1], padded[:, :, 2])


def attention_probs(queries, key_rows, valid_keys):
    scores = jnp.einsum("sqhe,skhe->shqk", queries, key_rows, preferred_element_type=jnp.float32)
    scores = scores * queries.shape[-1] ** (-0.5)
    scores = jnp.where(valid_keys[:, None, None, :], scores, -1e30)
    return jax.nn.softmax(scores, axis=-1)


def layer_forward(layer_in, seq_units, weights):
    w_qkv, b_qv, w_out, w_in, b_in, w_down, gains, shifts, gate_probs = weights
    gather_index, valid_keys, back_index = slot_layout(seq_units)
    shard_rows = layer_in.shape[0]
    head_width = w_qkv.shape[2]
    x_rows = gather_rows(layer_in.astype(jnp.bfloat16))
    projected = times(x_rows, w_qkv.reshape(w_qkv.shape[0], 3 * head_width)).reshape(
        -1, 3, head_width
    )
    qkv_bias = jnp.stack([b_qv[0], jnp.zeros_like(b_qv[0]), b_qv[1]])
    projected = (projected + qkv_bias).astype(jnp.bfloat16)
    queries, key_rows, values = split_heads(
        projected, gather_index, valid_keys, gate_probs.shape[0]
    )
    attention = attention_probs(queries, key_rows, valid_keys)
    mixed_probs = (attention * gate_probs[None]).astype(jnp.bfloat16)
    context = jnp.einsum("shqk,skhe->sqhe", mixed_probs, values, preferred_element_type=jnp.float32)
    context = context.astype(jnp.bfloat16).reshape(-1, head_width)[back_index]

    def attend_out(anchor, amount):
        return times(context, w_out)

    residual = layer_in + sum_rows(attend_out, shard_rows) + shifts[0]
    hidden, normed_one, scale_one = norm_forward(residual, gains[0], shifts[1])
    h_rows = gather_rows(hidden.astype(jnp.bfloat16))
    pre_act = times(h_rows, w_in) + b_in
    activated = jax.nn.gelu(pre_act, approximate=False).astype(jnp.bfloat16)

    def feed_out(anchor, amount):
        return times(activated, w_down)

    output, normed_two, scale_two = norm_forward(
        hidden + sum_rows(feed_out, shard_rows) + shifts[2], gains[1], shifts[3]
    )
    saved = (
        x_rows,
        projected,
        context,
        normed_one,
        scale_one,
        h_rows,
        pre_act,
        activated,
        normed_two,
        scale_two,
    )
    return (output, saved)


def layer_backward(grad_out, seq_units, weights, saved):
    w_qkv, b_qv, w_out, w_in, b_in, w_down, gains, shifts, gate_probs = weights
    (
        x_rows,
        projected,
        context,
        normed_one,
        scale_one,
        h_rows,
        pre_act,
        activated,
        normed_two,
        scale_two,
    ) = saved
    gather_index, valid_keys, back_index = slot_layout(seq_units)
    shard_rows = grad_out.shape[0]
    head_width = w_qkv.shape[2]
    head_count = gate_probs.shape[0]
    w_flat = w_qkv.reshape(w_qkv.shape[0], 3 * head_width)
    d_sum_two, d_gain_two, d_shift_two = norm_backward(grad_out, normed_two, scale_two, gains[1])
    d_feed_rows = gather_rows(d_sum_two.astype(jnp.bfloat16))
    d_w_down = times_left(activated, d_feed_rows)
    d_act = times_right(d_feed_rows, w_down)
    gelu_pull = jax.vjp(lambda value_in: jax.nn.gelu(value_in, approximate=False), pre_act)[1]
    d_pre = gelu_pull(d_act)[0].astype(jnp.bfloat16)
    d_w_in = times_left(h_rows, d_pre)
    d_b_in = jnp.sum(d_pre.astype(jnp.float32), axis=0)

    def feed_back(anchor, amount):
        return times_right(d_pre, w_in)

    d_hidden = sum_rows(feed_back, shard_rows) + d_sum_two
    d_sum_one, d_gain_one, d_shift_one = norm_backward(d_hidden, normed_one, scale_one, gains[0])
    d_attn_rows = gather_rows(d_sum_one.astype(jnp.bfloat16))
    d_w_out = times_left(context, d_attn_rows)
    d_context = times_right(d_attn_rows, w_out).astype(jnp.bfloat16)
    queries, key_rows, values = split_heads(projected, gather_index, valid_keys, head_count)
    d_padded = jnp.where(
        valid_keys[:, :, None], d_context[gather_index], jnp.zeros((), jnp.bfloat16)
    )
    d_padded = d_padded.reshape(gather_index.shape[0], MAXLEN, head_count, -1)
    attention = attention_probs(queries, key_rows, valid_keys)
    d_mixed = jnp.einsum("sqhe,skhe->shqk", d_padded, values, preferred_element_type=jnp.float32)
    d_prob = d_mixed * gate_probs[None]
    d_gate = jnp.sum(d_mixed * attention, axis=0)
    d_scores = (attention * (d_prob - jnp.sum(d_prob * attention, axis=-1, keepdims=True))).astype(
        jnp.bfloat16
    )
    mixed_probs = (attention * gate_probs[None]).astype(jnp.bfloat16)
    head_scale = queries.shape[-1] ** (-0.5)
    d_queries = (
        jnp.einsum("shqk,skhe->sqhe", d_scores, key_rows, preferred_element_type=jnp.float32)
        * head_scale
    )
    d_keys = (
        jnp.einsum("shqk,sqhe->skhe", d_scores, queries, preferred_element_type=jnp.float32)
        * head_scale
    )
    d_values = jnp.einsum(
        "shqk,sqhe->skhe", mixed_probs, d_padded, preferred_element_type=jnp.float32
    )
    d_projected = jnp.stack([d_queries, d_keys, d_values], axis=2).reshape(-1, 3, head_width)[
        back_index
    ]
    d_projected = d_projected.astype(jnp.bfloat16)
    d_flat = d_projected.reshape(-1, 3 * head_width)
    d_w_qkv = times_left(x_rows, d_flat).reshape(w_qkv.shape)
    d_proj_sums = jnp.sum(d_projected.astype(jnp.float32), axis=0)
    d_b_qv = jnp.stack([d_proj_sums[0], d_proj_sums[2]])

    def qkv_back(anchor, amount):
        return times_right(d_flat, w_flat)

    d_layer_in = sum_rows(qkv_back, shard_rows) + d_sum_one
    d_gains = jnp.stack([d_gain_one, d_gain_two])
    d_shifts = jnp.stack(
        [jnp.sum(d_sum_one, axis=0), d_shift_one, jnp.sum(d_sum_two, axis=0), d_shift_two]
    )
    terms = (d_w_qkv, d_b_qv, d_w_out, d_w_in, d_b_in, d_w_down, d_gains, d_shifts, d_gate)
    return (d_layer_in, terms)


def shards(
    token_ids,
    targets,
    lengths,
    embedding,
    w_qkv,
    b_qv,
    w_out,
    w_in,
    b_in,
    w_down,
    norm_gains,
    shifts,
    mask_logits,
    mask_noise,
):
    section_index = lax.axis_index("section")
    first_section = section_index == 0
    last_section = section_index == 1
    micro_count = token_ids.shape[0]
    token_count = token_ids.shape[1]
    shard_rows = token_count // lax.axis_size("tensor")
    model_width = embedding.shape[1]
    vocab_rows = embedding.shape[0]
    vocab_start = lax.axis_index("tensor") * vocab_rows
    scale_in = model_width**0.5
    gate_probs = jax.nn.sigmoid(mask_logits[0] + mask_noise[0])
    weights = (
        w_qkv[0],
        b_qv[0],
        w_out[0],
        w_in[0],
        b_in[0],
        w_down[0],
        norm_gains[0],
        shifts[0],
        gate_probs,
    )
    vocab_iota = jnp.arange(vocab_rows, dtype=jnp.int32)
    zero_rows = jnp.zeros((shard_rows, model_width), jnp.float32)
    incoming = zero_rows
    layer_inputs = []
    layer_outputs = []
    saved_all = []
    head_grads = [zero_rows]
    d_embedding = jnp.zeros((vocab_rows, model_width), jnp.float32)
    for moment in range(micro_count + 1):
        if moment < micro_count:
            embed_local_ids = token_ids[moment] - vocab_start
            embed_in_block = (embed_local_ids >= 0) & (embed_local_ids < vocab_rows)
            safe_ids = jnp.clip(embed_local_ids, 0, vocab_rows - 1)

            def lookup(anchor, amount):
                return jnp.where(
                    embed_in_block[:, None], embedding[safe_ids].astype(jnp.float32), 0.0
                )

            layer_in = jnp.where(first_section, sum_rows(lookup, shard_rows) * scale_in, incoming)
        else:
            layer_in = incoming
        seq_units = jnp.where(
            first_section, lengths[min(moment, micro_count - 1)], lengths[max(moment - 1, 0)]
        )
        layer_out, saved = layer_forward(layer_in, seq_units, weights)
        layer_inputs.append(layer_in)
        layer_outputs.append(layer_out)
        saved_all.append(saved)
        if moment > 0:
            final_rows = gather_rows(layer_out.astype(jnp.bfloat16))
            target_hits = (targets[moment - 1] - vocab_start)[:, None] == vocab_iota[None, :]

            def vocab_logits(source):
                logits = times_right(source, embedding)
                row_max = jnp.max(logits, axis=-1)
                row_total = jnp.sum(jnp.exp(logits - row_max[:, None]), axis=-1)
                return (logits, row_max, row_total)

            def vocab_skipped(source):
                return (
                    jnp.zeros((source.shape[0], vocab_rows), jnp.float32),
                    jnp.zeros((source.shape[0],), jnp.float32),
                    jnp.ones((source.shape[0],), jnp.float32),
                )

            logits, row_max, row_total = lax.cond(
                last_section, vocab_logits, vocab_skipped, final_rows
            )
            row_max, row_total = joined((row_max, row_total), "tensor", merge_stats)
            spread = row_max + jnp.log(row_total)

            def head_terms(logit_block, spread_rows, source):
                probs_vocab = jnp.exp(logit_block - spread_rows[:, None])
                d_logits = (LOSS_SCALE * (probs_vocab - target_hits.astype(jnp.float32))).astype(
                    jnp.bfloat16
                )
                return (d_logits, times_left(d_logits, source))

            def head_none(logit_block, spread_rows, source):
                return (
                    jnp.zeros(logit_block.shape, jnp.bfloat16),
                    jnp.zeros((vocab_rows, model_width), jnp.float32),
                )

            d_logits, d_head = lax.cond(
                last_section, head_terms, head_none, logits, spread, final_rows
            )

            def project(anchor, amount):
                return lax.cond(
                    last_section,
                    lambda block_rows: times(block_rows, embedding),
                    lambda block_rows: jnp.zeros((block_rows.shape[0], model_width), jnp.float32),
                    d_logits,
                )

            d_final, d_head = (sum_rows(project, shard_rows), d_head)
            head_grads.append(d_final)
            d_embedding = d_embedding + d_head
        if moment < micro_count:
            incoming = passed_along(layer_out, "section", 1)
    totals = None
    back_in = zero_rows
    grads_list = []
    for back_step in range(micro_count + 1):
        grad_top = head_grads[back_step + 1] if back_step < micro_count else zero_rows
        grad_here = jnp.where(first_section, back_in, grad_top)
        low_tick = max(back_step - 1, 0)
        high_tick = min(back_step + 1, micro_count)
        seq_units = jnp.where(
            first_section,
            lengths[min(low_tick, micro_count - 1)],
            lengths[min(back_step, micro_count - 1)],
        )
        saved = jax.tree.map(
            lambda low_v, high_v: jnp.where(first_section, low_v, high_v),
            saved_all[low_tick],
            saved_all[high_tick],
        )
        d_layer_in, terms = layer_backward(grad_here, seq_units, weights, saved)
        totals = (
            terms
            if totals is None
            else jax.tree.map(lambda left, right: left + right, totals, terms)
        )
        grads_list.append(d_layer_in)
        if back_step > 0:
            sent_rows = gather_rows(d_layer_in.astype(jnp.bfloat16)).astype(jnp.float32) * scale_in
            local_ids = token_ids[back_step - 1] - vocab_start
            in_block = (local_ids >= 0) & (local_ids < vocab_rows) & first_section
            d_embedding = d_embedding.at[jnp.clip(local_ids, 0, vocab_rows - 1)].add(
                jnp.where(in_block[:, None], sent_rows, 0.0)
            )
        if back_step < micro_count:
            back_in = passed_along(d_layer_in, "section", -1)
    g_qkv, g_bqv, g_out, g_in, g_bin, g_down, g_gains, g_shifts, g_gate = totals
    g_mask = g_gate * gate_probs * (1.0 - gate_probs)
    g_gains, g_shifts = lax.psum((g_gains, g_shifts), "tensor")
    g_qkv, g_bqv, g_out, g_in, g_bin, g_down, g_mask, g_gains, g_shifts = lax.psum(
        (g_qkv, g_bqv, g_out, g_in, g_bin, g_down, g_mask, g_gains, g_shifts), "dp"
    )
    d_embed_out = lax.psum_scatter(d_embedding, ("section", "dp"), scatter_dimension=0, tiled=True)
    hidden_out = jnp.stack(
        [
            jnp.where(first_section, layer_outputs[index_m], layer_outputs[index_m + 1])
            for index_m in range(micro_count)
        ]
    )
    grads_out = jnp.stack(
        [
            jnp.where(first_section, grads_list[index_m + 1], grads_list[index_m])
            for index_m in range(micro_count)
        ]
    )
    return (
        hidden_out[None],
        grads_out[None],
        d_embed_out,
        g_qkv[None],
        g_bqv[None],
        g_out[None],
        g_in[None],
        g_bin[None],
        g_down[None],
        g_gains[None],
        g_shifts[None],
        g_mask[None],
    )


def solution(mesh):
    placed = (
        P("dp", None),
        P("dp", None),
        P("dp", None),
        P("tensor", None),
        P("section", None, None, "tensor"),
        P("section", None, "tensor"),
        P("section", "tensor", None),
        P("section", None, "tensor"),
        P("section", "tensor"),
        P("section", "tensor", None),
        P("section", None, None),
        P("section", None, None),
        P("section", "tensor", None, None),
        P("section", "tensor", None, None),
    )
    return jax.shard_map(
        shards,
        mesh=mesh,
        in_specs=placed,
        out_specs=(
            P("section", "dp", "tensor", None),
            P("section", "dp", "tensor", None),
            P(("tensor", "section", "dp"), None),
            P("section", None, None, "tensor"),
            P("section", None, "tensor"),
            P("section", "tensor", None),
            P("section", None, "tensor"),
            P("section", "tensor"),
            P("section", "tensor", None),
            P("section", None, None),
            P("section", None, None),
            P("section", "tensor", None, None),
        ),
        check_vma=False,
    )
```

profile of v0, /device:TPU:17, one launch (start us, length us, event | category | flops | bytes accessed | tf_op | source)
XLA Modules:
  0.0 2877.6 jit_solution(12525973565593835591)
XLA Ops:
  31.9 35.7 %reduce-scatter.18.cloned.1.call-done = f32[256,768]{1,0:T(8,128)} async-done(((f32[1024,768]{1,0:T(8,128)}), f32[256,768]{1,0:T(8,128)}) %reduce-scatter.18.cloned.1.call-update) | async-done | bytes 786448 | tf_op jit(solution)/shard_map/reduce_scatter | solution.py:52
  77.0 24.0 all-gather.21.cloned.1.call-done
  107.4 16.7 gather_fusion.1
  160.0 43.4 %reduce-scatter.20.cloned.1.call-done = f32[256,768]{1,0:T(8,128)} async-done(((f32[1024,768]{1,0:T(8,128)}), f32[256,768]{1,0:T(8,128)}) %reduce-scatter.20.cloned.1.call-update) | async-done | bytes 786448 | tf_op jit(solution)/shard_map/reduce_scatter | solution.py:52
  206.6 30.5 %all-gather.23.cloned.1.call-done = bf16[1024,768]{1,0:T(8,128)(2,1)} async-done(((bf16[256,768]{1,0:T(8,128)(2,1)}), bf16[1024,768]{1,0:T(8,128)(2,1)}) %all-gather.23.cloned.1.call-update) | async-done | bytes 1572880 | tf_op jit(solution)/shard_map/all_gather | solution.py:48
  252.6 10.8 gather_fusion.3
  266.1 29.4 %reduce-scatter.22.cloned.1.call-done = f32[256,768]{1,0:T(8,128)} async-done(((f32[1024,768]{1,0:T(8,128)}), f32[256,768]{1,0:T(8,128)}) %reduce-scatter.22.cloned.1.call-update) | async-done | bytes 786448 | tf_op jit(solution)/shard_map/reduce_scatter | solution.py:52
  299.4 42.9 %reduce-scatter.24.cloned.1.call-done = f32[256,768]{1,0:T(8,128)} async-done(((f32[1024,768]{1,0:T(8,128)}), f32[256,768]{1,0:T(8,128)}) %reduce-scatter.24.cloned.1.call-update) | async-done | bytes 786448 | tf_op jit(solution)/shard_map/reduce_scatter | solution.py:52
  346.5 29.2 %all-gather.25.cloned.1.call-done = bf16[1024,768]{1,0:T(8,128)(2,1)} async-done(((bf16[256,768]{1,0:T(8,128)(2,1)}), bf16[1024,768]{1,0:T(8,128)(2,1)}) %all-gather.25.cloned.1.call-update) | async-done | bytes 1572880 | tf_op jit(solution)/shard_map/all_gather | solution.py:48
  382.3 16.7 gather_fusion.4
  434.9 44.0 %reduce-scatter.26.cloned.1.call-done = f32[256,768]{1,0:T(8,128)} async-done(((f32[1024,768]{1,0:T(8,128)}), f32[256,768]{1,0:T(8,128)}) %reduce-scatter.26.cloned.1.call-update) | async-done | bytes 786448 | tf_op jit(solution)/shard_map/reduce_scatter | solution.py:52
  481.8 30.8 %all-gather.27.cloned.1.call-done = bf16[1024,768]{1,0:T(8,128)(2,1)} async-done(((bf16[256,768]{1,0:T(8,128)(2,1)}), bf16[1024,768]{1,0:T(8,128)(2,1)}) %all-gather.27.cloned.1.call-update) | async-done | bytes 1572880 | tf_op jit(solution)/shard_map/all_gather | solution.py:48
  528.2 44.0 %reduce-scatter.28.cloned.1.call-done = f32[256,768]{1,0:T(8,128)} async-done(((f32[1024,768]{1,0:T(8,128)}), f32[256,768]{1,0:T(8,128)}) %reduce-scatter.28.cloned.1.call-update) | async-done | bytes 786448 | tf_op jit(solution)/shard_map/reduce_scatter | solution.py:52
  581.8 30.2 %all-gather.29.cloned.1.call-done = bf16[1024,768]{1,0:T(8,128)(2,1)} async-done(((bf16[256,768]{1,0:T(8,128)(2,1)}), bf16[1024,768]{1,0:T(8,128)(2,1)}) %all-gather.29.cloned.1.call-update) | async-done | bytes 1572880 | tf_op jit(solution)/shard_map/all_gather | solution.py:48
  620.3 16.7 gather_fusion.6
  648.4 16.7 gather_fusion.14
  708.6 43.6 %reduce-scatter.30.cloned.1.call-done = f32[256,768]{1,0:T(8,128)} async-done(((f32[1024,768]{1,0:T(8,128)}), f32[256,768]{1,0:T(8,128)}) %reduce-scatter.30.cloned.1.call-update) | async-done | bytes 786448 | tf_op jit(solution)/shard_map/reduce_scatter | solution.py:52
  756.5 30.5 %all-gather.31.cloned.1.call-done = bf16[1024,768]{1,0:T(8,128)(2,1)} async-done(((bf16[256,768]{1,0:T(8,128)(2,1)}), bf16[1024,768]{1,0:T(8,128)(2,1)}) %all-gather.31.cloned.1.call-update) | async-done | bytes 1572880 | tf_op jit(solution)/shard_map/all_gather | solution.py:48
  801.2 19.0 all-gather.33.cloned.1.call-done
  820.3 35.7 %conditional.6 = (f32[1024,7680]{1,0:T(8,128)}, f32[1024]{0:T(1024)}, f32[1024]{0:T(1024)S(1)}) conditional(s32[]{:T(128)} %convert_element_type.261, () %tuple.98, (bf16[1024,768]{1,0:T(8,128)(2,1)}, bf16[7680,768]{1,0:T(8,128)(2,1)}) %tuple.99), branch_computations={%region_40.41_spmd, %region_41.44_spmd} | conditional | flops 12103186432 | bytes 76296216 | solution.py:329
  820.4 22.2 fusion.309
  842.7 13.3 exponential_reduce_fusion
  868.8 14.3 eq.119
  883.1 46.4 %conditional.7 = (bf16[1024,7680]{1,0:T(8,128)(2,1)}, f32[7680,768]{1,0:T(8,128)}) conditional(s32[]{:T(128)} %convert_element_type.261, () %tuple.97, (f32[1024]{0:T(1024)S(1)}, f32[1024]{0:T(1024)S(1)}, f32[1024,7680]{1,0:T(8,128)}, s32[2,1024]{1,0:T(2,128)S(1)}, s32[1024,1]{0,1:T(1,128)S(1)}, /*index=5*/s32[1024,7680]{1,0:T(8,128)}, ...), branch_computations={%region_46.47_spmd, %region_47.48_spmd} | conditional | flops 12126783488 | bytes 119570448 | solution.py:348
  883.4 25.8 multiply_convert_fusion
  909.2 20.3 fusion.322
  929.5 18.1 conditional.8
  929.5 18.1 fusion.320
  952.0 39.3 %reduce-scatter.34.cloned.1.call-done = f32[256,768]{1,0:T(8,128)} async-done(((f32[1024,768]{1,0:T(8,128)}), f32[256,768]{1,0:T(8,128)}) %reduce-scatter.34.cloned.1.call-update) | async-done | bytes 786448 | tf_op jit(solution)/shard_map/reduce_scatter | solution.py:52
  997.4 30.8 %all-gather.35.cloned.1.call-done = bf16[1024,768]{1,0:T(8,128)(2,1)} async-done(((bf16[256,768]{1,0:T(8,128)(2,1)}), bf16[1024,768]{1,0:T(8,128)(2,1)}) %all-gather.35.cloned.1.call-update) | async-done | bytes 1572880 | tf_op jit(solution)/shard_map/all_gather | solution.py:48
  1028.2 11.3 convert_reduce_fusion.5
  1044.0 44.1 %reduce-scatter.36.cloned.1.call-done = f32[256,768]{1,0:T(8,128)} async-done(((f32[1024,768]{1,0:T(8,128)}), f32[256,768]{1,0:T(8,128)}) %reduce-scatter.36.cloned.1.call-update) | async-done | bytes 786448 | tf_op jit(solution)/shard_map/reduce_scatter | solution.py:52
  1096.6 16.7 gather_fusion.9
  1144.2 14.1 multiply_reduce_fusion.2
  1231.5 35.7 %conditional.9 = (f32[1024,7680]{1,0:T(8,128)}, f32[1024]{0:T(1024)}, f32[1024]{0:T(1024)S(1)}) conditional(s32[]{:T(128)} %convert_element_type.261, () %tuple.105, (bf16[1024,768]{1,0:T(8,128)(2,1)}, bf16[7680,768]{1,0:T(8,128)(2,1)}) %tuple.106), branch_computations={%region_58.59_spmd, %region_59.62_spmd} | conditional | flops 12103186432 | bytes 76296216 | solution.py:329
  1231.5 22.0 fusion.310
  1253.6 13.7 exponential_reduce_fusion.1
  1280.0 14.3 eq.120
  1294.3 46.5 %conditional.10 = (bf16[1024,7680]{1,0:T(8,128)(2,1)}, f32[7680,768]{1,0:T(8,128)}) conditional(s32[]{:T(128)} %convert_element_type.261, () %tuple.104, (f32[1024]{0:T(1024)S(1)}, f32[1024]{0:T(1024)S(1)}, f32[1024,7680]{1,0:T(8,128)}, s32[2,1024]{1,0:T(2,128)S(1)}, s32[1024,1]{0,1:T(1,128)S(1)}, /*index=5*/s32[1024,7680]{1,0:T(8,128)}, ...), branch_computations={%region_64.65_spmd, %region_65.66_spmd} | conditional | flops 12126783488 | bytes 119570448 | solution.py:348
  1294.5 25.8 multiply_convert_fusion.1
  1320.3 20.4 fusion.323
  1340.7 18.1 conditional.11
  1340.7 18.1 fusion.321
  1364.3 38.2 %reduce-scatter.40.cloned.1.call-done = f32[256,768]{1,0:T(8,128)} async-done(((f32[1024,768]{1,0:T(8,128)}), f32[256,768]{1,0:T(8,128)}) %reduce-scatter.40.cloned.1.call-update) | async-done | bytes 786448 | tf_op jit(solution)/shard_map/reduce_scatter | solution.py:52
  1408.5 30.6 %all-gather.41.cloned.1.call-done = bf16[1024,768]{1,0:T(8,128)(2,1)} async-done(((bf16[256,768]{1,0:T(8,128)(2,1)}), bf16[1024,768]{1,0:T(8,128)(2,1)}) %all-gather.41.cloned.1.call-update) | async-done | bytes 1572880 | tf_op jit(solution)/shard_map/all_gather | solution.py:48
  1439.1 12.1 convert_reduce_fusion.4
  1458.2 41.4 %reduce-scatter.42.cloned.1.call-done = f32[256,768]{1,0:T(8,128)} async-done(((f32[1024,768]{1,0:T(8,128)}), f32[256,768]{1,0:T(8,128)}) %reduce-scatter.42.cloned.1.call-update) | async-done | bytes 786448 | tf_op jit(solution)/shard_map/reduce_scatter | solution.py:52
  1510.4 18.3 gather_fusion.8
  1572.7 12.8 multiply_reduce_fusion.1
  1642.5 10.8 gather_fusion.13
  1662.1 44.0 %reduce-scatter.44.cloned.1.call-done = f32[256,768]{1,0:T(8,128)} async-done(((f32[1024,768]{1,0:T(8,128)}), f32[256,768]{1,0:T(8,128)}) %reduce-scatter.44.cloned.1.call-update) | async-done | bytes 786448 | tf_op jit(solution)/shard_map/reduce_scatter | solution.py:52
  1717.2 30.7 %all-gather.45.cloned.1.call-done = bf16[1024,768]{1,0:T(8,128)(2,1)} async-done(((bf16[256,768]{1,0:T(8,128)(2,1)}), bf16[1024,768]{1,0:T(8,128)(2,1)}) %all-gather.45.cloned.1.call-update) | async-done | bytes 1572880 | tf_op jit(solution)/shard_map/all_gather | solution.py:48
  1748.0 12.1 convert_reduce_fusion.3
  1764.4 44.0 %reduce-scatter.46.cloned.1.call-done = f32[256,768]{1,0:T(8,128)} async-done(((f32[1024,768]{1,0:T(8,128)}), f32[256,768]{1,0:T(8,128)}) %reduce-scatter.46.cloned.1.call-update) | async-done | bytes 786448 | tf_op jit(solution)/shard_map/reduce_scatter | solution.py:52
  1822.9 22.4 all-gather.47.cloned.1.call-done
  1856.5 13.8 multiply_reduce_fusion
  1964.4 19.1 reduce-scatter.48.cloned.1.call-done
  2005.8 24.2 add.831
  2030.0 24.0 scatter_custom_fusion
  2054.1 24.9 scatter_custom_fusion.1
  2085.5 12.5 all-reduce
  2099.1 22.1 all-reduce.1
  2123.8 282.8 %all-reduce.5.cloned.1.call-done = (f32[1,768,3,192]{1,3,2,0:T(8,128)}, f32[1,192,768]{2,1,0:T(8,128)}, f32[1,768,768]{2,1,0:T(8,128)}, f32[1,768,768]{2,1,0:T(8,128)}, f32[1,3,512,512]{2,3,1,0:T(8,128)}) async-done(((f32[1,768,3,192]{1,3,2,0:T(8,128)}, f32[1,192,768]{2,1,0:T(8,128)}, f32[1,768,768]{2,1,0:T(8,128)}, f32[1,768,768]{2,1,0:T(8,128)}, f32[1,3,512,512]{2,3,1,0:T(8,128)}), ...) | async-done | bytes 10223632 | tf_op jit(solution)/shard_map/psum | solution.py:402
  2410.1 453.9 %reduce-scatter.50.cloned.1.call-done = f32[960,768]{1,0:T(8,128)} async-done(((f32[7680,768]{1,0:T(8,128)}), f32[960,768]{1,0:T(8,128)}) %reduce-scatter.50.cloned.1.call-update) | async-done | bytes 2949136 | tf_op jit(solution)/shard_map/reduce_scatter | solution.py:405
  (865 shorter events, 725.1 us)
Async XLA Ops:
  7.2 229.9 %copy-start = (bf16[1,768,768]{2,1,0:T(8,128)(2,1)S(1)}, bf16[1,768,768]{2,1,0:T(8,128)(2,1)}, u32[]{:S(2)}) copy-start(bf16[1,768,768]{2,1,0:T(8,128)(2,1)} %param.37) | copy-start | bytes 3538948
  7.2 60.4 %reduce-scatter.18.cloned.1.call-start = ((), (), s32[]{:S(2)}) async-start(), calls=%async_computation.17 | async-start | bytes 3932160 | tf_op jit(solution)/shard_map/reduce_scatter | solution.py:52
  22.4 78.6 %all-gather.21.cloned.1.call-start = ((), (), s32[]{:S(2)}) async-start(), calls=%async_computation.18 | async-start | bytes 1966080 | tf_op jit(solution)/shard_map/all_gather | solution.py:48
  69.6 133.8 %reduce-scatter.20.cloned.1.call-start = ((), (), s32[]{:S(2)}) async-start(), calls=%async_computation.19 | async-start | bytes 3932160 | tf_op jit(solution)/shard_map/reduce_scatter | solution.py:52
  71.5 63.8 %copy-start.122 = (pred[4,512]{1,0:T(4,128)(4,1)}, pred[4,512]{1,0:T(4,128)(4,1)S(1)}, u32[]{:S(2)}) copy-start(pred[4,512]{1,0:T(4,128)(4,1)S(1)} %get-tuple-element.616) | copy-start | bytes 6148
  71.5 80.4 %copy-start.120 = (s32[1024]{0:T(1024)}, s32[1024]{0:T(1024)S(1)}, u32[]{:S(2)}) copy-start(s32[1024]{0:T(1024)S(1)} %broadcast_clamp_fusion.7) | copy-start | bytes 12292
  159.3 77.8 %all-gather.23.cloned.1.call-start = ((), (), s32[]{:S(2)}) async-start(), calls=%async_computation.20 | async-start | bytes 1966080 | tf_op jit(solution)/shard_map/all_gather | solution.py:48
  159.4 414.6 %copy-start.90 = (f32[768]{0:T(1024)}, f32[768]{0:T(1024)S(1)}, u32[]{:S(2)}) copy-start(f32[768]{0:T(1024)S(1)} %get-tuple-element.450) | copy-start | bytes 9220
  159.4 595.0 %copy-start.86 = (f32[768]{0:T(1024)}, f32[768]{0:T(1024)S(1)}, u32[]{:S(2)}) copy-start(f32[768]{0:T(1024)S(1)} %get-tuple-element.451) | copy-start | bytes 9220
  160.0 87.0 %copy-start.102 = (f32[768]{0:T(1024)}, f32[768]{0:T(1024)S(1)}, u32[]{:S(2)}) copy-start(f32[768]{0:T(1024)S(1)} %get-tuple-element.446) | copy-start | bytes 9220
  160.0 412.2 %copy-start.100 = (f32[768]{0:T(1024)}, f32[768]{0:T(1024)S(1)}, u32[]{:S(2)}) copy-start(f32[768]{0:T(1024)S(1)} %get-tuple-element.447) | copy-start | bytes 9220
  160.0 594.4 %copy-start.93 = (f32[768]{0:T(1024)}, f32[768]{0:T(1024)S(1)}, u32[]{:S(2)}) copy-start(f32[768]{0:T(1024)S(1)} %get-tuple-element.445) | copy-start | bytes 9220
  204.8 90.7 %copy-start.8 = (f32[256,768]{1,0:T(8,128)}, f32[256,768]{1,0:T(8,128)S(1)}, u32[]{:S(2)}) copy-start(f32[256,768]{1,0:T(8,128)S(1)} %get-tuple-element.524) | copy-start | bytes 2359300
  206.0 89.5 %reduce-scatter.22.cloned.1.call-start = ((), (), s32[]{:S(2)}) async-start(), calls=%async_computation.21 | async-start | bytes 3932160 | tf_op jit(solution)/shard_map/reduce_scatter | solution.py:52
  251.3 90.9 %reduce-scatter.24.cloned.1.call-start = ((), (), s32[]{:S(2)}) async-start(), calls=%async_computation.22 | async-start | bytes 3932160 | tf_op jit(solution)/shard_map/reduce_scatter | solution.py:52
  266.1 109.6 %all-gather.25.cloned.1.call-start = ((), (), s32[]{:S(2)}) async-start(), calls=%async_computation.23 | async-start | bytes 1966080 | tf_op jit(solution)/shard_map/all_gather | solution.py:48
  295.5 80.2 %copy-start.193 = (f32[3,192]{1,0:T(4,128)S(1)}, f32[3,192]{1,0:T(4,128)}, u32[]{:S(2)}) copy-start(f32[3,192]{1,0:T(4,128)} %copy-done.192) | copy-start | bytes 6916
  297.0 78.7 %copy-start.137 = (f32[256]{0:T(256)}, f32[256]{0:T(256)S(1)}, u32[]{:S(2)}) copy-start(f32[256]{0:T(256)S(1)} %broadcast_multiply_fusion.20) | copy-start | bytes 3076
  297.2 78.5 %copy-start.172 = (f32[256]{0:T(256)}, f32[256]{0:T(256)S(1)}, u32[]{:S(2)}) copy-start(f32[256]{0:T(256)S(1)} %multiply_reduce_fusion.22) | copy-start | bytes 3076
  297.2 78.4 %copy-start.170 = (f32[256]{0:T(256)}, f32[256]{0:T(256)S(1)}, u32[]{:S(2)}) copy-start(f32[256]{0:T(256)S(1)} %add_rsqrt_fusion.4) | copy-start | bytes 3076
  298.1 44.2 %collective-permute-start = (f32[256,768]{1,0:T(8,128)S(1)}, f32[256,768]{1,0:T(8,128)S(1)}, u32[]{:S(2)}, u32[]{:S(2)}) collective-permute-start(f32[256,768]{1,0:T(8,128)S(1)} %multiply_add_fusion.6), channel_id=1, source_target_pairs={{0,16},{1,17},{2,18},{3,19},{4,20},{5,21},{6,22},{7,23},{8,24},{9,... | collective-permute-start | bytes 2359304 | tf_op jit(solution)/shard_map/ppermute | solution.py:28
  344.6 134.3 %reduce-scatter.26.cloned.1.call-start = ((), (), s32[]{:S(2)}) async-start(), calls=%async_computation.24 | async-start | bytes 3932160 | tf_op jit(solution)/shard_map/reduce_scatter | solution.py:52
  434.8 77.8 %copy-start.188 = (f32[768]{0:T(1024)S(1)}, f32[768]{0:T(1024)}, u32[]{:S(2)}) copy-start(f32[768]{0:T(1024)} %copy-done.187) | copy-start | bytes 9220
  434.8 77.8 %all-gather.27.cloned.1.call-start = ((), (), s32[]{:S(2)}) async-start(), calls=%async_computation.25 | async-start | bytes 1966080 | tf_op jit(solution)/shard_map/all_gather | solution.py:48
  480.5 91.7 %copy-start.5 = (f32[256,768]{1,0:T(8,128)}, f32[256,768]{1,0:T(8,128)S(1)}, u32[]{:S(2)}) copy-start(f32[256,768]{1,0:T(8,128)S(1)} %get-tuple-element.520) | copy-start | bytes 2359300
  480.5 91.7 %copy-start.107 = (f32[256]{0:T(256)}, f32[256]{0:T(256)S(1)}, u32[]{:S(2)}) copy-start(f32[256]{0:T(256)S(1)} %broadcast_multiply_fusion.19) | copy-start | bytes 3076
  480.8 91.5 %copy-start.129 = (f32[256]{0:T(256)}, f32[256]{0:T(256)S(1)}, u32[]{:S(2)}) copy-start(f32[256]{0:T(256)S(1)} %add_rsqrt_fusion.3) | copy-start | bytes 3076
  481.7 90.5 %reduce-scatter.28.cloned.1.call-start = ((), (), s32[]{:S(2)}) async-start(), calls=%async_computation.26 | async-start | bytes 3932160 | tf_op jit(solution)/shard_map/reduce_scatter | solution.py:52
  528.1 53.6 %copy-start.124 = (s32[1,4,4,128]{3,2,1,0:T(4,128)S(1)}, s32[1,4,4,128]{3,2,1,0:T(4,128)}, u32[]{:S(2)}) copy-start(s32[1,4,4,128]{3,2,1,0:T(4,128)} %get-tuple-element.618) | copy-start | bytes 24580
  528.1 53.6 %copy-start.160 = (s32[1024]{0:T(1024)S(1)}, s32[1024]{0:T(1024)}, u32[]{:S(2)}) copy-start(s32[1024]{0:T(1024)} %get-tuple-element.558) | copy-start | bytes 12292
  528.1 53.6 %copy-start.161 = (s32[1024]{0:T(1024)S(1)}, s32[1024]{0:T(1024)}, u32[]{:S(2)}) copy-start(s32[1024]{0:T(1024)} %get-tuple-element.613) | copy-start | bytes 12292
  528.1 83.9 %copy-start.83 = (bf16[1024,3,192]{0,2,1:T(8,128)(2,1)S(1)}, bf16[1024,3,192]{0,2,1:T(8,128)(2,1)}, u32[]{:S(2)}) copy-start(bf16[1024,3,192]{0,2,1:T(8,128)(2,1)} %add_convert_fusion.2) | copy-start | bytes 3538948
  528.2 83.9 %copy-start.194 = (f32[3,192]{1,0:T(4,128)S(1)}, f32[3,192]{1,0:T(4,128)}, u32[]{:S(2)}) copy-start(f32[3,192]{1,0:T(4,128)} %copy-done.192) | copy-start | bytes 6916
  528.2 83.9 %all-gather.29.cloned.1.call-start = ((), (), s32[]{:S(2)}) async-start(), calls=%async_computation.27 | async-start | bytes 1966080 | tf_op jit(solution)/shard_map/all_gather | solution.py:48
  575.6 4.2 collective-permute-start.1
  581.5 170.8 %reduce-scatter.30.cloned.1.call-start = ((), (), s32[]{:S(2)}) async-start(), calls=%async_computation.28 | async-start | bytes 3932160 | tf_op jit(solution)/shard_map/reduce_scatter | solution.py:52
  581.8 120.1 %copy-start.118 = (s32[1024]{0:T(1024)}, s32[1024]{0:T(1024)S(1)}, u32[]{:S(2)}) copy-start(s32[1024]{0:T(1024)S(1)} %broadcast_clamp_fusion.5) | copy-start | bytes 12292
  708.1 78.9 %copy-start.189 = (f32[768]{0:T(1024)S(1)}, f32[768]{0:T(1024)}, u32[]{:S(2)}) copy-start(f32[768]{0:T(1024)} %copy-done.187) | copy-start | bytes 9220
  708.2 78.8 %all-gather.31.cloned.1.call-start = ((), (), s32[]{:S(2)}) async-start(), calls=%async_computation.29 | async-start | bytes 1966080 | tf_op jit(solution)/shard_map/all_gather | solution.py:48
  755.9 64.4 %all-gather.33.cloned.1.call-start = ((), (), s32[]{:S(2)}) async-start(), calls=%async_computation.31 | async-start | bytes 1966080 | tf_op jit(solution)/shard_map/all_gather | solution.py:48
  756.5 191.7 %reduce-scatter.32.cloned.1.call-start = ((), (), s32[]{:S(2)}) async-start(), calls=%async_computation.30 | async-start | bytes 3932160 | tf_op jit(solution)/shard_map/reduce_scatter | solution.py:52
  801.2 190.2 %reduce-scatter.34.cloned.1.call-start = ((), (), s32[]{:S(2)}) async-start(), calls=%async_computation.32 | async-start | bytes 3932160 | tf_op jit(solution)/shard_map/reduce_scatter | solution.py:52
  947.7 80.5 %all-gather.35.cloned.1.call-start = ((), (), s32[]{:S(2)}) async-start(), calls=%async_computation.33 | async-start | bytes 1966080 | tf_op jit(solution)/shard_map/all_gather | solution.py:48
  997.4 90.7 %reduce-scatter.36.cloned.1.call-start = ((), (), s32[]{:S(2)}) async-start(), calls=%async_computation.34 | async-start | bytes 3932160 | tf_op jit(solution)/shard_map/reduce_scatter | solution.py:52
  1044.0 89.0 %all-gather.37.cloned.1.call-start = ((), (), s32[]{:S(2)}) async-start(), calls=%async_computation.35 | async-start | bytes 1966080 | tf_op jit(solution)/shard_map/all_gather | solution.py:48
  1093.6 137.9 %all-gather.39.cloned.1.call-start = ((), (), s32[]{:S(2)}) async-start(), calls=%async_computation.37 | async-start | bytes 1966080 | tf_op jit(solution)/shard_map/all_gather | solution.py:48
  1132.7 226.3 %reduce-scatter.38.cloned.1.call-start = ((), (), s32[]{:S(2)}) async-start(), calls=%async_computation.36 | async-start | bytes 3932160 | tf_op jit(solution)/shard_map/reduce_scatter | solution.py:52
  1231.4 171.1 %reduce-scatter.40.cloned.1.call-start = ((), (), s32[]{:S(2)}) async-start(), calls=%async_computation.38 | async-start | bytes 3932160 | tf_op jit(solution)/shard_map/reduce_scatter | solution.py:52
  1358.9 80.2 %all-gather.41.cloned.1.call-start = ((), (), s32[]{:S(2)}) async-start(), calls=%async_computation.39 | async-start | bytes 1966080 | tf_op jit(solution)/shard_map/all_gather | solution.py:48
  1362.1 40.4 %collective-permute-start.2 = (f32[256,768]{1,0:T(8,128)}, f32[256,768]{1,0:T(8,128)}, u32[]{:S(2)}, u32[]{:S(2)}) collective-permute-start(f32[256,768]{1,0:T(8,128)} %add.824), channel_id=1, source_target_pairs={{16,0},{17,1},{18,2},{19,3},{20,4},{21,5},{22,6},{23,7},{24,8},{25... | collective-permute-start | bytes 2359304 | tf_op jit(solution)/shard_map/ppermute | solution.py:28
  1408.0 91.6 %reduce-scatter.42.cloned.1.call-start = ((), (), s32[]{:S(2)}) async-start(), calls=%async_computation.40 | async-start | bytes 3932160 | tf_op jit(solution)/shard_map/reduce_scatter | solution.py:52
  1455.5 99.7 %all-gather.43.cloned.1.call-start = ((), (), s32[]{:S(2)}) async-start(), calls=%async_computation.41 | async-start | bytes 1966080 | tf_op jit(solution)/shard_map/all_gather | solution.py:48
  1505.4 200.8 %reduce-scatter.44.cloned.1.call-start = ((), (), s32[]{:S(2)}) async-start(), calls=%async_computation.42 | async-start | bytes 3932160 | tf_op jit(solution)/shard_map/reduce_scatter | solution.py:52
  1662.0 51.0 %copy-start.136 = (f32[256]{0:T(256)S(1)}, f32[256]{0:T(256)}, u32[]{:S(2)}) copy-start(f32[256]{0:T(256)} %copy-done.135) | copy-start | bytes 3076
  1662.1 85.9 %all-gather.45.cloned.1.call-start = ((), (), s32[]{:S(2)}) async-start(), calls=%async_computation.43 | async-start | bytes 1966080 | tf_op jit(solution)/shard_map/all_gather | solution.py:48
  1708.4 4.7 collective-permute-start.3
  1717.2 91.2 %reduce-scatter.46.cloned.1.call-start = ((), (), s32[]{:S(2)}) async-start(), calls=%async_computation.44 | async-start | bytes 3932160 | tf_op jit(solution)/shard_map/reduce_scatter | solution.py:52
  1764.3 80.9 %all-gather.47.cloned.1.call-start = ((), (), s32[]{:S(2)}) async-start(), calls=%async_computation.45 | async-start | bytes 1966080 | tf_op jit(solution)/shard_map/all_gather | solution.py:48
  1814.1 169.4 %reduce-scatter.48.cloned.1.call-start = ((), (), s32[]{:S(2)}) async-start(), calls=%async_computation.46 | async-start | bytes 3932160 | tf_op jit(solution)/shard_map/reduce_scatter | solution.py:52
  1939.4 90.6 %all-gather.49.cloned.1.call-start = ((), (), s32[]{:S(2)}) async-start(), calls=%async_computation.47 | async-start | bytes 1966080 | tf_op jit(solution)/shard_map/all_gather | solution.py:48
  1948.6 105.5 %all-gather.51.cloned.1.call-start = ((), (), s32[]{:S(2)}) async-start(), calls=%async_computation.48 | async-start | bytes 1966080 | tf_op jit(solution)/shard_map/all_gather | solution.py:48
  1986.8 419.8 %all-reduce.5.cloned.1.call-start = ((), (), s32[]{:S(2)}) async-start(), calls=%async_computation.50 | async-start | bytes 20447232 | tf_op jit(solution)/shard_map/psum | solution.py:402
  2005.2 858.9 %reduce-scatter.50.cloned.1.call-start = ((), (), s32[]{:S(2)}) async-start(), calls=%async_computation.49 | async-start | bytes 26542080 | tf_op jit(solution)/shard_map/reduce_scatter | solution.py:405
  2410.1 457.6 %copy-start.70 = (f32[1,768,768]{2,1,0:T(8,128)S(1)}, f32[1,768,768]{2,1,0:T(8,128)}, u32[]{:S(2)}) copy-start(f32[1,768,768]{2,1,0:T(8,128)} %get-tuple-element.771) | copy-start | bytes 7077892
  (197 other events, 3143.7 us)
Sparse Core Ops, SparseCore 0:
  22.5 45.0 reduce-scatter.17
  70.0 30.9 all-gather.20
  159.4 43.9 reduce-scatter.19
  206.1 30.9 all-gather.22
  251.5 43.9 reduce-scatter.21
  298.3 43.9 reduce-scatter.23
  344.7 30.9 all-gather.24
  434.9 43.9 reduce-scatter.25
  481.9 30.7 all-gather.26
  528.2 43.9 reduce-scatter.27
  581.6 30.4 all-gather.28
  708.3 43.9 reduce-scatter.29
  756.0 30.9 all-gather.30
  789.3 30.9 all-gather.32
  823.1 44.0 reduce-scatter.31
  947.8 43.4 reduce-scatter.33
  997.5 30.6 all-gather.34
  1044.1 43.9 reduce-scatter.35
  1093.8 30.9 all-gather.36
  1132.8 31.0 all-gather.38
  1231.6 44.0 reduce-scatter.37
  1359.0 43.4 reduce-scatter.39
  1408.2 30.9 all-gather.40
  1455.6 43.9 reduce-scatter.41
  1505.5 30.9 all-gather.42
  1662.2 43.9 reduce-scatter.43
  1717.3 30.6 all-gather.44
  1764.5 43.9 reduce-scatter.45
  1814.2 30.9 all-gather.46
  1939.5 43.9 reduce-scatter.47
  1985.4 30.9 all-gather.48
  2018.8 30.9 all-gather.50
  2053.9 352.6 all-reduce.4
  2409.5 454.4 reduce-scatter.49
where the time goes:
time: 2890 us; the launch traced here: 2880 us
  waiting for transfers between devices  1600 us (55%)
  local copies, waits for them, and re-layouts  440 us (15%)
  matrix products  425 us (15%)
  other arithmetic  318 us (11%)
  blocking collectives  59.7 us (2%)
    reduce_scatter x16, waiting for transfers between devices, sum_rows(): lax.psum_scatter(work(jnp.int32(0), shard_rows * lax.axis_size('tensor'))...  553 us
    reduce_scatter x1, waiting for transfers between devices, shards(): lax.psum_scatter(d_embedding, ('section', 'dp'), scatter_dimension=0, til...  454 us
    all_gather x16, waiting for transfers between devices, gather_rows(): return lax.all_gather(shard, 'tensor', axis=0, tiled=True)  309 us
    psum x1, waiting for transfers between devices, shards(): lax.psum((g_qkv, g_bqv, g_out, g_in, g_bin, g_down, g_mask, g_gains, g_sh...  283 us
    gather x18, local copies, waits for them, and re-layouts, split_heads(): projected[gather_index]  162 us
    dot_general x14, matrix products, times_right(): lax.dot_general(left, right, (((1,), (1,)), ((), ())), preferred_element_...  110 us
    dot_general x14, matrix products, times(): return jnp.dot(left, right, preferred_element_type=jnp.float32)  98.1 us
    dot_general x14, matrix products, times_left(): lax.dot_general(left, right, (((0,), (0,)), ((), ())), preferred_element_...  72.9 us
  transfers between devices with their start and end apart: 38, of which 29 were waited for; matrix products, arithmetic and copies ran while one was open for 21% of the time, Pallas kernels for 0%

commit v1 on v0

v1 whole, which is shorter than its diff:
```python
import functools

import jax
import jax.numpy as jnp
from jax import lax
from jax.experimental import pallas as pl
from jax.experimental.pallas import tpu as pltpu
from jax.sharding import PartitionSpec as P

BUCKET = 128
MAXLEN = 512
EPSILON = 1e-12
LOSS_SCALE = 16.0
BF = jnp.bfloat16
F32 = jnp.float32
MIB = 1 << 20
LANES = 128
HEAD_DIM = 64
VOCAB_STEP = 480
BACK_STEP = 960


def nn(left, right):
    return jnp.dot(left, right, preferred_element_type=F32)


def nt(left, right):
    return lax.dot_general(left, right, (((1,), (1,)), ((), ())), preferred_element_type=F32)


def tn(left, right):
    return lax.dot_general(left, right, (((0,), (0,)), ((), ())), preferred_element_type=F32)


def sds(shape, dtype):
    return jax.ShapeDtypeStruct(shape, dtype)


def whole_specs(count):
    return [pl.BlockSpec(memory_space=pltpu.VMEM)] * count


def scalar_specs(count):
    return [pl.BlockSpec(memory_space=pltpu.SMEM)] * count


def kernel_call(kernel, name, outs, scalars, arrays, scratch=(), flops=0, vmem=32):
    moved = sum(a.size * a.dtype.itemsize for a in arrays)
    moved += sum(jnp.dtype(o.dtype).itemsize * functools.reduce(lambda a, b: a * b, o.shape, 1) for o in outs)
    return pl.pallas_call(
        kernel,
        name=name,
        out_shape=outs,
        in_specs=scalar_specs(len(scalars)) + whole_specs(len(arrays)),
        out_specs=whole_specs(len(outs)),
        scratch_shapes=list(scratch),
        compiler_params=pltpu.CompilerParams(vmem_limit_bytes=vmem * MIB),
        cost_estimate=pl.CostEstimate(flops=flops, bytes_accessed=moved, transcendentals=0),
    )(*scalars, *arrays)


def swap(array, axis, bit):
    count = lax.axis_size(axis)
    return lax.ppermute(array, axis, [(i, i ^ bit) for i in range(count)])


def gather_pieces(own):
    half = own.shape[0] // 2
    near = swap(own, "tensor", 1)
    far = swap(own, "tensor", 2)
    corner_low = swap(near[:half], "tensor", 2)
    corner_high = swap(far[half:], "tensor", 1)
    return [own, near, far, corner_low, corner_high]


def reduce_pieces(near, far, corner_low, corner_high):
    half = near.shape[0] // 2
    low = swap(corner_low, "tensor", 1)
    high = swap(corner_high, "tensor", 2)
    far_sum = jnp.concatenate([(far[:half].astype(F32) + low.astype(F32)).astype(BF), far[half:]])
    near_sum = jnp.concatenate([near[:half], (near[half:].astype(F32) + high.astype(F32)).astype(BF)])
    return swap(near_sum, "tensor", 1), swap(far_sum, "tensor", 2)


def copy_pieces(pieces, target):
    at = 0
    for piece in pieces:
        rows = piece.shape[0]
        target[at : at + rows, :] = piece[...]
        at += rows


def store_block(r, value, own, near, far, corner_low, corner_high):
    half = near.shape[0] // 2
    if r == 0:
        own[...] = value
    elif r == 1:
        near[...] = value.astype(BF)
    elif r == 2:
        far[...] = value.astype(BF)
    else:
        corner_low[...] = value[:half].astype(BF)
        corner_high[...] = value[half:].astype(BF)


def piece_outs(rows, width):
    return [
        sds((rows, width), F32),
        sds((rows, width), BF),
        sds((rows, width), BF),
        sds((rows // 2, width), BF),
        sds((rows // 2, width), BF),
    ]


def sequence_of(bucket, len_ref):
    start, length, total = jnp.int32(0), len_ref[0], jnp.int32(0)
    for i in range(len_ref.shape[0]):
        begun = bucket >= total
        start = jnp.where(begun, total, start)
        length = jnp.where(begun, len_ref[i], length)
        total = total + len_ref[i]
    return start, length


def half_masks():
    lane = lax.broadcasted_iota(jnp.int32, (1, LANES), 1)
    low = (lane < HEAD_DIM).astype(F32)
    return [low.astype(BF), (1.0 - low).astype(BF)], lane < HEAD_DIM


TILES = ((0, (0, 1)), (1, (2,)))
PART = 2 * LANES


def block_rows(me, r, rows):
    return pl.ds(pl.multiple_of((me ^ r) * rows, rows), rows)


def attention_forward(len_ref, me_ref, *refs):
    pieces, refs = refs[:5], refs[5:]
    w_ref, b_ref, g_ref, wo_ref, own, near, far, c_low, c_high, x_rel, proj, ctx_rel, ctx = refs
    me = me_ref[0]
    rows = own.shape[0]
    tokens = proj.shape[0]
    copy_pieces(pieces, x_rel)

    @pl.loop(0, 4)
    def project(r):
        value = nn(x_rel[pl.ds(pl.multiple_of(r * rows, rows), rows), :], w_ref[...]) + b_ref[...]
        proj[block_rows(me, r, rows), :] = value.astype(BF)

    masks, low_lane = half_masks()

    @pl.loop(0, tokens // BUCKET)
    def attend(bucket):
        start, length = sequence_of(bucket, len_ref)
        q_rows = pl.ds(pl.multiple_of(bucket * BUCKET, BUCKET), BUCKET)
        gate_rows = pl.ds(pl.multiple_of((bucket - start) * BUCKET, BUCKET), BUCKET)

        def body(size):
            k_rows = pl.ds(pl.multiple_of(start * BUCKET, BUCKET), size)
            for tile, heads in TILES:
                at = tile * LANES
                q = proj[q_rows, at : at + LANES]
                k = proj[k_rows, PART + at : PART + at + LANES]
                v = proj[k_rows, 2 * PART + at : 2 * PART + at + LANES]
                mixed = []
                for i, head in enumerate(heads):
                    qm = q * masks[i] if len(heads) > 1 else q
                    scores = nt(qm, k) * HEAD_DIM ** (-0.5)
                    powers = jnp.exp(scores - jnp.max(scores, axis=-1, keepdims=True))
                    attention = powers * (1.0 / jnp.sum(powers, axis=-1, keepdims=True))
                    gated = (attention * g_ref[head, gate_rows, 0:size]).astype(BF)
                    mixed.append(nn(gated, v))
                value = jnp.where(low_lane, mixed[0], mixed[1]) if len(heads) > 1 else mixed[0]
                ctx[q_rows, at : at + LANES] = value.astype(BF)

        for buckets in range(1, MAXLEN // BUCKET + 1):
            pl.when(length == buckets)(functools.partial(body, buckets * BUCKET))

    for r in range(4):
        block = ctx[block_rows(me, r, rows), :]
        ctx_rel[r * rows : (r + 1) * rows, :] = block
        store_block(r, nn(block, wo_ref[...]), own, near, far, c_low, c_high)


def attention_backward(len_ref, me_ref, *refs):
    pieces, refs = refs[:5], refs[5:]
    w_ref, g_ref, wo_ref, proj, own, near, far, c_low, c_high, d_rel, dproj_rel, d_bias, d_gate, d_ctx, d_key, d_val, dproj = refs
    me = me_ref[0]
    rows = own.shape[0]
    tokens = proj.shape[0]
    copy_pieces(pieces, d_rel)

    @pl.loop(0, 4)
    def context_grad(r):
        value = nt(d_rel[pl.ds(pl.multiple_of(r * rows, rows), rows), :], wo_ref[...])
        d_ctx[block_rows(me, r, rows), :] = value.astype(BF)

    d_gate[...] = jnp.zeros_like(d_gate)
    d_key[...] = jnp.zeros_like(d_key)
    d_val[...] = jnp.zeros_like(d_val)
    masks, low_lane = half_masks()

    @pl.loop(0, tokens // BUCKET)
    def attend(bucket):
        start, length = sequence_of(bucket, len_ref)
        q_rows = pl.ds(pl.multiple_of(bucket * BUCKET, BUCKET), BUCKET)
        gate_rows = pl.ds(pl.multiple_of((bucket - start) * BUCKET, BUCKET), BUCKET)

        def body(size):
            k_rows = pl.ds(pl.multiple_of(start * BUCKET, BUCKET), size)
            for tile, heads in TILES:
                at = tile * LANES
                q = proj[q_rows, at : at + LANES]
                k = proj[k_rows, PART + at : PART + at + LANES]
                v = proj[k_rows, 2 * PART + at : 2 * PART + at + LANES]
                d_out = d_ctx[q_rows, at : at + LANES]
                d_q = []
                key_sum = val_sum = None
                for i, head in enumerate(heads):
                    qm = q * masks[i] if len(heads) > 1 else q
                    dm = d_out * masks[i] if len(heads) > 1 else d_out
                    scores = nt(qm, k) * HEAD_DIM ** (-0.5)
                    powers = jnp.exp(scores - jnp.max(scores, axis=-1, keepdims=True))
                    attention = powers * (1.0 / jnp.sum(powers, axis=-1, keepdims=True))
                    gate = g_ref[head, gate_rows, 0:size]
                    d_mixed = nt(dm, v)
                    d_gate[head, gate_rows, 0:size] += d_mixed * attention
                    d_prob = d_mixed * gate
                    inner = jnp.sum(d_prob * attention, axis=-1, keepdims=True)
                    d_scores = (attention * (d_prob - inner)).astype(BF)
                    gated = (attention * gate).astype(BF)
                    val = tn(gated, dm)
                    key = tn(d_scores, qm)
                    val_sum = val if val_sum is None else val_sum + val
                    key_sum = key if key_sum is None else key_sum + key
                    d_q.append(nn(d_scores, k))
                value = jnp.where(low_lane, d_q[0], d_q[1]) if len(heads) > 1 else d_q[0]
                dproj[q_rows, at : at + LANES] = (value * HEAD_DIM ** (-0.5)).astype(BF)
                d_key[k_rows, at : at + LANES] += key_sum
                d_val[k_rows, at : at + LANES] += val_sum

        for buckets in range(1, MAXLEN // BUCKET + 1):
            pl.when(length == buckets)(functools.partial(body, buckets * BUCKET))

    dproj[:, PART : 2 * PART] = (d_key[...] * HEAD_DIM ** (-0.5)).astype(BF)
    dproj[:, 2 * PART : 3 * PART] = d_val[...].astype(BF)
    sums = jnp.zeros((1, dproj.shape[1]), F32)
    for r in range(4):
        block = dproj[block_rows(me, r, rows), :]
        dproj_rel[r * rows : (r + 1) * rows, :] = block
        sums = sums + jnp.sum(block.astype(F32), axis=0, keepdims=True)
        store_block(r, nt(block, w_ref[...]), own, near, far, c_low, c_high)
    d_bias[...] = sums


def feed_forward(*refs):
    pieces, refs = refs[:5], refs[5:]
    w_in, b_in, w_down, own, near, far, c_low, c_high, h_rel, act, slope = refs
    rows = own.shape[0]
    copy_pieces(pieces, h_rel)
    for r in range(4):
        at = slice(r * rows, (r + 1) * rows)
        pre = nn(h_rel[at, :], w_in[...]) + b_in[...]
        below = 0.5 * (1.0 + lax.erf(pre * 0.7071067811865476))
        active = (pre * below).astype(BF)
        act[at, :] = active
        slope[at, :] = below + pre * jnp.exp(-0.5 * pre * pre) * 0.3989422804014327
        store_block(r, nn(active, w_down[...]), own, near, far, c_low, c_high)


def feed_backward(*refs):
    pieces, refs = refs[:5], refs[5:]
    w_in, w_down, slope, own, near, far, c_low, c_high, d_rel, d_pre, d_bias = refs
    rows = own.shape[0]
    copy_pieces(pieces, d_rel)
    sums = jnp.zeros((1, d_pre.shape[1]), F32)
    for r in range(4):
        at = slice(r * rows, (r + 1) * rows)
        value = (slope[at, :] * nt(d_rel[at, :], w_down[...])).astype(BF)
        d_pre[at, :] = value
        sums = sums + jnp.sum(value.astype(F32), axis=0, keepdims=True)
        store_block(r, nt(value, w_in[...]), own, near, far, c_low, c_high)
    d_bias[...] = sums


def norm_forward(own, near, far, residual, bias, gain, shift, hidden, hidden_low, normed_ref, scale_ref):
    value = residual[...] + (own[...] + near[...].astype(F32) + far[...].astype(F32)) + bias[...]
    centered = value - jnp.mean(value, axis=-1, keepdims=True)
    scale = lax.rsqrt(jnp.mean(centered * centered, axis=-1, keepdims=True) + EPSILON)
    normed = centered * scale
    out = normed * gain[...] + shift[...]
    hidden[...] = out
    hidden_low[...] = out.astype(BF)
    normed_ref[...] = normed
    scale_ref[...] = scale


def norm_grad(grad, normed, scale, gain, d_sum_ref, d_low_ref, sums_ref):
    scaled = grad * gain
    d_sum = scale * (
        scaled
        - jnp.mean(scaled, axis=-1, keepdims=True)
        - normed * jnp.mean(scaled * normed, axis=-1, keepdims=True)
    )
    d_sum_ref[...] = d_sum
    d_low_ref[...] = d_sum.astype(BF)
    sums_ref[0:1, :] = jnp.sum(grad * normed, axis=0, keepdims=True)
    sums_ref[1:2, :] = jnp.sum(grad, axis=0, keepdims=True)
    sums_ref[2:3, :] = jnp.sum(d_sum, axis=0, keepdims=True)


def norm_backward(own, near, far, residual, normed, scale, gain, d_out, d_sum, d_low, sums):
    grad = residual[...] + (own[...] + near[...].astype(F32) + far[...].astype(F32))
    d_out[...] = grad
    norm_grad(grad, normed[...], scale[...], gain[...], d_sum, d_low, sums)


def merge_head(own, near, far, corner, target_rows, normed, scale, gain, d_sum, d_low, sums, spread_ref):
    width = target_rows.shape[1]
    blocks = [own[...], near[...].astype(F32), far[...].astype(F32), corner[...].astype(F32)]
    spreads = [jnp.sum(block[:, width : width + 3], axis=-1, keepdims=True) for block in blocks]
    top = functools.reduce(jnp.maximum, spreads)
    shares = [jnp.exp(spread - top) for spread in spreads]
    total = functools.reduce(lambda a, b: a + b, shares)
    expected = functools.reduce(
        lambda a, b: a + b, [block[:, :width] * (share / total) for block, share in zip(blocks, shares)]
    )
    grad = LOSS_SCALE * (expected - target_rows[...].astype(F32))
    norm_grad(grad, normed[...], scale[...], gain[...], d_sum, d_low, sums)
    spread = top + jnp.log(total)
    spread_ref[...] = jnp.transpose(jnp.broadcast_to(spread, (spread.shape[0], LANES)))[0:8, :]


def head_forward(*refs):
    pieces, refs = refs[:5], refs[5:]
    e_ref, own, near, far, corner, powers_ref, tops_ref, x_rel, grown, top_ref, total_ref = refs
    step = pl.program_id(0)
    rows = own.shape[0]
    width = x_rel.shape[1]

    @pl.when(step == 0)
    def begin():
        copy_pieces(pieces, x_rel)
        grown[...] = jnp.zeros_like(grown)
        top_ref[...] = jnp.full_like(top_ref, -1e30)
        total_ref[...] = jnp.zeros_like(total_ref)

    for r in range(4):
        at = slice(r * rows, (r + 1) * rows)
        logits = nt(e_ref[...], x_rel[at, :])
        old = top_ref[:, at]
        top = jnp.maximum(old, jnp.max(logits, axis=0, keepdims=True))
        fade = jnp.exp(old - top)
        powers = jnp.exp(logits - top)
        total_ref[:, at] = total_ref[:, at] * fade + jnp.sum(powers, axis=0, keepdims=True)
        top_ref[:, at] = top
        low = powers.astype(BF)
        powers_ref[:, at] = low
        grown[0:width, at] = grown[0:width, at] * fade + tn(e_ref[...], low)
    tops_ref[0] = top_ref[...]

    @pl.when(step == pl.num_programs(0) - 1)
    def end():
        total = total_ref[...]
        spread = top_ref[...] + jnp.log(total)
        first = spread.astype(BF).astype(F32)
        second = (spread - first).astype(BF).astype(F32)
        third = spread - first - second
        tail = [first, second, third, jnp.zeros((LANES - 3, total.shape[1]), F32)]
        grown[width : width + LANES, :] = jnp.concatenate(tail, axis=0)
        share = 1.0 / total
        for r, target in enumerate((own, near, far, corner)):
            at = slice(r * rows, (r + 1) * rows)
            target[:, 0:width] = jnp.transpose(grown[0:width, at] * share[:, at]).astype(target.dtype)
            target[:, width : width + LANES] = jnp.transpose(grown[width : width + LANES, at]).astype(target.dtype)


def head_backward(first_ref, *refs):
    pieces, refs = refs[:5], refs[5:]
    spread_refs, refs = refs[:4], refs[4:]
    powers_ref, tops_ref, hit_ref, out, x_rel, spread = refs
    step = pl.program_id(0)

    @pl.when(step == 0)
    def begin():
        copy_pieces(pieces, x_rel)
        for r, ref in enumerate(spread_refs):
            rows = ref.shape[1]
            spread[:, r * rows : (r + 1) * rows] = ref[0:1, :]

    count = tops_ref.shape[0]
    rows = powers_ref.shape[0] // count
    for i in range(count):
        at = slice(i * rows, (i + 1) * rows)
        scale = LOSS_SCALE * jnp.exp(tops_ref[i] - spread[...])
        index = lax.broadcasted_iota(jnp.int32, (rows, 1), 0) + ((step + first_ref[0]) * count + i) * rows
        hit = jnp.where(index == hit_ref[...], LOSS_SCALE, 0.0)
        grads = powers_ref[at, :].astype(F32) * scale - hit
        out[at, :] = nn(grads.astype(BF), x_rel[...]).astype(BF)


def embed_backward(first_ref, *refs):
    pieces, refs = refs[:5], refs[5:]
    id_ref, so_far, out = refs
    vocab = out.shape[0]
    total = so_far[...]
    index = lax.broadcasted_iota(jnp.int32, (vocab, 1), 0) + first_ref[pl.program_id(0)]
    at = 0
    for piece in pieces:
        ids = id_ref[:, at : at + piece.shape[0]]
        total = total + nn(jnp.where(index == ids, 1.0, 0.0).astype(BF), piece[...])
        at += piece.shape[0]
    out[...] = total


def layer_forward(x, x_low, lens, me, weights):
    w_qkv, b_qkv, w_out, w_in, b_in, w_down, gains, shifts, gates = weights
    rows, width = x.shape
    tokens = 4 * rows
    outs = piece_outs(rows, width) + [sds((tokens, width), BF), sds((tokens, 3 * PART), BF), sds((tokens, PART), BF)]
    *parts, x_rel, proj, ctx_rel = kernel_call(
        attention_forward,
        "attention_forward",
        outs,
        [lens, me],
        gather_pieces(x_low) + [w_qkv, b_qkv, gates, w_out],
        [pltpu.VMEM((tokens, PART), BF)],
        flops=2 * tokens * width * 4 * PART,
    )
    near, far = reduce_pieces(*parts[1:])
    norm_outs = [sds((rows, width), F32), sds((rows, width), BF), sds((rows, width), F32), sds((rows, 1), F32)]
    hidden, hidden_low, normed_one, scale_one = kernel_call(
        norm_forward,
        "first_norm",
        norm_outs,
        [],
        [parts[0], near, far, x, shifts[0:1], gains[0:1], shifts[1:2]],
    )
    units = w_in.shape[1]
    outs = piece_outs(rows, width) + [sds((tokens, width), BF), sds((tokens, units), BF), sds((tokens, units), F32)]
    *parts, h_rel, act, slope = kernel_call(
        feed_forward,
        "feed_forward",
        outs,
        [],
        gather_pieces(hidden_low) + [w_in, b_in, w_down],
        flops=4 * tokens * width * units,
    )
    near, far = reduce_pieces(*parts[1:])
    out, out_low, normed_two, scale_two = kernel_call(
        norm_forward,
        "second_norm",
        norm_outs,
        [],
        [parts[0], near, far, hidden, shifts[2:3], gains[1:2], shifts[3:4]],
    )
    return out, out_low, (x_rel, proj, ctx_rel, h_rel, act, slope, normed_one, scale_one, normed_two, scale_two)


def layer_backward(d_two, d_two_low, lens, me, weights, saved, section, head_width):
    w_qkv, b_qkv, w_out, w_in, b_in, w_down, gains, shifts, gates = weights
    x_rel, proj, ctx_rel, h_rel, act, slope, normed_one, scale_one = saved[:8]
    rows, width = d_two.shape
    tokens = 4 * rows
    units = w_in.shape[1]
    outs = piece_outs(rows, width) + [sds((tokens, width), BF), sds((tokens, units), BF), sds((1, units), F32)]
    *parts, d_rel, d_pre, d_b_in = kernel_call(
        feed_backward,
        "feed_backward",
        outs,
        [],
        gather_pieces(d_two_low) + [w_in, w_down, slope],
        flops=4 * tokens * width * units,
    )
    near, far = reduce_pieces(*parts[1:])
    d_w_down = tn(act, d_rel).astype(BF)
    d_w_in = tn(h_rel, d_pre).astype(BF)
    first = section == 0
    sent = swap(jnp.where(first, d_w_down, d_w_in), "section", 1)
    d_feed = dp_sum(plus(jnp.where(first, d_w_in, d_w_down), sent))
    outs = [sds((rows, width), F32), sds((rows, width), F32), sds((rows, width), BF), sds((8, width), F32)]
    _, d_one, d_one_low, sums = kernel_call(
        norm_backward,
        "first_norm_grad",
        outs,
        [],
        [parts[0], near, far, d_two, normed_one, scale_one, gains[0:1]],
    )
    outs = piece_outs(rows, width) + [
        sds((tokens, width), BF),
        sds((tokens, 3 * PART), BF),
        sds((1, 3 * PART), F32),
        sds(gates.shape, F32),
    ]
    *parts, d_rel, dproj, d_b_qkv, d_gate = kernel_call(
        attention_backward,
        "attention_backward",
        outs,
        [lens, me],
        gather_pieces(d_one_low) + [w_qkv, gates, w_out, proj],
        [
            pltpu.VMEM((tokens, PART), BF),
            pltpu.VMEM((tokens, PART), F32),
            pltpu.VMEM((tokens, PART), F32),
            pltpu.VMEM((tokens, 3 * PART), BF),
        ],
        flops=2 * tokens * width * 4 * PART,
        vmem=40,
    )
    near, far = reduce_pieces(*parts[1:])
    d_w_qkv = tn(x_rel, dproj).astype(BF).reshape(width, 3, PART)[:, :, :head_width].reshape(width, 3 * head_width)
    d_w_out = tn(d_rel, ctx_rel).astype(BF)[:, :head_width]
    d_attn = dp_sum(halves(jnp.concatenate([d_w_qkv, d_w_out], axis=1), section))
    d_gate = dp_sum(halves(d_gate.astype(BF).reshape(-1, d_gate.shape[2]), section))
    return (parts[0], near, far, d_one), (d_feed, d_attn, d_gate), (d_b_qkv, d_b_in, sums)


def head_step(pieces, embedding, target_hits):
    rows, width = pieces[0].shape
    tokens = 4 * rows
    vocab = embedding.shape[0]
    steps = vocab // VOCAB_STEP
    fixed = [pl.BlockSpec(p.shape, lambda i: (0, 0)) for p in pieces]
    wide = width + LANES
    block = pl.BlockSpec((rows, wide), lambda i: (0, 0))
    params = pltpu.CompilerParams(vmem_limit_bytes=48 * MIB)
    own, near, far, corner, powers, tops = pl.pallas_call(
        head_forward,
        name="head_forward",
        grid=(steps,),
        in_specs=fixed + [pl.BlockSpec((VOCAB_STEP, width), lambda i: (i, 0))],
        out_specs=[block] * 4
        + [
            pl.BlockSpec((VOCAB_STEP, tokens), lambda i: (i, 0)),
            pl.BlockSpec((1, 1, tokens), lambda i: (i, 0, 0)),
        ],
        out_shape=[sds((rows, wide), F32)]
        + [sds((rows, wide), BF)] * 3
        + [sds((vocab, tokens), BF), sds((steps, 1, tokens), F32)],
        scratch_shapes=[
            pltpu.VMEM((tokens, width), BF),
            pltpu.VMEM((wide, tokens), F32),
            pltpu.VMEM((1, tokens), F32),
            pltpu.VMEM((1, tokens), F32),
        ],
        compiler_params=params,
        cost_estimate=pl.CostEstimate(
            flops=4 * tokens * vocab * width, bytes_accessed=2 * vocab * (width + tokens), transcendentals=vocab * tokens
        ),
    )(*pieces, embedding)

    def finish(spreads, section):
        half_steps = vocab // 2 // BACK_STEP
        def part(which):
            first = (which * half_steps)[None].astype(jnp.int32)
            fixed_two = [pl.BlockSpec(p.shape, lambda i, f: (0, 0)) for p in pieces]
            return pl.pallas_call(
                head_backward,
                name="head_backward",
                grid_spec=pltpu.PrefetchScalarGridSpec(
                    num_scalar_prefetch=1,
                    grid=(half_steps,),
                    in_specs=fixed_two
                    + [pl.BlockSpec(s.shape, lambda i, f: (0, 0)) for s in spreads]
                    + [
                        pl.BlockSpec((BACK_STEP, tokens), lambda i, f: (i + f[0], 0)),
                        pl.BlockSpec((BACK_STEP // VOCAB_STEP, 1, tokens), lambda i, f: (i + f[0], 0, 0)),
                        pl.BlockSpec((1, tokens), lambda i, f: (0, 0)),
                    ],
                    out_specs=pl.BlockSpec((BACK_STEP, width), lambda i, f: (i, 0)),
                    scratch_shapes=[pltpu.VMEM((tokens, width), BF), pltpu.VMEM((1, tokens), F32)],
                ),
                out_shape=sds((vocab // 2, width), BF),
                compiler_params=params,
                cost_estimate=pl.CostEstimate(
                    flops=tokens * vocab * width, bytes_accessed=vocab * (width + tokens), transcendentals=0
                ),
            )(first, *pieces, *spreads, powers, tops, target_hits)

        sent = part(1 - section)
        kept = part(section)
        return plus(kept, swap(sent, "section", 1))

    return (own, near, far, corner), finish


def embed_grad(pieces, ids, firsts, so_far):
    count, width = so_far.shape
    steps = firsts.shape[0]
    tokens = ids.shape[1]
    part = pl.BlockSpec((count // steps, width), lambda i: (i, 0))
    return pl.pallas_call(
        embed_backward,
        name="embed_backward",
        grid=(steps,),
        in_specs=scalar_specs(1)
        + [pl.BlockSpec(p.shape, lambda i: (0, 0)) for p in pieces]
        + [pl.BlockSpec((1, tokens), lambda i: (0, 0)), part],
        out_specs=part,
        out_shape=sds((count, width), F32),
        input_output_aliases={2 + len(pieces): 0},
        compiler_params=pltpu.CompilerParams(vmem_limit_bytes=32 * MIB),
        cost_estimate=pl.CostEstimate(
            flops=2 * tokens * count * width, bytes_accessed=8 * count * width, transcendentals=0
        ),
    )(firsts, *pieces, ids, so_far)


def pad_parts(array, axis):
    pads = [(0, 0)] * array.ndim
    pads[axis] = (0, PART - array.shape[axis])
    return jnp.pad(array, pads)


def lookup_rows(ids, embedding):
    rows = embedding.shape[0]
    inside = (ids >= 0) & (ids < rows)
    found = jnp.where(inside[:, None], embedding[jnp.clip(ids, 0, rows - 1)], jnp.zeros((), BF))
    count = found.shape[0] // 4
    own, near, far, corner = [found[r * count : (r + 1) * count] for r in range(4)]
    near, far = reduce_pieces(near, far, corner[: count // 2], corner[count // 2 :])
    return own + near + far


def halves(array, section):
    half = array.shape[0] // 2
    mine = lax.dynamic_slice_in_dim(array, section * half, half, 0)
    other = lax.dynamic_slice_in_dim(array, (1 - section) * half, half, 0)
    return (mine.astype(F32) + swap(other, "section", 1).astype(F32)).astype(BF)


def plus(left, right):
    return (left.astype(F32) + right.astype(F32)).astype(BF)


def dp_sum(array):
    if lax.axis_size("dp") != 4:
        return lax.psum(array, "dp")
    z = lax.axis_index("dp")
    inward = plus(array, lax.ppermute(array, "dp", [(0, 1), (3, 2)]))
    total = plus(inward, lax.ppermute(inward, "dp", [(1, 2), (2, 1)]))
    outward = lax.ppermute(total, "dp", [(1, 0), (2, 3)])
    return jnp.where((z == 1) | (z == 2), total, outward)


def sum_everywhere(array):
    for axis in ("tensor", "section", "dp"):
        bit = 1
        while bit < lax.axis_size(axis):
            array = array + swap(array, axis, bit)
            bit *= 2
    return array


def shards(
    token_ids,
    targets,
    lengths,
    embedding,
    w_qkv,
    b_qv,
    w_out,
    w_in,
    b_in,
    w_down,
    norm_gains,
    shifts,
    mask_logits,
    mask_noise,
):
    section = lax.axis_index("section")
    first = section == 0
    place = lax.axis_index("tensor")
    me = place[None].astype(jnp.int32)
    tokens = token_ids.shape[1]
    rows = tokens // lax.axis_size("tensor")
    width = embedding.shape[1]
    vocab_rows = embedding.shape[0]
    vocab_start = place * vocab_rows
    head_width = w_qkv.shape[3]
    order = place ^ jnp.arange(4, dtype=jnp.int32)

    gate_own = jax.nn.sigmoid(mask_logits[0] + mask_noise[0])
    small = jnp.concatenate(
        [
            norm_gains[0],
            shifts[0],
            b_in[0][None],
            jnp.pad(b_qv[0], ((0, 0), (0, width - head_width))),
        ]
    )
    held = (w_qkv[0].reshape(width, 3 * head_width), w_out[0], w_in[0], w_down[0], small, gate_own)
    brought = jax.tree.map(lambda a: swap(a, "section", 1), held)

    def weights_of(layer):
        kept = section == layer
        wq, wo, wi, wd, vec, gates = jax.tree.map(lambda a, b: jnp.where(kept, a, b), held, brought)
        bias = jnp.concatenate(
            [
                vec[7:8, :PART],
                jnp.zeros((1, PART), F32),
                vec[8:9, :PART],
            ],
            axis=1,
        )
        wq = pad_parts(wq.reshape(width, 3, head_width), 2).reshape(width, 3 * PART)
        return (wq, bias, pad_parts(wo, 0), wi, vec[6:7], wd, vec[0:2], vec[2:6], gates)

    layers = [weights_of(0), weights_of(1)]
    lens = lax.dynamic_index_in_dim(lengths, section, 0, keepdims=False)

    def mine(ids):
        row = lax.dynamic_index_in_dim(ids, section, 0, keepdims=False)
        return row.reshape(4, rows)[order].reshape(tokens) - vocab_start

    target_local = mine(targets)
    x = lookup_rows(mine(token_ids), embedding).astype(F32) * width**0.5
    target_rows = lookup_rows(target_local, embedding)
    hidden, hidden_low, saved_first = layer_forward(x, x.astype(BF), lens, me, layers[0])
    final, final_low, saved_last = layer_forward(hidden, hidden_low, lens, me, layers[1])

    pieces = gather_pieces(final_low)
    parts, finish_head = head_step(pieces, embedding, target_local[None])
    own, near, far, corner = parts
    outs = [sds((rows, width), F32), sds((rows, width), BF), sds((8, width), F32), sds((8, rows), F32)]
    d_two, d_two_low, sums_two_last, spread = kernel_call(
        merge_head,
        "merge_head",
        outs,
        [],
        [own, swap(near, "tensor", 1), swap(far, "tensor", 2), swap(corner, "tensor", 3), target_rows]
        + [saved_last[8], saved_last[9], layers[1][6][1:2]],
    )
    spreads = [spread] + [swap(spread, "tensor", bit) for bit in (1, 2, 3)]
    d_head = finish_head(spreads, section)
    half_vocab = vocab_rows // 2
    d_head = lax.psum_scatter(d_head, "dp", scatter_dimension=0, tiled=True)

    d_x, grads_last, vecs_last = layer_backward(d_two, d_two_low, lens, me, layers[1], saved_last, section, head_width)
    outs = [sds((rows, width), F32), sds((rows, width), F32), sds((rows, width), BF), sds((8, width), F32)]
    grad_last, d_two, d_two_low, sums_two_first = kernel_call(
        norm_backward,
        "second_norm_grad",
        outs,
        [],
        list(d_x) + [saved_first[8], saved_first[9], layers[0][6][1:2]],
    )
    d_x, grads_first, vecs_first = layer_backward(d_two, d_two_low, lens, me, layers[0], saved_first, section, head_width)
    grad_first = d_x[3] + (d_x[0] + d_x[1].astype(F32) + d_x[2].astype(F32))

    dp = lax.axis_size("dp")
    share = half_vocab // dp
    firsts = lax.axis_index("dp") * share + jnp.arange(2, dtype=jnp.int32) * half_vocab
    rows_here, d_head = lax.optimization_barrier((grad_first.astype(BF), d_head))
    ids_here = mine(token_ids)[None] + vocab_start
    d_rows = jnp.zeros((2 * share, width), F32)
    for other in range(dp):
        ids = ids_here if other == 0 else swap(ids_here, "dp", other)
        rows_there = rows_here if other == 0 else swap(rows_here, "dp", other)
        d_rows = embed_grad(gather_pieces(rows_there), ids - vocab_start, firsts, d_rows)
    kept = lax.dynamic_slice_in_dim(d_rows, section * share, share, 0)
    sent = lax.dynamic_slice_in_dim(d_rows, (1 - section) * share, share, 0).astype(BF)
    d_embedding = d_head.astype(F32) + width**0.5 * (kept + swap(sent, "section", 1).astype(F32))

    def vec_rows(vecs, sums_two):
        d_b_qkv, d_b_in, sums_one = vecs
        wide = jnp.concatenate([sums_one[0:1], sums_two[0:1], sums_one[2:3], sums_one[1:2], sums_two[2:3], sums_two[1:2]])
        narrow = jnp.concatenate(
            [jnp.pad(d_b_qkv[:, :PART], ((0, 0), (0, width - PART))), jnp.pad(d_b_qkv[:, 2 * PART :], ((0, 0), (0, width - PART))), d_b_in]
        )
        spread_out = jnp.where((jnp.arange(4) == place)[:, None, None], narrow[None], 0.0).reshape(12, width)
        return jnp.concatenate([wide, spread_out])

    vecs = jnp.stack([vec_rows(vecs_first, sums_two_first), vec_rows(vecs_last, sums_two_last)])
    vecs = sum_everywhere(vecs)
    vecs = lax.dynamic_index_in_dim(vecs, section, 0, keepdims=False)
    narrow = lax.dynamic_slice_in_dim(vecs, 6 + 3 * place, 3, 0)

    def assembled(low_layer, high_layer):
        got = swap(jnp.where(first, high_layer, low_layer), "section", 1)
        return jnp.where(first, low_layer, got).astype(F32), jnp.where(first, got, high_layer).astype(F32)

    (g_in, g_down), attn, gate = jax.tree.map(assembled, grads_first, grads_last)
    attn = jnp.concatenate(attn)
    g_qkv = attn[:, : 3 * head_width].reshape(width, 3, head_width)
    g_out = attn[:, 3 * head_width :].T
    g_mask = jnp.concatenate(gate).reshape(gate_own.shape) * gate_own * (1.0 - gate_own)

    def placed_rows(low_layer, high_layer):
        got = swap(jnp.where(first, high_layer, low_layer), "section", 1)
        return jnp.where(first, jnp.stack([low_layer, got]), jnp.stack([got, high_layer]))

    return (
        placed_rows(hidden, final)[None],
        placed_rows(grad_first, grad_last)[None],
        d_embedding,
        g_qkv[None],
        narrow[None, 0:2, :head_width],
        g_out[None],
        g_in[None],
        narrow[None, 2],
        g_down[None],
        vecs[None, 0:2],
        vecs[None, 2:6],
        g_mask[None],
    )


def solution(mesh):
    placed = (
        P("dp", None),
        P("dp", None),
        P("dp", None),
        P("tensor", None),
        P("section", None, None, "tensor"),
        P("section", None, "tensor"),
        P("section", "tensor", None),
        P("section", None, "tensor"),
        P("section", "tensor"),
        P("section", "tensor", None),
        P("section", None, None),
        P("section", None, None),
        P("section", "tensor", None, None),
        P("section", "tensor", None, None),
    )
    return jax.shard_map(
        shards,
        mesh=mesh,
        in_specs=placed,
        out_specs=(
            P("section", "dp", "tensor", None),
            P("section", "dp", "tensor", None),
            P(("tensor", "section", "dp"), None),
            P("section", None, None, "tensor"),
            P("section", None, "tensor"),
            P("section", "tensor", None),
            P("section", None, "tensor"),
            P("section", "tensor"),
            P("section", "tensor", None),
            P("section", None, None),
            P("section", None, None),
            P("section", "tensor", None, None),
        ),
        check_vma=False,
    )
```

time: 2890 us -> 936 us (0.32)
  waiting for transfers between devices: 1600 us -> 329 us
  matrix products: 425 us -> 10.1 us
  local copies, waits for them, and re-layouts: 440 us -> 93.2 us
  other arithmetic: 318 us -> 83.4 us
  starting transfers between devices: 12.7 us -> 211 us
  Pallas kernels: 0 us -> 178 us
  blocking collectives: 59.7 us -> 0 us
    reduce_scatter x17 -> x1, waiting for transfers between devices: 1010 us -> 0.01 us  [shards(): d_head = lax.psum_scatter(d_head, 'dp', scatter_dimension=0, tiled=True)]
    dot_general x57 -> x8, matrix products: 372 us -> 10.1 us  [tn(): lax.dot_general(left, right, (((0,), (0,)), ((), ())), preferred_element_...]
    ppermute x4 -> x146, waiting for transfers between devices: 4.72 us -> 329 us  [the longest x128 140 us: swap(): return lax.ppermute(array, axis, [(i, i ^ bit) for i in range(count)])]
    all_gather x16 -> x0, waiting for transfers between devices: 309 us -> none  [gather_rows(): return lax.all_gather(shard, 'tensor', axis=0, tiled=True)]
    psum x1 -> x0, waiting for transfers between devices: 283 us -> none  [shards(): lax.psum((g_qkv, g_bqv, g_out, g_in, g_bin, g_down, g_mask, g_gains, g_sh...]
    gather x35 -> x4, local copies, waits for them, and re-layouts: 247 us -> 23.3 us  [the longest x2 22.2 us: lookup_rows(): embedding[jnp.clip(ids, 0, rows - 1)]]
    ppermute x4 -> x146, starting transfers between devices: 7.63 us -> 211 us  [the longest x128 172 us: swap(): return lax.ppermute(array, axis, [(i, i ^ bit) for i in range(count)])]
    pallas_call x0 -> x23, Pallas kernels: none -> 178 us  [the longest x16 82 us: kernel_call(): pl.pallas_call(kernel, name=name, out_shape=outs, in_specs=scalar_specs(l...]
  transfers between devices with their start and end apart: 38 -> 147, of which waited for: 29 -> 57; matrix products, arithmetic and copies ran while one was open for 21% -> 16% of each run, Pallas kernels for 0% -> 16%
where the time goes in v1:
time: 936 us; the launch traced here: 921 us
  waiting for transfers between devices  329 us (35%)
  starting transfers between devices  211 us (23%)
  Pallas kernels  178 us (19%)
  local copies, waits for them, and re-layouts  93.2 us (10%)
  other arithmetic  83.4 us (9%)
  between operations  17.2 us (2%)
  matrix products  10.1 us (1%)
    ppermute x128, starting transfers between devices, swap(): return lax.ppermute(array, axis, [(i, i ^ bit) for i in range(count)])  172 us
    ppermute x128, waiting for transfers between devices, swap(): return lax.ppermute(array, axis, [(i, i ^ bit) for i in range(count)])  140 us
    ppermute x6, waiting for transfers between devices, dp_sum(): total = plus(inward, lax.ppermute(inward, 'dp', [(1, 2), (2, 1)]))  99.1 us
    pallas_call x16, Pallas kernels, kernel_call(): pl.pallas_call(kernel, name=name, out_shape=outs, in_specs=scalar_specs(l...  82 us
    pallas_call x1, Pallas kernels, head_step(): pl.pallas_call(head_forward, name='head_forward', grid=(steps,), in_specs...  54.9 us
    ppermute x6, waiting for transfers between devices, dp_sum(): outward = lax.ppermute(total, 'dp', [(1, 0), (2, 3)])  50.3 us
    ppermute x6, waiting for transfers between devices, dp_sum(): inward = plus(array, lax.ppermute(array, 'dp', [(0, 1), (3, 2)]))  39.4 us
    unnamed x350, local copies, waits for them, and re-layouts  37.4 us
  transfers between devices with their start and end apart: 147, of which 57 were waited for; matrix products, arithmetic and copies ran while one was open for 16% of the time, Pallas kernels for 16%

profile of v1, /device:TPU:17, one launch (start us, length us, event | category | flops | bytes accessed | tf_op | source)
XLA Modules:
  0.0 921.3 jit_solution(7439809449765923135)
XLA Ops:
  7.3 5.4 add_divide_fusion
  15.8 10.3 %gather_fusion.1 = bf16[1024,768]{1,0:T(8,128)(2,1)S(1)} fusion(bf16[7680,768]{1,0:T(8,128)(2,1)} %refs_5_.1, s32[1024]{0:T(1024)S(1)} %broadcast_clamp_fusion.1), kind=kCustom, calls=%fused_computation.1 | custom fusion | bytes 3149824 | tf_op jit(solution)/shard_map/gather | solution.py:621
  39.1 5.7 collective-permute-done.3
  58.9 5.7 broadcast_select_fusion.2
  64.7 12.3 %attention_forward.2 = (f32[256,768]{1,0:T(8,128)S(1)}, bf16[256,768]{1,0:T(8,128)(2,1)S(1)}, bf16[256,768]{1,0:T(8,128)(2,1)S(1)}, bf16[128,768]{1,0:T(8,128)(2...) custom-call(s32[4]{0:T(128)S(1)} %fusion.14.len_ref, ...), custom_call_target="tpu_custom_call" | custom-call | flops 1610612736 | bytes 11930624 | tf_op jit(solution)/shard_map/attention_forward/pallas_call | solution.py:50
  79.3 3.2 collective-permute-start.20
  84.4 4.4 collective-permute-done.14
  90.3 6.9 collective-permute-done.13.near
  100.6 4.9 collective-permute-done.16.refs_1_
  108.3 2.9 collective-permute-done.18.refs_3_
  111.2 3.3 feed_forward.2
  118.4 3.0 collective-permute-done.22
  123.1 6.4 collective-permute-done.23.near
  135.9 6.2 collective-permute-done.26.refs_1_
  158.7 12.8 %attention_forward.3 = (f32[256,768]{1,0:T(8,128)S(1)}, bf16[256,768]{1,0:T(8,128)(2,1)S(1)}, bf16[256,768]{1,0:T(8,128)(2,1)S(1)}, bf16[128,768]{1,0:T(8,128)(2...) custom-call(s32[4]{0:T(128)S(1)} %copy-done.93, ...), custom_call_target="tpu_custom_call" | custom-call | flops 1610612736 | bytes 11930624 | tf_op jit(solution)/shard_map/attention_forward/pallas_call | solution.py:50
  173.9 2.9 collective-permute-done.30
  180.2 3.4 collective-permute-done.31.near
  188.0 8.6 collective-permute-done.34.refs_1_
  201.6 11.8 %gather_fusion.3 = bf16[1024,768]{1,0:T(8,128)(2,1)} fusion(bf16[7680,768]{1,0:T(8,128)(2,1)} %refs_5_.1, s32[1024]{0:T(1024)} %broadcast_clamp_fusion), kind=kCustom, calls=%fused_computation.3 | custom fusion | bytes 3149824 | tf_op jit(solution)/shard_map/gather | solution.py:621
  217.2 5.0 feed_forward.3
  250.0 4.4 collective-permute-done.43.refs_1_
  260.7 54.9 %head_forward.1 = (f32[256,896]{1,0:T(8,128)S(1)}, bf16[256,896]{1,0:T(8,128)(2,1)S(1)}, bf16[256,896]{1,0:T(8,128)(2,1)S(1)}, bf16[256,896]{1,0:T(8,128)(2,1)S(...) custom-call(bf16[256,768]{1,0:T(8,128)(2,1)S(1)} %get-tuple-element.143.refs_0_, ...), custom_call_target="tpu_custom_call" | custom-call | flops 24159191040 | bytes 27525120 | tf_op jit(solution)/shard_map/head_forward/pallas_call | solution.py:530
  319.9 3.2 collective-permute-start.102
  324.2 5.3 collective-permute-done.48.far
  342.1 10.4 %head_backward.3 = bf16[3840,768]{1,0:T(8,128)(2,1)} custom-call(s32[1]{0:T(128)} %bitcast.24.first_ref, bf16[256,768]{1,0:T(8,128)(2,1)S(1)} %get-tuple-element.143.refs_0_, bf16[256,768]{1,0:T(8,128)(2,1)S(1)} %collective-permute-done.43.refs_1_, bf16[256,768]{1,0:T(8,128)(2,1)S(1)} %collective-permute-done.44.refs_2_, ...), custom_call_target="tpu_custom_call" | custom-call | flops 6039797760 | bytes 13762560 | tf_op jit(solution)/shard_map/head_backward/pallas_call | solution.py:560
  352.5 29.0 %collective-permute-start.90 = (bf16[3840,768]{1,0:T(8,128)(2,1)}, bf16[3840,768]{1,0:T(8,128)(2,1)}, u32[]{:S(2)}, u32[]{:S(2)}) collective-permute-start(bf16[3840,768]{1,0:T(8,128)(2,1)} %head_backward.3), channel_id=1, source_target_pairs={{0,16},{16,0},{1,17},{17,1},{2,18},{18,2},{3,19},{19,3},{4,20},{20... | collective-permute-start | bytes 17694728 | tf_op jit(solution)/shard_map/ppermute | solution.py:64
  386.4 4.2 collective-permute-done.56.refs_3_
  391.2 2.8 feed_backward.2
  406.6 5.1 collective-permute-done.59.near
  414.9 10.1 %head_backward.2 = bf16[3840,768]{1,0:T(8,128)(2,1)} custom-call(s32[1]{0:T(128)} %bitcast.23.first_ref, bf16[256,768]{1,0:T(8,128)(2,1)S(1)} %get-tuple-element.143.refs_0_, bf16[256,768]{1,0:T(8,128)(2,1)S(1)} %collective-permute-done.43.refs_1_, bf16[256,768]{1,0:T(8,128)(2,1)S(1)} %collective-permute-done.44.refs_2_, bf16[128,768]{1,0:T(8,128)(2,1)S(1)} %copy-done.38, ...), custom_call_target="tpu_custom_call" | custom-call | flops 6039797760 | bytes 13762560 | tf_op jit(solution)/shard_map/head_backward/pallas_call | solution.py:560
  431.3 18.5 %attention_backward.2 = (f32[256,768]{1,0:T(8,128)S(1)}, bf16[256,768]{1,0:T(8,128)(2,1)S(1)}, bf16[256,768]{1,0:T(8,128)(2,1)S(1)}, bf16[128,768]{1,0:T(8,128)(...) custom-call(s32[4]{0:T(128)S(1)} %copy-done.94, ...), custom_call_target="tpu_custom_call" | custom-call | flops 1610612736 | bytes 16124928 | tf_op jit(solution)/shard_map/attention_backward/pallas_call | solution.py:50
  458.2 6.7 collective-permute-start.118
  471.6 7.0 add_convert_fusion
  494.8 5.5 collective-permute-done.119
  500.4 3.2 collective-permute-start.120
  506.7 9.8 %collective-permute-start.128 = (bf16[768,768]{1,0:T(8,128)(2,1)S(1)}, bf16[768,768]{1,0:T(8,128)(2,1)S(1)}, u32[]{:S(2)}, u32[]{:S(2)}) collective-permute-start(bf16[768,768]{1,0:T(8,128)(2,1)S(1)} %get-tuple-element.292), channel_id=1, source_target_pairs={{0,16},{16,0},{1,17},{17,1},{2,18},{18,2},{3,19},{19,3},{4,20},{20... | collective-permute-start | bytes 3538952 | tf_op jit(solution)/shard_map/ppermute | solution.py:64
  518.1 15.9 %collective-permute-done.142 = bf16[768,512]{1,0:T(8,128)(2,1)S(1)} collective-permute-done((bf16[768,512]{1,0:T(8,128)(2,1)S(1)}, bf16[768,512]{1,0:T(8,128)(2,1)S(1)}, u32[]{:S(2)}, u32[]{:S(2)}) %collective-permute-start.142) | collective-permute-done | bytes 786464 | tf_op jit(solution)/shard_map/ppermute | solution.py:643
  535.9 5.1 collective-permute-done.77.far
  543.2 72.6 %collective-permute-done.120 = bf16[384,768]{0,1:T(8,128)(2,1)S(1)} collective-permute-done((bf16[384,768]{0,1:T(8,128)(2,1)S(1)}, bf16[384,768]{0,1:T(8,128)(2,1)S(1)}, u32[]{:S(2)}, u32[]{:S(2)}) %collective-permute-start.120) | collective-permute-done | bytes 589856 | tf_op jit(solution)/shard_map/ppermute | solution.py:644
  625.9 18.9 %attention_backward.3 = (f32[256,768]{1,0:T(8,128)S(1)}, bf16[256,768]{1,0:T(8,128)(2,1)S(1)}, bf16[256,768]{1,0:T(8,128)(2,1)S(1)}, bf16[128,768]{1,0:T(8,128)(...) custom-call(s32[4]{0:T(128)S(1)} %copy-done.94, ...), custom_call_target="tpu_custom_call" | custom-call | flops 1610612736 | bytes 16124928 | tf_op jit(solution)/shard_map/attention_backward/pallas_call | solution.py:50
  660.8 5.5 collective-permute-start.114
  668.2 3.7 collective-permute-done.124
  674.8 3.1 collective-permute-start.126
  677.9 3.9 collective-permute-done.126
  684.5 6.6 collective-permute-done.127
  698.5 9.6 %collective-permute-done.115 = bf16[384,768]{0,1:T(8,128)(2,1)S(1)} collective-permute-done((bf16[384,768]{0,1:T(8,128)(2,1)S(1)}, bf16[384,768]{0,1:T(8,128)(2,1)S(1)}, u32[]{:S(2)}, u32[]{:S(2)}) %collective-permute-start.115) | collective-permute-done | bytes 589856 | tf_op jit(solution)/shard_map/ppermute | solution.py:643
  708.1 3.5 collective-permute-start.130
  716.5 8.4 collective-permute-done.138
  725.2 3.5 collective-permute-start.139
  728.8 18.6 %collective-permute-done.116 = bf16[384,768]{0,1:T(8,128)(2,1)S(1)} collective-permute-done((bf16[384,768]{0,1:T(8,128)(2,1)S(1)}, bf16[384,768]{0,1:T(8,128)(2,1)S(1)}, u32[]{:S(2)}, u32[]{:S(2)}) %collective-permute-start.116) | collective-permute-done | bytes 589856 | tf_op jit(solution)/shard_map/ppermute | solution.py:644
  747.4 7.1 collective-permute-start.86
  756.4 7.9 collective-permute-done.139
  769.9 4.1 collective-permute-start.140
  780.9 4.2 collective-permute-done.144
  785.6 3.2 collective-permute-start.103
  789.7 46.1 %collective-permute-done.140 = bf16[768,512]{1,0:T(8,128)(2,1)} collective-permute-done((bf16[768,512]{1,0:T(8,128)(2,1)}, bf16[768,512]{1,0:T(8,128)(2,1)}, u32[]{:S(2)}, u32[]{:S(2)}) %collective-permute-start.140) | collective-permute-done | bytes 786464 | tf_op jit(solution)/shard_map/ppermute | solution.py:645
  849.2 9.5 %collective-permute-done.97.refs_0_ = bf16[256,768]{1,0:T(8,128)(2,1)S(1)} collective-permute-done((bf16[256,768]{1,0:T(8,128)(2,1)S(1)}, bf16[256,768]{1,0:T(8,128)(2,1)S(1)}, u32[]{:S(2)}, u32[]{:S(2)}) %collective-permute-start.97) | collective-permute-done | bytes 393248 | tf_op jit(solution)/shard_map/ppermute | solution.py:64
  862.0 3.7 collective-permute-done.112.refs_4_
  867.8 5.0 embed_backward.4.refs_6_
  872.9 4.9 collective-permute-start.145
  883.3 5.0 embed_backward.5.refs_6_
  890.9 5.0 embed_backward.6.refs_6_
  896.0 5.0 embed_backward.7
  905.2 4.2 fusion
  (822 shorter events, 305.1 us)
Async XLA Ops:
  7.2 773.7 %reduce-scatter.2.cloned.1.call-start = ((), (), s32[]{:S(2)}) async-start(), calls=%async_computation.1 | async-start | bytes 7372800 | tf_op jit(solution)/shard_map/reduce_scatter | solution.py:740
  12.7 46.2 %collective-permute-start.10 = (f32[3,512,512]{2,1,0:T(8,128)}, f32[3,512,512]{2,1,0:T(8,128)}, u32[]{:S(2)}, u32[]{:S(2)}) collective-permute-start(f32[3,512,512]{2,1,0:T(8,128)} %bitcast.10), channel_id=1, source_target_pairs={{0,16},{16,0},{1,17},{17,1},{2,18},{18,2},{3,19},{19,3},{4,20},{20... | collective-permute-start | bytes 9437192 | tf_op jit(solution)/shard_map/ppermute | solution.py:64
  29.1 22.0 %collective-permute-start.8 = (bf16[768,576]{0,1:T(8,128)(2,1)S(1)}, bf16[768,576]{0,1:T(8,128)(2,1)}, u32[]{:S(2)}, u32[]{:S(2)}) collective-permute-start(bf16[768,576]{0,1:T(8,128)(2,1)S(1)} %bitcast.127), channel_id=1, source_target_pairs={{0,16},{16,0},{1,17},{17,1},{2,18},{18,2},{3,19},{19,3},{4,20},{20... | collective-permute-start | bytes 2654216 | tf_op jit(solution)/shard_map/ppermute | solution.py:64
  33.3 16.0 %collective-permute-start.11 = (bf16[192,768]{1,0:T(8,128)(2,1)}, bf16[192,768]{1,0:T(8,128)(2,1)S(1)}, u32[]{:S(2)}, u32[]{:S(2)}) collective-permute-start(bf16[192,768]{1,0:T(8,128)(2,1)} %bitcast.11), channel_id=1, source_target_pairs={{0,16},{16,0},{1,17},{17,1},{2,18},{18,2},{3,19},{19,3},{4,20},{20... | collective-permute-start | bytes 884744 | tf_op jit(solution)/shard_map/ppermute | solution.py:64
  79.3 20.0 %collective-permute-start.20 = (bf16[768,768]{1,0:T(8,128)(2,1)S(1)}, bf16[768,768]{1,0:T(8,128)(2,1)S(1)}, u32[]{:S(2)}, u32[]{:S(2)}) collective-permute-start(bf16[768,768]{1,0:T(8,128)(2,1)S(1)} %bitcast.119), channel_id=1, source_target_pairs={{0,16},{16,0},{1,17},{17,1},{2,18},{18,2},{3,19},{19,3},{4,20},{20... | collective-permute-start | bytes 3538952 | tf_op jit(solution)/shard_map/ppermute | solution.py:64
  82.6 24.5 %collective-permute-start.21 = (bf16[768,768]{1,0:T(8,128)(2,1)S(1)}, bf16[768,768]{1,0:T(8,128)(2,1)S(1)}, u32[]{:S(2)}, u32[]{:S(2)}) collective-permute-start(bf16[768,768]{1,0:T(8,128)(2,1)S(1)} %bitcast.120), channel_id=1, source_target_pairs={{0,16},{16,0},{1,17},{17,1},{2,18},{18,2},{3,19},{19,3},{4,20},{20... | collective-permute-start | bytes 3538952 | tf_op jit(solution)/shard_map/ppermute | solution.py:64
  198.1 15.4 %collective-permute-start.36 = (bf16[128,768]{1,0:T(8,128)(2,1)}, bf16[128,768]{1,0:T(8,128)(2,1)}, u32[]{:S(2)}, u32[]{:S(2)}) collective-permute-start(bf16[128,768]{1,0:T(8,128)(2,1)} %slice.539), channel_id=1, source_target_pairs={{0,2},{1,3},{2,0},{3,1},{4,6},{5,7},{6,4},{7,5},{8,10},{9,11},{10,... | collective-permute-start | bytes 589832 | tf_op jit(solution)/shard_map/ppermute | solution.py:64
  257.0 62.8 %collective-permute-start.53 = (bf16[256,768]{1,0:T(8,128)(2,1)S(1)}, bf16[256,768]{1,0:T(8,128)(2,1)S(1)}, u32[]{:S(2)}, u32[]{:S(2)}) collective-permute-start(bf16[256,768]{1,0:T(8,128)(2,1)S(1)} %pad_maximum_fusion.12), channel_id=1, source_target_pairs={{0,2},{1,3},{2,0},{3,1},{4,6},{5,7},{6,4},{7,5},{8,10},{9,11},{10,... | collective-permute-start | bytes 1179656 | tf_op jit(solution)/shard_map/ppermute | solution.py:64
  259.1 60.8 %collective-permute-start.51 = (bf16[256,768]{1,0:T(8,128)(2,1)S(1)}, bf16[256,768]{1,0:T(8,128)(2,1)S(1)}, u32[]{:S(2)}, u32[]{:S(2)}) collective-permute-start(bf16[256,768]{1,0:T(8,128)(2,1)S(1)} %pad_maximum_fusion.11), channel_id=1, source_target_pairs={{0,1},{1,0},{2,3},{3,2},{4,5},{5,4},{6,7},{7,6},{8,9},{9,8},{10,11... | collective-permute-start | bytes 1179656 | tf_op jit(solution)/shard_map/ppermute | solution.py:64
  319.7 32.7 %collective-permute-start.96 = (s32[1,1024]{1,0:T(1,128)}, s32[1,1024]{1,0:T(1,128)}, u32[]{:S(2)}, u32[]{:S(2)}) collective-permute-start(s32[1,1024]{1,0:T(1,128)} %bitcast.59), channel_id=1, source_target_pairs={{0,12},{4,8},{8,4},{12,0},{1,13},{5,9},{9,5},{13,1},{2,14},{6,10},... | collective-permute-start | bytes 12296 | tf_op jit(solution)/shard_map/ppermute | solution.py:64
  319.9 62.9 %collective-permute-start.102 = (s32[1,1024]{1,0:T(1,128)}, s32[1,1024]{1,0:T(1,128)}, u32[]{:S(2)}, u32[]{:S(2)}) collective-permute-start(s32[1,1024]{1,0:T(1,128)} %bitcast.59), channel_id=1, source_target_pairs={{0,8},{4,12},{8,0},{12,4},{1,9},{5,13},{9,1},{13,5},{2,10},{6,14},... | collective-permute-start | bytes 12296 | tf_op jit(solution)/shard_map/ppermute | solution.py:64
  338.4 64.0 %collective-permute-start.108 = (s32[1,1024]{1,0:T(1,128)}, s32[1,1024]{1,0:T(1,128)S(1)}, u32[]{:S(2)}, u32[]{:S(2)}) collective-permute-start(s32[1,1024]{1,0:T(1,128)} %bitcast.59), channel_id=1, source_target_pairs={{0,4},{4,0},{8,12},{12,8},{1,5},{5,1},{9,13},{13,9},{2,6},{6,2},{1... | collective-permute-start | bytes 12296 | tf_op jit(solution)/shard_map/ppermute | solution.py:64
  339.7 44.3 %collective-permute-start.54 = (bf16[256,768]{1,0:T(8,128)(2,1)}, bf16[256,768]{1,0:T(8,128)(2,1)S(1)}, u32[]{:S(2)}, u32[]{:S(2)}) collective-permute-start(bf16[256,768]{1,0:T(8,128)(2,1)} %copy-done.107), channel_id=1, source_target_pairs={{0,1},{1,0},{2,3},{3,2},{4,5},{5,4},{6,7},{7,6},{8,9},{9,8},{10,11... | collective-permute-start | bytes 1179656 | tf_op jit(solution)/shard_map/ppermute | solution.py:64
  340.5 44.4 %collective-permute-start.55 = (bf16[256,768]{1,0:T(8,128)(2,1)}, bf16[256,768]{1,0:T(8,128)(2,1)S(1)}, u32[]{:S(2)}, u32[]{:S(2)}) collective-permute-start(bf16[256,768]{1,0:T(8,128)(2,1)} %copy-done.107), channel_id=1, source_target_pairs={{0,2},{1,3},{2,0},{3,1},{4,6},{5,7},{6,4},{7,5},{8,10},{9,11},{10,... | collective-permute-start | bytes 1179656 | tf_op jit(solution)/shard_map/ppermute | solution.py:64
  352.5 118.4 %collective-permute-start.90 = (bf16[3840,768]{1,0:T(8,128)(2,1)}, bf16[3840,768]{1,0:T(8,128)(2,1)}, u32[]{:S(2)}, u32[]{:S(2)}) collective-permute-start(bf16[3840,768]{1,0:T(8,128)(2,1)} %head_backward.3), channel_id=1, source_target_pairs={{0,16},{16,0},{1,17},{17,1},{2,18},{18,2},{3,19},{19,3},{4,20},{20... | collective-permute-start | bytes 17694728 | tf_op jit(solution)/shard_map/ppermute | solution.py:64
  385.8 18.0 %collective-permute-start.42 = (f32[256,768]{1,0:T(8,128)S(1)}, f32[256,768]{1,0:T(8,128)S(1)}, u32[]{:S(2)}, u32[]{:S(2)}) collective-permute-start(f32[256,768]{1,0:T(8,128)S(1)} %broadcast_select_fusion.26), channel_id=1, source_target_pairs={{0,16},{16,0},{1,17},{17,1},{2,18},{18,2},{3,19},{19,3},{4,20},{20... | collective-permute-start | bytes 2359304 | tf_op jit(solution)/shard_map/ppermute | solution.py:64
  399.3 27.9 %collective-permute-start.132 = (bf16[768,768]{1,0:T(8,128)(2,1)S(1)}, bf16[768,768]{1,0:T(8,128)(2,1)S(1)}, u32[]{:S(2)}, u32[]{:S(2)}) collective-permute-start(bf16[768,768]{1,0:T(8,128)(2,1)S(1)} %get-tuple-element.294), channel_id=1, source_target_pairs={{0,16},{16,0},{1,17},{17,1},{2,18},{18,2},{3,19},{19,3},{4,20},{20... | collective-permute-start | bytes 3538952 | tf_op jit(solution)/shard_map/ppermute | solution.py:64
  428.8 57.5 %collective-permute-start.133 = (bf16[768,768]{1,0:T(8,128)(2,1)}, bf16[768,768]{1,0:T(8,128)(2,1)}, u32[]{:S(2)}, u32[]{:S(2)}) collective-permute-start(bf16[768,768]{1,0:T(8,128)(2,1)} %add_convert_fusion.3), channel_id=1, source_target_pairs={{0,4},{12,8},{1,5},{13,9},{2,6},{14,10},{3,7},{15,11},{16,20},{28,... | collective-permute-start | bytes 3538952 | tf_op jit(solution)/shard_map/ppermute | solution.py:643
  458.2 20.4 %collective-permute-start.118 = (bf16[384,768]{0,1:T(8,128)(2,1)}, bf16[384,768]{0,1:T(8,128)(2,1)}, u32[]{:S(2)}, u32[]{:S(2)}) collective-permute-start(bf16[384,768]{0,1:T(8,128)(2,1)} %fusion.1), channel_id=1, source_target_pairs={{0,16},{16,0},{1,17},{17,1},{2,18},{18,2},{3,19},{19,3},{4,20},{20... | collective-permute-start | bytes 1769480 | tf_op jit(solution)/shard_map/ppermute | solution.py:64
  466.7 14.6 %collective-permute-start.141 = (bf16[768,512]{1,0:T(8,128)(2,1)}, bf16[768,512]{1,0:T(8,128)(2,1)}, u32[]{:S(2)}, u32[]{:S(2)}) collective-permute-start(bf16[768,512]{1,0:T(8,128)(2,1)} %constant_dynamic-slice_fusion), channel_id=1, source_target_pairs={{0,16},{16,0},{1,17},{17,1},{2,18},{18,2},{3,19},{19,3},{4,20},{20... | collective-permute-start | bytes 2359304 | tf_op jit(solution)/shard_map/ppermute | solution.py:64
  470.9 14.5 %collective-permute-start.71 = (bf16[256,768]{1,0:T(8,128)(2,1)S(1)}, bf16[256,768]{1,0:T(8,128)(2,1)S(1)}, u32[]{:S(2)}, u32[]{:S(2)}) collective-permute-start(bf16[256,768]{1,0:T(8,128)(2,1)S(1)} %get-tuple-element.170.refs_0_), channel_id=1, source_target_pairs={{0,2},{1,3},{2,0},{3,1},{4,6},{5,7},{6,4},{7,5},{8,10},{9,11},{10,... | collective-permute-start | bytes 1179656 | tf_op jit(solution)/shard_map/ppermute | solution.py:64
  480.0 20.2 %collective-permute-start.119 = (bf16[384,768]{0,1:T(8,128)(2,1)S(1)}, bf16[384,768]{0,1:T(8,128)(2,1)S(1)}, u32[]{:S(2)}, u32[]{:S(2)}) collective-permute-start(bf16[384,768]{0,1:T(8,128)(2,1)S(1)} %add_convert_fusion.15), channel_id=1, source_target_pairs={{0,4},{12,8},{1,5},{13,9},{2,6},{14,10},{3,7},{15,11},{16,20},{28,... | collective-permute-start | bytes 1769480 | tf_op jit(solution)/shard_map/ppermute | solution.py:643
  482.9 51.1 %collective-permute-start.142 = (bf16[768,512]{1,0:T(8,128)(2,1)S(1)}, bf16[768,512]{1,0:T(8,128)(2,1)S(1)}, u32[]{:S(2)}, u32[]{:S(2)}) collective-permute-start(bf16[768,512]{1,0:T(8,128)(2,1)S(1)} %add_convert_fusion.9), channel_id=1, source_target_pairs={{0,4},{12,8},{1,5},{13,9},{2,6},{14,10},{3,7},{15,11},{16,20},{28,... | collective-permute-start | bytes 2359304 | tf_op jit(solution)/shard_map/ppermute | solution.py:643
  488.7 132.2 %collective-permute-start.134 = (bf16[768,768]{1,0:T(8,128)(2,1)S(1)}, bf16[768,768]{1,0:T(8,128)(2,1)S(1)}, u32[]{:S(2)}, u32[]{:S(2)}) collective-permute-start(bf16[768,768]{1,0:T(8,128)(2,1)S(1)} %add_convert_fusion.2), channel_id=1, source_target_pairs={{4,8},{8,4},{5,9},{9,5},{6,10},{10,6},{7,11},{11,7},{20,24},{24,20... | collective-permute-start | bytes 3538952 | tf_op jit(solution)/shard_map/ppermute | solution.py:644
  494.1 22.5 %collective-permute-start.76 = (bf16[128,768]{1,0:T(8,128)(2,1)S(1)}, bf16[128,768]{1,0:T(8,128)(2,1)S(1)}, u32[]{:S(2)}, u32[]{:S(2)}) collective-permute-start(bf16[128,768]{1,0:T(8,128)(2,1)S(1)} %get-tuple-element.176), channel_id=1, source_target_pairs={{0,1},{1,0},{2,3},{3,2},{4,5},{5,4},{6,7},{7,6},{8,9},{9,8},{10,11... | collective-permute-start | bytes 589832 | tf_op jit(solution)/shard_map/ppermute | solution.py:64
  500.4 115.4 %collective-permute-start.120 = (bf16[384,768]{0,1:T(8,128)(2,1)S(1)}, bf16[384,768]{0,1:T(8,128)(2,1)S(1)}, u32[]{:S(2)}, u32[]{:S(2)}) collective-permute-start(bf16[384,768]{0,1:T(8,128)(2,1)S(1)} %add_convert_fusion.14), channel_id=1, source_target_pairs={{4,8},{8,4},{5,9},{9,5},{6,10},{10,6},{7,11},{11,7},{20,24},{24,20... | collective-permute-start | bytes 1769480 | tf_op jit(solution)/shard_map/ppermute | solution.py:644
  506.7 116.1 %collective-permute-start.128 = (bf16[768,768]{1,0:T(8,128)(2,1)S(1)}, bf16[768,768]{1,0:T(8,128)(2,1)S(1)}, u32[]{:S(2)}, u32[]{:S(2)}) collective-permute-start(bf16[768,768]{1,0:T(8,128)(2,1)S(1)} %get-tuple-element.292), channel_id=1, source_target_pairs={{0,16},{16,0},{1,17},{17,1},{2,18},{18,2},{3,19},{19,3},{4,20},{20... | collective-permute-start | bytes 3538952 | tf_op jit(solution)/shard_map/ppermute | solution.py:64
  516.5 19.4 %collective-permute-start.75 = (bf16[256,768]{1,0:T(8,128)(2,1)S(1)}, bf16[256,768]{1,0:T(8,128)(2,1)S(1)}, u32[]{:S(2)}, u32[]{:S(2)}) collective-permute-start(bf16[256,768]{1,0:T(8,128)(2,1)S(1)} %pad_maximum_fusion.17), channel_id=1, source_target_pairs={{0,1},{1,0},{2,3},{3,2},{4,5},{5,4},{6,7},{7,6},{8,9},{9,8},{10,11... | collective-permute-start | bytes 1179656 | tf_op jit(solution)/shard_map/ppermute | solution.py:64
  542.1 76.6 %collective-permute-start.78 = (bf16[256,768]{1,0:T(8,128)(2,1)S(1)}, bf16[256,768]{1,0:T(8,128)(2,1)S(1)}, u32[]{:S(2)}, u32[]{:S(2)}) collective-permute-start(bf16[256,768]{1,0:T(8,128)(2,1)S(1)} %get-tuple-element.181.refs_0_), channel_id=1, source_target_pairs={{0,1},{1,0},{2,3},{3,2},{4,5},{5,4},{6,7},{7,6},{8,9},{9,8},{10,11... | collective-permute-start | bytes 1179656 | tf_op jit(solution)/shard_map/ppermute | solution.py:64
  542.4 78.4 %collective-permute-start.79 = (bf16[256,768]{1,0:T(8,128)(2,1)S(1)}, bf16[256,768]{1,0:T(8,128)(2,1)S(1)}, u32[]{:S(2)}, u32[]{:S(2)}) collective-permute-start(bf16[256,768]{1,0:T(8,128)(2,1)S(1)} %get-tuple-element.181.refs_0_), channel_id=1, source_target_pairs={{0,2},{1,3},{2,0},{3,1},{4,6},{5,7},{6,4},{7,5},{8,10},{9,11},{10,... | collective-permute-start | bytes 1179656 | tf_op jit(solution)/shard_map/ppermute | solution.py:64
  615.8 41.0 %collective-permute-start.143 = (bf16[768,512]{1,0:T(8,128)(2,1)}, bf16[768,512]{1,0:T(8,128)(2,1)}, u32[]{:S(2)}, u32[]{:S(2)}) collective-permute-start(bf16[768,512]{1,0:T(8,128)(2,1)} %add_convert_fusion.8), channel_id=1, source_target_pairs={{4,8},{8,4},{5,9},{9,5},{6,10},{10,6},{7,11},{11,7},{20,24},{24,20... | collective-permute-start | bytes 2359304 | tf_op jit(solution)/shard_map/ppermute | solution.py:644
  618.7 148.9 %collective-permute-start.121 = (bf16[384,768]{0,1:T(8,128)(2,1)}, bf16[384,768]{0,1:T(8,128)(2,1)}, u32[]{:S(2)}, u32[]{:S(2)}) collective-permute-start(bf16[384,768]{0,1:T(8,128)(2,1)} %add_convert_fusion.13), channel_id=1, source_target_pairs={{4,0},{8,12},{5,1},{9,13},{6,2},{10,14},{7,3},{11,15},{20,16},{24,... | collective-permute-start | bytes 1769480 | tf_op jit(solution)/shard_map/ppermute | solution.py:645
  624.4 70.8 %collective-permute-start.129 = (bf16[768,768]{1,0:T(8,128)(2,1)}, bf16[768,768]{1,0:T(8,128)(2,1)}, u32[]{:S(2)}, u32[]{:S(2)}) collective-permute-start(bf16[768,768]{1,0:T(8,128)(2,1)} %add_convert_fusion.6), channel_id=1, source_target_pairs={{0,4},{12,8},{1,5},{13,9},{2,6},{14,10},{3,7},{15,11},{16,20},{28,... | collective-permute-start | bytes 3538952 | tf_op jit(solution)/shard_map/ppermute | solution.py:643
  644.8 21.5 %collective-permute-start.84 = (bf16[128,768]{1,0:T(8,128)(2,1)}, bf16[128,768]{1,0:T(8,128)(2,1)}, u32[]{:S(2)}, u32[]{:S(2)}) collective-permute-start(bf16[128,768]{1,0:T(8,128)(2,1)} %get-tuple-element.187), channel_id=1, source_target_pairs={{0,1},{1,0},{2,3},{3,2},{4,5},{5,4},{6,7},{7,6},{8,9},{9,8},{10,11... | collective-permute-start | bytes 589832 | tf_op jit(solution)/shard_map/ppermute | solution.py:64
  645.8 26.9 %collective-permute-start.82 = (bf16[128,768]{1,0:T(8,128)(2,1)}, bf16[128,768]{1,0:T(8,128)(2,1)}, u32[]{:S(2)}, u32[]{:S(2)}) collective-permute-start(bf16[128,768]{1,0:T(8,128)(2,1)} %get-tuple-element.185), channel_id=1, source_target_pairs={{0,2},{1,3},{2,0},{3,1},{4,6},{5,7},{6,4},{7,5},{8,10},{9,11},{10,... | collective-permute-start | bytes 589832 | tf_op jit(solution)/shard_map/ppermute | solution.py:64
  660.8 31.2 %collective-permute-start.114 = (bf16[384,768]{0,1:T(8,128)(2,1)S(1)}, bf16[384,768]{0,1:T(8,128)(2,1)S(1)}, u32[]{:S(2)}, u32[]{:S(2)}) collective-permute-start(bf16[384,768]{0,1:T(8,128)(2,1)S(1)} %fusion.3), channel_id=1, source_target_pairs={{0,16},{16,0},{1,17},{17,1},{2,18},{18,2},{3,19},{19,3},{4,20},{20... | collective-permute-start | bytes 1769480 | tf_op jit(solution)/shard_map/ppermute | solution.py:64
  671.9 22.2 %collective-permute-start.137 = (bf16[768,512]{1,0:T(8,128)(2,1)S(1)}, bf16[768,512]{1,0:T(8,128)(2,1)S(1)}, u32[]{:S(2)}, u32[]{:S(2)}) collective-permute-start(bf16[768,512]{1,0:T(8,128)(2,1)S(1)} %constant_dynamic-slice_fusion.1), channel_id=1, source_target_pairs={{0,16},{16,0},{1,17},{17,1},{2,18},{18,2},{3,19},{19,3},{4,20},{20... | collective-permute-start | bytes 2359304 | tf_op jit(solution)/shard_map/ppermute | solution.py:64
  691.2 20.6 %collective-permute-start.85 = (bf16[256,768]{1,0:T(8,128)(2,1)S(1)}, bf16[256,768]{1,0:T(8,128)(2,1)S(1)}, u32[]{:S(2)}, u32[]{:S(2)}) collective-permute-start(bf16[256,768]{1,0:T(8,128)(2,1)S(1)} %pad_maximum_fusion.20), channel_id=1, source_target_pairs={{0,2},{1,3},{2,0},{3,1},{4,6},{5,7},{6,4},{7,5},{8,10},{9,11},{10,... | collective-permute-start | bytes 1179656 | tf_op jit(solution)/shard_map/ppermute | solution.py:64
  692.2 15.9 %collective-permute-start.115 = (bf16[384,768]{0,1:T(8,128)(2,1)S(1)}, bf16[384,768]{0,1:T(8,128)(2,1)S(1)}, u32[]{:S(2)}, u32[]{:S(2)}) collective-permute-start(bf16[384,768]{0,1:T(8,128)(2,1)S(1)} %add_convert_fusion.18), channel_id=1, source_target_pairs={{0,4},{12,8},{1,5},{13,9},{2,6},{14,10},{3,7},{15,11},{16,20},{28,... | collective-permute-start | bytes 1769480 | tf_op jit(solution)/shard_map/ppermute | solution.py:643
  694.1 20.1 %collective-permute-start.83 = (bf16[256,768]{1,0:T(8,128)(2,1)S(1)}, bf16[256,768]{1,0:T(8,128)(2,1)S(1)}, u32[]{:S(2)}, u32[]{:S(2)}) collective-permute-start(bf16[256,768]{1,0:T(8,128)(2,1)S(1)} %pad_maximum_fusion.19), channel_id=1, source_target_pairs={{0,1},{1,0},{2,3},{3,2},{4,5},{5,4},{6,7},{7,6},{8,9},{9,8},{10,11... | collective-permute-start | bytes 1179656 | tf_op jit(solution)/shard_map/ppermute | solution.py:64
  695.2 29.8 %collective-permute-start.138 = (bf16[768,512]{1,0:T(8,128)(2,1)S(1)}, bf16[768,512]{1,0:T(8,128)(2,1)S(1)}, u32[]{:S(2)}, u32[]{:S(2)}) collective-permute-start(bf16[768,512]{1,0:T(8,128)(2,1)S(1)} %add_convert_fusion.12), channel_id=1, source_target_pairs={{0,4},{12,8},{1,5},{13,9},{2,6},{14,10},{3,7},{15,11},{16,20},{28,... | collective-permute-start | bytes 2359304 | tf_op jit(solution)/shard_map/ppermute | solution.py:643
  708.1 46.6 %collective-permute-start.130 = (bf16[768,768]{1,0:T(8,128)(2,1)S(1)}, bf16[768,768]{1,0:T(8,128)(2,1)S(1)}, u32[]{:S(2)}, u32[]{:S(2)}) collective-permute-start(bf16[768,768]{1,0:T(8,128)(2,1)S(1)} %add_convert_fusion.5), channel_id=1, source_target_pairs={{4,8},{8,4},{5,9},{9,5},{6,10},{10,6},{7,11},{11,7},{20,24},{24,20... | collective-permute-start | bytes 3538952 | tf_op jit(solution)/shard_map/ppermute | solution.py:644
  711.8 73.8 %collective-permute-start.135 = (bf16[768,768]{1,0:T(8,128)(2,1)S(1)}, bf16[768,768]{1,0:T(8,128)(2,1)}, u32[]{:S(2)}, u32[]{:S(2)}) collective-permute-start(bf16[768,768]{1,0:T(8,128)(2,1)S(1)} %copy-done.124), channel_id=1, source_target_pairs={{4,0},{8,12},{5,1},{9,13},{6,2},{10,14},{7,3},{11,15},{20,16},{24,... | collective-permute-start | bytes 3538952 | tf_op jit(solution)/shard_map/ppermute | solution.py:645
  714.2 33.2 %collective-permute-start.116 = (bf16[384,768]{0,1:T(8,128)(2,1)S(1)}, bf16[384,768]{0,1:T(8,128)(2,1)S(1)}, u32[]{:S(2)}, u32[]{:S(2)}) collective-permute-start(bf16[384,768]{0,1:T(8,128)(2,1)S(1)} %add_convert_fusion.17), channel_id=1, source_target_pairs={{4,8},{8,4},{5,9},{9,5},{6,10},{10,6},{7,11},{11,7},{20,24},{24,20... | collective-permute-start | bytes 1769480 | tf_op jit(solution)/shard_map/ppermute | solution.py:644
  725.2 39.1 %collective-permute-start.139 = (bf16[768,512]{1,0:T(8,128)(2,1)S(1)}, bf16[768,512]{1,0:T(8,128)(2,1)S(1)}, u32[]{:S(2)}, u32[]{:S(2)}) collective-permute-start(bf16[768,512]{1,0:T(8,128)(2,1)S(1)} %add_convert_fusion.11), channel_id=1, source_target_pairs={{4,8},{8,4},{5,9},{9,5},{6,10},{10,6},{7,11},{11,7},{20,24},{24,20... | collective-permute-start | bytes 2359304 | tf_op jit(solution)/shard_map/ppermute | solution.py:644
  747.4 28.6 %collective-permute-start.86 = (f32[256,768]{1,0:T(8,128)S(1)}, f32[256,768]{1,0:T(8,128)S(1)}, u32[]{:S(2)}, u32[]{:S(2)}) collective-permute-start(f32[256,768]{1,0:T(8,128)S(1)} %broadcast_select_fusion.25), channel_id=1, source_target_pairs={{0,16},{16,0},{1,17},{17,1},{2,18},{18,2},{3,19},{19,3},{4,20},{20... | collective-permute-start | bytes 2359304 | tf_op jit(solution)/shard_map/ppermute | solution.py:64
  754.7 15.2 %collective-permute-start.117 = (bf16[384,768]{0,1:T(8,128)(2,1)S(1)}, bf16[384,768]{0,1:T(8,128)(2,1)S(1)}, u32[]{:S(2)}, u32[]{:S(2)}) collective-permute-start(bf16[384,768]{0,1:T(8,128)(2,1)S(1)} %add_convert_fusion.16), channel_id=1, source_target_pairs={{4,0},{8,12},{5,1},{9,13},{6,2},{10,14},{7,3},{11,15},{20,16},{24,... | collective-permute-start | bytes 1769480 | tf_op jit(solution)/shard_map/ppermute | solution.py:645
  764.3 20.8 %collective-permute-start.144 = (bf16[768,512]{1,0:T(8,128)(2,1)S(1)}, bf16[768,512]{1,0:T(8,128)(2,1)}, u32[]{:S(2)}, u32[]{:S(2)}) collective-permute-start(bf16[768,512]{1,0:T(8,128)(2,1)S(1)} %add_convert_fusion.7), channel_id=1, source_target_pairs={{4,0},{8,12},{5,1},{9,13},{6,2},{10,14},{7,3},{11,15},{20,16},{24,... | collective-permute-start | bytes 2359304 | tf_op jit(solution)/shard_map/ppermute | solution.py:645
  767.6 72.0 %collective-permute-start.131 = (bf16[768,768]{1,0:T(8,128)(2,1)S(1)}, bf16[768,768]{1,0:T(8,128)(2,1)}, u32[]{:S(2)}, u32[]{:S(2)}) collective-permute-start(bf16[768,768]{1,0:T(8,128)(2,1)S(1)} %add_convert_fusion.4), channel_id=1, source_target_pairs={{4,0},{8,12},{5,1},{9,13},{6,2},{10,14},{7,3},{11,15},{20,16},{24,... | collective-permute-start | bytes 3538952 | tf_op jit(solution)/shard_map/ppermute | solution.py:645
  769.9 65.9 %collective-permute-start.140 = (bf16[768,512]{1,0:T(8,128)(2,1)}, bf16[768,512]{1,0:T(8,128)(2,1)}, u32[]{:S(2)}, u32[]{:S(2)}) collective-permute-start(bf16[768,512]{1,0:T(8,128)(2,1)} %add_convert_fusion.10), channel_id=1, source_target_pairs={{4,0},{8,12},{5,1},{9,13},{6,2},{10,14},{7,3},{11,15},{20,16},{24,... | collective-permute-start | bytes 2359304 | tf_op jit(solution)/shard_map/ppermute | solution.py:645
  785.1 61.3 %collective-permute-start.91 = (bf16[256,768]{1,0:T(8,128)(2,1)S(1)}, bf16[256,768]{1,0:T(8,128)(2,1)S(1)}, u32[]{:S(2)}, u32[]{:S(2)}) collective-permute-start(bf16[256,768]{1,0:T(8,128)(2,1)S(1)} %get-tuple-element.193.refs_0_), channel_id=1, source_target_pairs={{0,12},{4,8},{8,4},{12,0},{1,13},{5,9},{9,5},{13,1},{2,14},{6,10},... | collective-permute-start | bytes 1179656 | tf_op jit(solution)/shard_map/ppermute | solution.py:64
  785.6 58.4 %collective-permute-start.103 = (bf16[256,768]{1,0:T(8,128)(2,1)S(1)}, bf16[256,768]{1,0:T(8,128)(2,1)S(1)}, u32[]{:S(2)}, u32[]{:S(2)}) collective-permute-start(bf16[256,768]{1,0:T(8,128)(2,1)S(1)} %get-tuple-element.193.refs_0_), channel_id=1, source_target_pairs={{0,4},{4,0},{8,12},{12,8},{1,5},{5,1},{9,13},{13,9},{2,6},{6,2},{1... | collective-permute-start | bytes 1179656 | tf_op jit(solution)/shard_map/ppermute | solution.py:64
  788.9 56.0 %collective-permute-start.109 = (bf16[256,768]{1,0:T(8,128)(2,1)S(1)}, bf16[256,768]{1,0:T(8,128)(2,1)S(1)}, u32[]{:S(2)}, u32[]{:S(2)}) collective-permute-start(bf16[256,768]{1,0:T(8,128)(2,1)S(1)} %get-tuple-element.193.refs_0_), channel_id=1, source_target_pairs={{0,1},{1,0},{2,3},{3,2},{4,5},{5,4},{6,7},{7,6},{8,9},{9,8},{10,11... | collective-permute-start | bytes 1179656 | tf_op jit(solution)/shard_map/ppermute | solution.py:64
  839.5 19.2 %collective-permute-start.97 = (bf16[256,768]{1,0:T(8,128)(2,1)S(1)}, bf16[256,768]{1,0:T(8,128)(2,1)S(1)}, u32[]{:S(2)}, u32[]{:S(2)}) collective-permute-start(bf16[256,768]{1,0:T(8,128)(2,1)S(1)} %get-tuple-element.193.refs_0_), channel_id=1, source_target_pairs={{0,8},{4,12},{8,0},{12,4},{1,9},{5,13},{9,1},{13,5},{2,10},{6,14},... | collective-permute-start | bytes 1179656 | tf_op jit(solution)/shard_map/ppermute | solution.py:64
  844.0 16.3 %collective-permute-start.104 = (bf16[256,768]{1,0:T(8,128)(2,1)S(1)}, bf16[256,768]{1,0:T(8,128)(2,1)S(1)}, u32[]{:S(2)}, u32[]{:S(2)}) collective-permute-start(bf16[256,768]{1,0:T(8,128)(2,1)S(1)} %collective-permute-done.103.refs_0_), channel_id=1, source_target_pairs={{0,1},{1,0},{2,3},{3,2},{4,5},{5,4},{6,7},{7,6},{8,9},{9,8},{10,11... | collective-permute-start | bytes 1179656 | tf_op jit(solution)/shard_map/ppermute | solution.py:64
  844.9 16.1 %collective-permute-start.105 = (bf16[256,768]{1,0:T(8,128)(2,1)S(1)}, bf16[256,768]{1,0:T(8,128)(2,1)S(1)}, u32[]{:S(2)}, u32[]{:S(2)}) collective-permute-start(bf16[256,768]{1,0:T(8,128)(2,1)S(1)} %collective-permute-done.103.refs_0_), channel_id=1, source_target_pairs={{0,2},{1,3},{2,0},{3,1},{4,6},{5,7},{6,4},{7,5},{8,10},{9,11},{10,... | collective-permute-start | bytes 1179656 | tf_op jit(solution)/shard_map/ppermute | solution.py:64
  847.3 19.2 %collective-permute-start.92 = (bf16[256,768]{1,0:T(8,128)(2,1)S(1)}, bf16[256,768]{1,0:T(8,128)(2,1)S(1)}, u32[]{:S(2)}, u32[]{:S(2)}) collective-permute-start(bf16[256,768]{1,0:T(8,128)(2,1)S(1)} %collective-permute-done.91.refs_0_), channel_id=1, source_target_pairs={{0,1},{1,0},{2,3},{3,2},{4,5},{5,4},{6,7},{7,6},{8,9},{9,8},{10,11... | collective-permute-start | bytes 1179656 | tf_op jit(solution)/shard_map/ppermute | solution.py:64
  860.4 17.4 %collective-permute-start.98 = (bf16[256,768]{1,0:T(8,128)(2,1)S(1)}, bf16[256,768]{1,0:T(8,128)(2,1)S(1)}, u32[]{:S(2)}, u32[]{:S(2)}) collective-permute-start(bf16[256,768]{1,0:T(8,128)(2,1)S(1)} %collective-permute-done.97.refs_0_), channel_id=1, source_target_pairs={{0,1},{1,0},{2,3},{3,2},{4,5},{5,4},{6,7},{7,6},{8,9},{9,8},{10,11... | collective-permute-start | bytes 1179656 | tf_op jit(solution)/shard_map/ppermute | solution.py:64
  861.0 17.8 %collective-permute-start.99 = (bf16[256,768]{1,0:T(8,128)(2,1)S(1)}, bf16[256,768]{1,0:T(8,128)(2,1)S(1)}, u32[]{:S(2)}, u32[]{:S(2)}) collective-permute-start(bf16[256,768]{1,0:T(8,128)(2,1)S(1)} %collective-permute-done.97.refs_0_), channel_id=1, source_target_pairs={{0,2},{1,3},{2,0},{3,1},{4,6},{5,7},{6,4},{7,5},{8,10},{9,11},{10,... | collective-permute-start | bytes 1179656 | tf_op jit(solution)/shard_map/ppermute | solution.py:64
  865.6 16.1 %collective-permute-start.106 = (bf16[128,768]{1,0:T(8,128)(2,1)S(1)}, bf16[128,768]{1,0:T(8,128)(2,1)S(1)}, u32[]{:S(2)}, u32[]{:S(2)}) collective-permute-start(bf16[128,768]{1,0:T(8,128)(2,1)S(1)} %slice.566), channel_id=1, source_target_pairs={{0,2},{1,3},{2,0},{3,1},{4,6},{5,7},{6,4},{7,5},{8,10},{9,11},{10,... | collective-permute-start | bytes 589832 | tf_op jit(solution)/shard_map/ppermute | solution.py:64
  866.5 16.3 %collective-permute-start.107 = (bf16[128,768]{1,0:T(8,128)(2,1)S(1)}, bf16[128,768]{1,0:T(8,128)(2,1)S(1)}, u32[]{:S(2)}, u32[]{:S(2)}) collective-permute-start(bf16[128,768]{1,0:T(8,128)(2,1)S(1)} %slice.567), channel_id=1, source_target_pairs={{0,1},{1,0},{2,3},{3,2},{4,5},{5,4},{6,7},{7,6},{8,9},{9,8},{10,11... | collective-permute-start | bytes 589832 | tf_op jit(solution)/shard_map/ppermute | solution.py:64
  872.9 30.8 %collective-permute-start.145 = (bf16[768,512]{1,0:T(8,128)(2,1)S(1)}, bf16[768,512]{1,0:T(8,128)(2,1)S(1)}, u32[]{:S(2)}, u32[]{:S(2)}) collective-permute-start(bf16[768,512]{1,0:T(8,128)(2,1)S(1)} %broadcast_select_fusion.19), channel_id=1, source_target_pairs={{0,16},{16,0},{1,17},{17,1},{2,18},{18,2},{3,19},{19,3},{4,20},{20... | collective-permute-start | bytes 2359304 | tf_op jit(solution)/shard_map/ppermute | solution.py:64
  877.8 31.6 %collective-permute-start.136 = (bf16[768,768]{1,0:T(8,128)(2,1)S(1)}, bf16[768,768]{1,0:T(8,128)(2,1)S(1)}, u32[]{:S(2)}, u32[]{:S(2)}) collective-permute-start(bf16[768,768]{1,0:T(8,128)(2,1)S(1)} %broadcast_select_fusion.8), channel_id=1, source_target_pairs={{0,16},{16,0},{1,17},{17,1},{2,18},{18,2},{3,19},{19,3},{4,20},{20... | collective-permute-start | bytes 3538952 | tf_op jit(solution)/shard_map/ppermute | solution.py:64
  878.8 17.2 %collective-permute-start.94 = (bf16[128,768]{1,0:T(8,128)(2,1)S(1)}, bf16[128,768]{1,0:T(8,128)(2,1)S(1)}, u32[]{:S(2)}, u32[]{:S(2)}) collective-permute-start(bf16[128,768]{1,0:T(8,128)(2,1)S(1)} %slice.562), channel_id=1, source_target_pairs={{0,2},{1,3},{2,0},{3,1},{4,6},{5,7},{6,4},{7,5},{8,10},{9,11},{10,... | collective-permute-start | bytes 589832 | tf_op jit(solution)/shard_map/ppermute | solution.py:64
  (256 other events, 2050.4 us)
Sparse Core Ops, SparseCore 0:
  478.8 143.3 reduce-scatter.1

commit v2 on v1

--- a/solution.py
+++ b/solution.py
@@ -16,8 +16,8 @@
 MIB = 1 << 20
 LANES = 128
 HEAD_DIM = 64
-VOCAB_STEP = 480
-BACK_STEP = 960
+VOCAB_STEP = 1536
+HEAD_CHUNK = 256
 
 
 def nn(left, right):
@@ -334,12 +334,13 @@
     spread_ref[...] = jnp.transpose(jnp.broadcast_to(spread, (spread.shape[0], LANES)))[0:8, :]
 
 
-def head_forward(*refs):
-    pieces, refs = refs[:5], refs[5:]
-    e_ref, own, near, far, corner, powers_ref, tops_ref, x_rel, grown, top_ref, total_ref = refs
+def head_forward(count, *refs):
+    pieces, refs = refs[:count], refs[count:]
+    e_ref, *outs = refs[:-4]
+    x_rel, grown, top_ref, total_ref = refs[-4:]
     step = pl.program_id(0)
-    rows = own.shape[0]
-    width = x_rel.shape[1]
+    tokens, width = x_rel.shape
+    chunks = [slice(at, at + HEAD_CHUNK) for at in range(0, tokens, HEAD_CHUNK)]
 
     @pl.when(step == 0)
     def begin():
@@ -348,72 +349,62 @@
         top_ref[...] = jnp.full_like(top_ref, -1e30)
         total_ref[...] = jnp.zeros_like(total_ref)
 
-    for r in range(4):
-        at = slice(r * rows, (r + 1) * rows)
-        logits = nt(e_ref[...], x_rel[at, :])
-        old = top_ref[:, at]
-        top = jnp.maximum(old, jnp.max(logits, axis=0, keepdims=True))
+    logits = [nt(x_rel[at, :], e_ref[...]) for at in chunks]
+    shares = []
+    for at, block in zip(chunks, logits):
+        old = top_ref[at, :]
+        top = jnp.maximum(old, jnp.max(block, axis=1, keepdims=True))
         fade = jnp.exp(old - top)
-        powers = jnp.exp(logits - top)
-        total_ref[:, at] = total_ref[:, at] * fade + jnp.sum(powers, axis=0, keepdims=True)
-        top_ref[:, at] = top
-        low = powers.astype(BF)
-        powers_ref[:, at] = low
-        grown[0:width, at] = grown[0:width, at] * fade + tn(e_ref[...], low)
-    tops_ref[0] = top_ref[...]
+        powers = jnp.exp(block - top)
+        total_ref[at, :] = total_ref[at, :] * fade + jnp.sum(powers, axis=1, keepdims=True)
+        top_ref[at, :] = top
+        shares.append((fade, powers.astype(BF)))
+    for at, (fade, powers) in zip(chunks, shares):
+        grown[at, :] = grown[at, :] * fade + nn(powers, e_ref[...])
 
     @pl.when(step == pl.num_programs(0) - 1)
     def end():
-        total = total_ref[...]
-        spread = top_ref[...] + jnp.log(total)
-        first = spread.astype(BF).astype(F32)
-        second = (spread - first).astype(BF).astype(F32)
-        third = spread - first - second
-        tail = [first, second, third, jnp.zeros((LANES - 3, total.shape[1]), F32)]
-        grown[width : width + LANES, :] = jnp.concatenate(tail, axis=0)
-        share = 1.0 / total
-        for r, target in enumerate((own, near, far, corner)):
-            at = slice(r * rows, (r + 1) * rows)
-            target[:, 0:width] = jnp.transpose(grown[0:width, at] * share[:, at]).astype(target.dtype)
-            target[:, width : width + LANES] = jnp.transpose(grown[width : width + LANES, at]).astype(target.dtype)
-
-
-def head_backward(first_ref, *refs):
-    pieces, refs = refs[:5], refs[5:]
-    spread_refs, refs = refs[:4], refs[4:]
-    powers_ref, tops_ref, hit_ref, out, x_rel, spread = refs
-    step = pl.program_id(0)
-
-    @pl.when(step == 0)
-    def begin():
-        copy_pieces(pieces, x_rel)
-        for r, ref in enumerate(spread_refs):
-            rows = ref.shape[1]
-            spread[:, r * rows : (r + 1) * rows] = ref[0:1, :]
-
-    count = tops_ref.shape[0]
-    rows = powers_ref.shape[0] // count
-    for i in range(count):
-        at = slice(i * rows, (i + 1) * rows)
-        scale = LOSS_SCALE * jnp.exp(tops_ref[i] - spread[...])
-        index = lax.broadcasted_iota(jnp.int32, (rows, 1), 0) + ((step + first_ref[0]) * count + i) * rows
-        hit = jnp.where(index == hit_ref[...], LOSS_SCALE, 0.0)
-        grads = powers_ref[at, :].astype(F32) * scale - hit
-        out[at, :] = nn(grads.astype(BF), x_rel[...]).astype(BF)
-
-
-def embed_backward(first_ref, *refs):
-    pieces, refs = refs[:5], refs[5:]
-    id_ref, so_far, out = refs
-    vocab = out.shape[0]
+        first_row = 0
+        for out in outs:
+            rows = out.shape[0]
+            at = slice(first_row, first_row + rows)
+            first_row += rows
+            total = total_ref[at, :]
+            out[:, 0:width] = (grown[at, :] * (1.0 / total)).astype(out.dtype)
+            spread = top_ref[at, :] + jnp.log(total)
+            first = spread.astype(BF).astype(F32)
+            second = (spread - first).astype(BF).astype(F32)
+            third = spread - first - second
+            lane = lax.broadcasted_iota(jnp.int32, (rows, LANES), 1)
+            tail = jnp.where(lane == 0, first, jnp.where(lane == 1, second, jnp.where(lane == 2, third, 0.0)))
+            out[:, width : width + LANES] = tail.astype(out.dtype)
+
+
+def vocab_backward(first_ref, *refs):
+    *pieces, spread_ref, id_ref, e_ref, so_far, out = refs
     total = so_far[...]
-    index = lax.broadcasted_iota(jnp.int32, (vocab, 1), 0) + first_ref[pl.program_id(0)]
+    index = lax.broadcasted_iota(jnp.int32, (out.shape[0], 1), 0) + first_ref[pl.program_id(0)]
     at = 0
     for piece in pieces:
-        ids = id_ref[:, at : at + piece.shape[0]]
-        total = total + nn(jnp.where(index == ids, 1.0, 0.0).astype(BF), piece[...])
+        columns = slice(at, at + piece.shape[0])
+        rows = piece[...]
+        probs = jnp.exp(nt(e_ref[...], rows) - spread_ref[:, columns])
+        hits = jnp.where(index == id_ref[:, columns], 1.0, 0.0)
+        total = total + nn((LOSS_SCALE * (probs - hits)).astype(BF), rows)
         at += piece.shape[0]
     out[...] = total
+
+
+def embed_backward(first_ref, *refs):
+    *pieces, id_ref, so_far, out = refs
+    total = jnp.zeros(out.shape, F32)
+    index = lax.broadcasted_iota(jnp.int32, (out.shape[0], 1), 0) + first_ref[pl.program_id(0)]
+    at = 0
+    for piece in pieces:
+        hits = jnp.where(index == id_ref[:, at : at + piece.shape[0]], 1.0, 0.0)
+        total = total + nn(hits.astype(BF), piece[...])
+        at += piece.shape[0]
+    out[...] = so_far[...] + total * piece.shape[1] ** 0.5
 
 
 def layer_forward(x, x_low, lens, me, weights):
@@ -460,7 +451,7 @@
     return out, out_low, (x_rel, proj, ctx_rel, h_rel, act, slope, normed_one, scale_one, normed_two, scale_two)
 
 
-def layer_backward(d_two, d_two_low, lens, me, weights, saved, section, head_width):
+def layer_backward(d_two, pieces, lens, me, weights, saved, section, head_width, fill):
     w_qkv, b_qkv, w_out, w_in, b_in, w_down, gains, shifts, gates = weights
     x_rel, proj, ctx_rel, h_rel, act, slope, normed_one, scale_one = saved[:8]
     rows, width = d_two.shape
@@ -472,15 +463,15 @@
         "feed_backward",
         outs,
         [],
-        gather_pieces(d_two_low) + [w_in, w_down, slope],
+        pieces + [w_in, w_down, slope],
         flops=4 * tokens * width * units,
     )
-    near, far = reduce_pieces(*parts[1:])
+    near, far = fill[0](reduce_pieces(*parts[1:]))
     d_w_down = tn(act, d_rel).astype(BF)
     d_w_in = tn(h_rel, d_pre).astype(BF)
     first = section == 0
     sent = swap(jnp.where(first, d_w_down, d_w_in), "section", 1)
-    d_feed = dp_sum(plus(jnp.where(first, d_w_in, d_w_down), sent))
+    d_feed = plus(jnp.where(first, d_w_in, d_w_down), sent)
     outs = [sds((rows, width), F32), sds((rows, width), F32), sds((rows, width), BF), sds((8, width), F32)]
     _, d_one, d_one_low, sums = kernel_call(
         norm_backward,
@@ -489,6 +480,8 @@
         [],
         [parts[0], near, far, d_two, normed_one, scale_one, gains[0:1]],
     )
+    pieces, d_feed = lax.optimization_barrier((gather_pieces(d_one_low), d_feed))
+    pieces = fill[1](pieces)
     outs = piece_outs(rows, width) + [
         sds((tokens, width), BF),
         sds((tokens, 3 * PART), BF),
@@ -500,7 +493,7 @@
         "attention_backward",
         outs,
         [lens, me],
-        gather_pieces(d_one_low) + [w_qkv, gates, w_out, proj],
+        pieces + [w_qkv, gates, w_out, proj],
         [
             pltpu.VMEM((tokens, PART), BF),
             pltpu.VMEM((tokens, PART), F32),
@@ -510,103 +503,62 @@
         flops=2 * tokens * width * 4 * PART,
         vmem=40,
     )
-    near, far = reduce_pieces(*parts[1:])
+    near, far = fill[2](reduce_pieces(*parts[1:]))
     d_w_qkv = tn(x_rel, dproj).astype(BF).reshape(width, 3, PART)[:, :, :head_width].reshape(width, 3 * head_width)
     d_w_out = tn(d_rel, ctx_rel).astype(BF)[:, :head_width]
-    d_attn = dp_sum(halves(jnp.concatenate([d_w_qkv, d_w_out], axis=1), section))
-    d_gate = dp_sum(halves(d_gate.astype(BF).reshape(-1, d_gate.shape[2]), section))
+    d_attn = halves(jnp.concatenate([d_w_qkv, d_w_out], axis=1), section)
+    d_gate = (halves(d_gate.astype(BF).reshape(-1, d_gate.shape[2]), section))
     return (parts[0], near, far, d_one), (d_feed, d_attn, d_gate), (d_b_qkv, d_b_in, sums)
 
 
-def head_step(pieces, embedding, target_hits):
-    rows, width = pieces[0].shape
-    tokens = 4 * rows
+def head_blocks(pieces, embedding, outs):
+    width = embedding.shape[1]
     vocab = embedding.shape[0]
-    steps = vocab // VOCAB_STEP
-    fixed = [pl.BlockSpec(p.shape, lambda i: (0, 0)) for p in pieces]
+    tokens = sum(p.shape[0] for p in pieces)
     wide = width + LANES
-    block = pl.BlockSpec((rows, wide), lambda i: (0, 0))
-    params = pltpu.CompilerParams(vmem_limit_bytes=48 * MIB)
-    own, near, far, corner, powers, tops = pl.pallas_call(
-        head_forward,
+    return pl.pallas_call(
+        functools.partial(head_forward, len(pieces)),
         name="head_forward",
-        grid=(steps,),
-        in_specs=fixed + [pl.BlockSpec((VOCAB_STEP, width), lambda i: (i, 0))],
-        out_specs=[block] * 4
-        + [
-            pl.BlockSpec((VOCAB_STEP, tokens), lambda i: (i, 0)),
-            pl.BlockSpec((1, 1, tokens), lambda i: (i, 0, 0)),
-        ],
-        out_shape=[sds((rows, wide), F32)]
-        + [sds((rows, wide), BF)] * 3
-        + [sds((vocab, tokens), BF), sds((steps, 1, tokens), F32)],
+        grid=(vocab // VOCAB_STEP,),
+        in_specs=[pl.BlockSpec(p.shape, lambda i: (0, 0)) for p in pieces]
+        + [pl.BlockSpec((VOCAB_STEP, width), lambda i: (i, 0))],
+        out_specs=[pl.BlockSpec((rows, wide), lambda i: (0, 0)) for rows, _ in outs],
+        out_shape=[sds((rows, wide), dtype) for rows, dtype in outs],
         scratch_shapes=[
             pltpu.VMEM((tokens, width), BF),
-            pltpu.VMEM((wide, tokens), F32),
-            pltpu.VMEM((1, tokens), F32),
-            pltpu.VMEM((1, tokens), F32),
+            pltpu.VMEM((tokens, width), F32),
+            pltpu.VMEM((tokens, 1), F32),
+            pltpu.VMEM((tokens, 1), F32),
         ],
-        compiler_params=params,
+        compiler_params=pltpu.CompilerParams(vmem_limit_bytes=44 * MIB),
         cost_estimate=pl.CostEstimate(
-            flops=4 * tokens * vocab * width, bytes_accessed=2 * vocab * (width + tokens), transcendentals=vocab * tokens
+            flops=4 * tokens * vocab * width, bytes_accessed=2 * vocab * width, transcendentals=vocab * tokens
         ),
     )(*pieces, embedding)
 
-    def finish(spreads, section):
-        half_steps = vocab // 2 // BACK_STEP
-        def part(which):
-            first = (which * half_steps)[None].astype(jnp.int32)
-            fixed_two = [pl.BlockSpec(p.shape, lambda i, f: (0, 0)) for p in pieces]
-            return pl.pallas_call(
-                head_backward,
-                name="head_backward",
-                grid_spec=pltpu.PrefetchScalarGridSpec(
-                    num_scalar_prefetch=1,
-                    grid=(half_steps,),
-                    in_specs=fixed_two
-                    + [pl.BlockSpec(s.shape, lambda i, f: (0, 0)) for s in spreads]
-                    + [
-                        pl.BlockSpec((BACK_STEP, tokens), lambda i, f: (i + f[0], 0)),
-                        pl.BlockSpec((BACK_STEP // VOCAB_STEP, 1, tokens), lambda i, f: (i + f[0], 0, 0)),
-                        pl.BlockSpec((1, tokens), lambda i, f: (0, 0)),
-                    ],
-                    out_specs=pl.BlockSpec((BACK_STEP, width), lambda i, f: (i, 0)),
-                    scratch_shapes=[pltpu.VMEM((tokens, width), BF), pltpu.VMEM((1, tokens), F32)],
-                ),
-                out_shape=sds((vocab // 2, width), BF),
-                compiler_params=params,
-                cost_estimate=pl.CostEstimate(
-                    flops=tokens * vocab * width, bytes_accessed=vocab * (width + tokens), transcendentals=0
-                ),
-            )(first, *pieces, *spreads, powers, tops, target_hits)
-
-        sent = part(1 - section)
-        kept = part(section)
-        return plus(kept, swap(sent, "section", 1))
-
-    return (own, near, far, corner), finish
-
-
-def embed_grad(pieces, ids, firsts, so_far):
+
+def owned_rows(kernel, name, pieces, columns, firsts, so_far, rows=None):
     count, width = so_far.shape
     steps = firsts.shape[0]
-    tokens = ids.shape[1]
+    tokens = columns[0].shape[1]
     part = pl.BlockSpec((count // steps, width), lambda i: (i, 0))
+    given = [] if rows is None else [rows]
     return pl.pallas_call(
-        embed_backward,
-        name="embed_backward",
+        kernel,
+        name=name,
         grid=(steps,),
         in_specs=scalar_specs(1)
         + [pl.BlockSpec(p.shape, lambda i: (0, 0)) for p in pieces]
-        + [pl.BlockSpec((1, tokens), lambda i: (0, 0)), part],
+        + [pl.BlockSpec((1, tokens), lambda i: (0, 0))] * len(columns)
+        + [part] * (len(given) + 1),
         out_specs=part,
         out_shape=sds((count, width), F32),
-        input_output_aliases={2 + len(pieces): 0},
-        compiler_params=pltpu.CompilerParams(vmem_limit_bytes=32 * MIB),
+        input_output_aliases={1 + len(pieces) + len(columns) + len(given): 0},
+        compiler_params=pltpu.CompilerParams(vmem_limit_bytes=44 * MIB),
         cost_estimate=pl.CostEstimate(
-            flops=2 * tokens * count * width, bytes_accessed=8 * count * width, transcendentals=0
+            flops=0, bytes_accessed=0, transcendentals=0
         ),
-    )(firsts, *pieces, ids, so_far)
+    )(firsts, *pieces, *columns, *given, so_far)
 
 
 def pad_parts(array, axis):
@@ -632,22 +584,18 @@
     return (mine.astype(F32) + swap(other, "section", 1).astype(F32)).astype(BF)
 
 
+def dp_sum(arrays, turn):
+    order = list(range(lax.axis_size("dp")))
+    order = order[turn:] + order[:turn]
+    return lax.psum(arrays, "dp", axis_index_groups=[order])
+
+
 def plus(left, right):
     return (left.astype(F32) + right.astype(F32)).astype(BF)
 
 
-def dp_sum(array):
-    if lax.axis_size("dp") != 4:
-        return lax.psum(array, "dp")
-    z = lax.axis_index("dp")
-    inward = plus(array, lax.ppermute(array, "dp", [(0, 1), (3, 2)]))
-    total = plus(inward, lax.ppermute(inward, "dp", [(1, 2), (2, 1)]))
-    outward = lax.ppermute(total, "dp", [(1, 0), (2, 3)])
-    return jnp.where((z == 1) | (z == 2), total, outward)
-
-
-def sum_everywhere(array):
-    for axis in ("tensor", "section", "dp"):
+def sum_over(array, axes):
+    for axis in axes:
         bit = 1
         while bit < lax.axis_size(axis):
             array = array + swap(array, axis, bit)
@@ -716,30 +664,76 @@
         row = lax.dynamic_index_in_dim(ids, section, 0, keepdims=False)
         return row.reshape(4, rows)[order].reshape(tokens) - vocab_start
 
-    target_local = mine(targets)
-    x = lookup_rows(mine(token_ids), embedding).astype(F32) * width**0.5
+    target_local, token_local = mine(targets), mine(token_ids)
+    x = lookup_rows(token_local, embedding).astype(F32) * width**0.5
     target_rows = lookup_rows(target_local, embedding)
     hidden, hidden_low, saved_first = layer_forward(x, x.astype(BF), lens, me, layers[0])
     final, final_low, saved_last = layer_forward(hidden, hidden_low, lens, me, layers[1])
 
+    dp = lax.axis_size("dp")
     pieces = gather_pieces(final_low)
-    parts, finish_head = head_step(pieces, embedding, target_local[None])
-    own, near, far, corner = parts
+    rows_of = [final_low] + [swap(final_low, "dp", other) for other in range(1, dp)]
+    (own,) = head_blocks(pieces[:1], embedding, [(rows, F32)])
+    own, *pieces[1:] = lax.optimization_barrier((own, *pieces[1:]))
+    near, far, corner = head_blocks(pieces[1:], embedding, [(rows, BF)] * 3)
+    there = [pieces] + [gather_pieces(r) for r in rows_of[1:]]
+    near, far, corner, there[1:2] = lax.optimization_barrier((near, far, corner, there[1:2]))
+    near, far, corner = swap(near, "tensor", 1), swap(far, "tensor", 2), swap(corner, "tensor", 3)
     outs = [sds((rows, width), F32), sds((rows, width), BF), sds((8, width), F32), sds((8, rows), F32)]
     d_two, d_two_low, sums_two_last, spread = kernel_call(
         merge_head,
         "merge_head",
         outs,
         [],
-        [own, swap(near, "tensor", 1), swap(far, "tensor", 2), swap(corner, "tensor", 3), target_rows]
-        + [saved_last[8], saved_last[9], layers[1][6][1:2]],
-    )
-    spreads = [spread] + [swap(spread, "tensor", bit) for bit in (1, 2, 3)]
-    d_head = finish_head(spreads, section)
+        [own, near, far, corner, target_rows, saved_last[8], saved_last[9], layers[1][6][1:2]],
+    )
+    d_pieces = gather_pieces(d_two_low)
+
     half_vocab = vocab_rows // 2
-    d_head = lax.psum_scatter(d_head, "dp", scatter_dimension=0, tiled=True)
-
-    d_x, grads_last, vecs_last = layer_backward(d_two, d_two_low, lens, me, layers[1], saved_last, section, head_width)
+    share = half_vocab // dp
+    steps = 2 if (share // 2) % 16 == 0 else 1
+    starts = [lax.axis_index("dp") * share + c * half_vocab for c in (section, 1 - section)]
+    firsts = [(start + jnp.arange(0, share, share // steps, dtype=jnp.int32)).astype(jnp.int32) for start in starts]
+    my_rows = [lax.dynamic_slice_in_dim(embedding, start, share, 0) for start in starts]
+    spread = jnp.concatenate([spread[0:1]] + [swap(spread, "tensor", bit)[0:1] for bit in (1, 2, 3)], axis=1)
+    d_rows = [jnp.zeros((share, width), F32)] * 2
+    id_pair = jnp.stack([token_local, target_local])
+    id_pairs = [id_pair] + [swap(id_pair, "dp", other) for other in range(1, dp)]
+    spreads = [spread] + [swap(spread, "dp", other) for other in range(1, dp)]
+
+    def dense_half(values, half):
+        total = d_rows[half]
+        for others in groups(4):
+            found = sum([there[other] for other in others], [])
+            columns = [jnp.concatenate([spreads[other] for other in others], axis=1)]
+            columns += [jnp.concatenate([id_pairs[other][1:2] for other in others], axis=1)]
+            total = owned_rows(vocab_backward, "vocab_backward", found, columns, firsts[half], total, my_rows[half])
+        values, d_rows[half] = lax.optimization_barrier((values, total))
+        return values
+
+    def groups(size):
+        return [range(at, min(at + size, dp)) for at in range(0, dp, size)]
+
+    sums = []
+
+    def early_sum(d_feed, turn):
+        sums.append(dp_sum(d_feed, turn))
+
+    def held(values, k):
+        values, sums[k] = lax.optimization_barrier((values, sums[k]))
+        return values
+
+    d_x, d_rest_last, vecs_last = layer_backward(
+        d_two,
+        d_pieces,
+        lens,
+        me,
+        layers[1],
+        saved_last,
+        section,
+        head_width,
+        [lambda v: v] * 3,
+    )
     outs = [sds((rows, width), F32), sds((rows, width), F32), sds((rows, width), BF), sds((8, width), F32)]
     grad_last, d_two, d_two_low, sums_two_first = kernel_call(
         norm_backward,
@@ -748,23 +742,19 @@
         [],
         list(d_x) + [saved_first[8], saved_first[9], layers[0][6][1:2]],
     )
-    d_x, grads_first, vecs_first = layer_backward(d_two, d_two_low, lens, me, layers[0], saved_first, section, head_width)
-    grad_first = d_x[3] + (d_x[0] + d_x[1].astype(F32) + d_x[2].astype(F32))
-
-    dp = lax.axis_size("dp")
-    share = half_vocab // dp
-    firsts = lax.axis_index("dp") * share + jnp.arange(2, dtype=jnp.int32) * half_vocab
-    rows_here, d_head = lax.optimization_barrier((grad_first.astype(BF), d_head))
-    ids_here = mine(token_ids)[None] + vocab_start
-    d_rows = jnp.zeros((2 * share, width), F32)
-    for other in range(dp):
-        ids = ids_here if other == 0 else swap(ids_here, "dp", other)
-        rows_there = rows_here if other == 0 else swap(rows_here, "dp", other)
-        d_rows = embed_grad(gather_pieces(rows_there), ids - vocab_start, firsts, d_rows)
-    kept = lax.dynamic_slice_in_dim(d_rows, section * share, share, 0)
-    sent = lax.dynamic_slice_in_dim(d_rows, (1 - section) * share, share, 0).astype(BF)
-    d_embedding = d_head.astype(F32) + width**0.5 * (kept + swap(sent, "section", 1).astype(F32))
-
+    d_pieces, d_rest_last, there[1:] = lax.optimization_barrier((gather_pieces(d_two_low), d_rest_last, there[1:]))
+    early_sum(d_rest_last, 0)
+    d_x, d_rest_first, vecs_first = layer_backward(
+        d_two,
+        d_pieces,
+        lens,
+        me,
+        layers[0],
+        saved_first,
+        section,
+        head_width,
+        [lambda v: v, lambda v: v, lambda v: held(dense_half(v, 1), 0)],
+    )
     def vec_rows(vecs, sums_two):
         d_b_qkv, d_b_in, sums_one = vecs
         wide = jnp.concatenate([sums_one[0:1], sums_two[0:1], sums_one[2:3], sums_one[1:2], sums_two[2:3], sums_two[1:2]])
@@ -775,14 +765,34 @@
         return jnp.concatenate([wide, spread_out])
 
     vecs = jnp.stack([vec_rows(vecs_first, sums_two_first), vec_rows(vecs_last, sums_two_last)])
-    vecs = sum_everywhere(vecs)
-    vecs = lax.dynamic_index_in_dim(vecs, section, 0, keepdims=False)
-    narrow = lax.dynamic_slice_in_dim(vecs, 6 + 3 * place, 3, 0)
+    vecs = sum_over(vecs, ("tensor", "section")).astype(BF).reshape(-1, width)
+    d_feed_first, d_attn, d_gate = d_rest_first
+    d_x, d_feed_first, d_attn, d_gate, vecs = lax.optimization_barrier((d_x, d_feed_first, d_attn, d_gate, vecs))
+    early_sum((d_feed_first, jnp.concatenate([d_attn, vecs]), d_gate), 1)
+    grad_first = d_x[3] + (d_x[0] + d_x[1].astype(F32) + d_x[2].astype(F32))
+
+    rows_here = grad_first.astype(BF)
+    arriving = [swap(rows_here, "dp", other) for other in range(1, dp)]
+    own_pieces, arriving = dense_half((gather_pieces(rows_here), arriving), 0)
+    found = [own_pieces] + [gather_pieces(r) for r in arriving]
+    for others in groups(3):
+        ids = jnp.concatenate([id_pairs[other][0:1] for other in others], axis=1)
+        pieces = sum([found[other] for other in others], [])
+        d_rows = [
+            owned_rows(embed_backward, "embed_backward", pieces, [ids], *part)
+            for part in reversed(list(zip(firsts, d_rows)))
+        ][::-1]
+    d_embedding = d_rows[0] + swap(d_rows[1].astype(BF), "section", 1).astype(F32)
 
     def assembled(low_layer, high_layer):
         got = swap(jnp.where(first, high_layer, low_layer), "section", 1)
         return jnp.where(first, low_layer, got).astype(F32), jnp.where(first, got, high_layer).astype(F32)
 
+    grads_last, (d_feed, d_attn, d_gate) = sums
+    grads_first = (d_feed, d_attn[: width // 2], d_gate)
+    vecs = d_attn[width // 2 :].reshape(2, -1, width)
+    vecs = lax.dynamic_index_in_dim(vecs, section, 0, keepdims=False).astype(F32)
+    narrow = lax.dynamic_slice_in_dim(vecs, 6 + 3 * place, 3, 0)
     (g_in, g_down), attn, gate = jax.tree.map(assembled, grads_first, grads_last)
     attn = jnp.concatenate(attn)
     g_qkv = attn[:, : 3 * head_width].reshape(width, 3, head_width)

time: 936 us -> 801 us (0.86)
  waiting for transfers between devices: 329 us -> 220 us
  starting transfers between devices: 211 us -> 163 us
  local copies, waits for them, and re-layouts: 93.2 us -> 117 us
    ppermute x18 -> x0, waiting for transfers between devices: 189 us -> none  [the longest x6 99.1 us: dp_sum(): total = plus(inward, lax.ppermute(inward, 'dp', [(1, 2), (2, 1)]))]
    ppermute x128 -> x143, waiting for transfers between devices: 140 us -> 204 us  [swap(): return lax.ppermute(array, axis, [(i, i ^ bit) for i in range(count)])]
    ppermute x18 -> x0, starting transfers between devices: 38.9 us -> none  [the longest x6 16.2 us: dp_sum(): total = plus(inward, lax.ppermute(inward, 'dp', [(1, 2), (2, 1)]))]
    convert_element_type x15 -> x2, other arithmetic: 21.7 us -> 4.74 us  [plus(): return (left.astype(F32) + right.astype(F32)).astype(BF)]
    psum x0 -> x2, waiting for transfers between devices: none -> 15 us  [dp_sum(): return lax.psum(arrays, 'dp', axis_index_groups=[order])]
    ppermute x128 -> x143, starting transfers between devices: 172 us -> 163 us  [swap(): return lax.ppermute(array, axis, [(i, i ^ bit) for i in range(count)])]
    pallas_call x7 -> x8, Pallas kernels: 95.5 us -> 99.5 us  [the longest x6 61.4 us: owned_rows(): pl.pallas_call(kernel, name=name, grid=(steps,), in_specs=scalar_specs(1)...]
    unnamed x350 -> x488, local copies, waits for them, and re-layouts: 37.4 us -> 39.8 us
  transfers between devices with their start and end apart: 147 -> 145, of which waited for: 57 -> 52; matrix products, arithmetic and copies ran while one was open for 16% -> 20% of each run, Pallas kernels for 16% -> 19%
where the time goes in v2:
time: 801 us; the launch traced here: 792 us
  waiting for transfers between devices  220 us (27%)
  Pallas kernels  186 us (23%)
  starting transfers between devices  163 us (20%)
  local copies, waits for them, and re-layouts  117 us (15%)
  other arithmetic  78.2 us (10%)
  between operations  17.3 us (2%)
  matrix products  11.6 us (1%)
    ppermute x143, waiting for transfers between devices, swap(): return lax.ppermute(array, axis, [(i, i ^ bit) for i in range(count)])  204 us
    ppermute x143, starting transfers between devices, swap(): return lax.ppermute(array, axis, [(i, i ^ bit) for i in range(count)])  163 us
    pallas_call x16, Pallas kernels, kernel_call(): pl.pallas_call(kernel, name=name, out_shape=outs, in_specs=scalar_specs(l...  86.2 us
    pallas_call x6, Pallas kernels, owned_rows(): pl.pallas_call(kernel, name=name, grid=(steps,), in_specs=scalar_specs(1)...  61.4 us
    unnamed x488, local copies, waits for them, and re-layouts  39.8 us
    pallas_call x2, Pallas kernels, head_blocks(): pl.pallas_call(functools.partial(head_forward, len(pieces)), name='head_f...  38.1 us
    gather x2, local copies, waits for them, and re-layouts, lookup_rows(): embedding[jnp.clip(ids, 0, rows - 1)]  22.2 us
  transfers between devices with their start and end apart: 145, of which 52 were waited for; matrix products, arithmetic and copies ran while one was open for 20% of the time, Pallas kernels for 19%

profile of v2, /device:TPU:17, one launch (start us, length us, event | category | flops | bytes accessed | tf_op | source)
XLA Modules:
  0.0 792.1 jit_solution(1467843603974583457)
XLA Ops:
  7.3 5.4 add_divide_fusion
  16.4 10.3 %gather_fusion.1 = bf16[1024,768]{1,0:T(8,128)(2,1)S(1)} fusion(bf16[7680,768]{1,0:T(8,128)(2,1)} %refs_4_.1, s32[1024]{0:T(1024)S(1)} %broadcast_clamp_fusion.1), kind=kCustom, calls=%fused_computation.1 | custom fusion | bytes 3149824 | tf_op jit(solution)/shard_map/gather | solution.py:573
  31.0 2.8 collective-permute-done
  39.6 5.7 collective-permute-done.3
  59.5 5.7 broadcast_select_fusion.2
  65.2 12.2 %attention_forward.2 = (f32[256,768]{1,0:T(8,128)S(1)}, bf16[256,768]{1,0:T(8,128)(2,1)S(1)}, bf16[256,768]{1,0:T(8,128)(2,1)S(1)}, bf16[128,768]{1,0:T(8,128)(2...) custom-call(s32[4]{0:T(128)S(1)} %fusion.14.len_ref, ...), custom_call_target="tpu_custom_call" | custom-call | flops 1610612736 | bytes 11930624 | tf_op jit(solution)/shard_map/attention_forward/pallas_call | solution.py:50
  79.9 3.2 collective-permute-start.20
  84.9 4.4 collective-permute-done.14
  90.8 6.9 collective-permute-done.13.near
  101.2 4.8 collective-permute-done.16.refs_1_
  108.8 2.9 collective-permute-done.18.refs_3_
  111.8 3.3 feed_forward.2
  119.0 3.0 collective-permute-done.22
  123.7 6.4 collective-permute-done.23.near
  136.4 6.2 collective-permute-done.26.refs_1_
  148.9 2.7 copy.51.refs_5_
  159.4 13.0 %attention_forward.3 = (f32[256,768]{1,0:T(8,128)S(1)}, bf16[256,768]{1,0:T(8,128)(2,1)S(1)}, bf16[256,768]{1,0:T(8,128)(2,1)S(1)}, bf16[128,768]{1,0:T(8,128)(2...) custom-call(s32[4]{0:T(128)S(1)} %fusion.14.len_ref, ...), custom_call_target="tpu_custom_call" | custom-call | flops 1610612736 | bytes 11930624 | tf_op jit(solution)/shard_map/attention_forward/pallas_call | solution.py:50
  174.8 2.9 collective-permute-done.30
  180.5 3.9 collective-permute-done.31.near
  190.4 11.8 %gather_fusion.3 = bf16[1024,768]{1,0:T(8,128)(2,1)} fusion(bf16[7680,768]{1,0:T(8,128)(2,1)} %refs_4_.1, s32[1024]{0:T(1024)} %broadcast_clamp_fusion), kind=kCustom, calls=%fused_computation.3 | custom fusion | bytes 3149824 | tf_op jit(solution)/shard_map/gather | solution.py:573
  209.5 4.7 collective-permute-done.37.refs_4_
  214.2 4.7 feed_forward.3
  223.6 5.0 collective-permute-done.38
  252.8 13.3 %head_forward.2.own = f32[256,896]{1,0:T(8,128)S(1)} custom-call(bf16[256,768]{1,0:T(8,128)(2,1)S(1)} %get-tuple-element.211.refs_0_, bf16[7680,768]{1,0:T(8,128)(2,1)} %refs_4_.1), custom_call_target="tpu_custom_call" | custom-call | flops 6039797760 | bytes 11796480 | tf_op jit(solution)/shard_map/head_forward/pallas_call | solution.py:519
  270.1 24.9 %head_forward.3 = (bf16[256,896]{1,0:T(8,128)(2,1)}, bf16[256,896]{1,0:T(8,128)(2,1)}, bf16[256,896]{1,0:T(8,128)(2,1)}) custom-call(bf16[256,768]{1,0:T(8,128)(2,1)S(1)} %collective-permute-done.43.refs_0_.refs_1_, bf16[256,768]{1,0:T(8,128)(2,1)S(1)} %collective-permute-done.44.refs_1_.refs_2_, ...), custom_call_target="tpu_custom_call" | custom-call | flops 18119393280 | bytes 11796480 | tf_op jit(solution)/shard_map/head_forward/pallas_call | solution.py:519
  300.3 3.4 constant_dynamic-slice_fusion
  304.0 3.2 collective-permute-start.112
  320.7 6.4 collective-permute-done.82.refs_10_
  328.5 6.3 collective-permute-done.87.refs_15_
  336.3 2.9 feed_backward.2
  345.7 5.0 collective-permute-done.65
  350.6 27.8 %collective-permute-start.71 = (bf16[768,768]{1,0:T(8,128)(2,1)S(1)}, bf16[768,768]{1,0:T(8,128)(2,1)S(1)}, u32[]{:S(2)}, u32[]{:S(2)}) collective-permute-start(bf16[768,768]{1,0:T(8,128)(2,1)S(1)} %get-tuple-element.452), channel_id=1, source_target_pairs={{0,16},{16,0},{1,17},{17,1},{2,18},{18,2},{3,19},{19,3},{4,20},{20... | collective-permute-start | bytes 3538952 | tf_op jit(solution)/shard_map/ppermute | solution.py:64
  385.0 4.4 collective-permute-done.64.near
  393.2 7.3 collective-permute-done.67.refs_1_
  406.1 18.7 %attention_backward.2 = (f32[256,768]{1,0:T(8,128)S(1)}, bf16[256,768]{1,0:T(8,128)(2,1)S(1)}, bf16[256,768]{1,0:T(8,128)(2,1)S(1)}, bf16[128,768]{1,0:T(8,128)(...) custom-call(s32[4]{0:T(128)S(1)} %copy-done.160, ...), custom_call_target="tpu_custom_call" | custom-call | flops 1610612736 | bytes 16124928 | tf_op jit(solution)/shard_map/attention_backward/pallas_call | solution.py:50
  431.5 6.7 collective-permute-start.80
  445.6 2.8 collective-permute-done.76.refs_1_
  450.2 4.8 collective-permute-done.77.refs_2_
  471.2 3.9 feed_backward.3
  478.2 3.0 broadcast_select_fusion.7
  481.3 6.1 collective-permute-start.100
  490.4 7.9 collective-permute-done.93.near
  503.3 6.9 collective-permute-done.96.refs_1_
  513.8 3.2 add_convert_fusion
  518.7 19.4 %attention_backward.3 = (f32[256,768]{1,0:T(8,128)S(1)}, bf16[256,768]{1,0:T(8,128)(2,1)S(1)}, bf16[256,768]{1,0:T(8,128)(2,1)S(1)}, bf16[128,768]{1,0:T(8,128)(...) custom-call(s32[4]{0:T(128)S(1)} %copy-done.160, ...), custom_call_target="tpu_custom_call" | custom-call | flops 1610612736 | bytes 16124928 | tf_op jit(solution)/shard_map/attention_backward/pallas_call | solution.py:50
  543.8 3.7 collective-permute-start.114
  554.1 3.2 collective-permute-done.116
  567.7 19.7 %vocab_backward.2.refs_16_ = f32[960,768]{1,0:T(8,128)} custom-call(s32[2]{0:T(128)S(1)} %copy-done.161, bf16[256,768]{1,0:T(8,128)(2,1)S(1)} %copy-done.64, bf16[256,768]{1,0:T(8,128)(2,1)S(1)} %collective-permute-done.43.refs_0_.refs_1_, bf16[256,768]{1,0:T(8,128)(2,1)S(1)} %collective-permute-done.44.refs_1_.refs_2_, ...), custom_call_target="tpu_custom_call", output_to_operand_aliasing={{}: (24, {})} | custom-call | tf_op jit(solution)/shard_map/vocab_backward/pallas_call | solution.py:546
  591.5 15.0 %all-reduce.12.cloned.1.call-done = (bf16[768,768]{1,0:T(8,128)(2,1)}, bf16[384,768]{0,1:T(8,128)(2,1)}, bf16[768,512]{1,0:T(8,128)(2,1)}) async-done(((bf16[768,768]{1,0:T(8,128)(2,1)}, bf16[384,768]{0,1:T(8,128)(2,1)}, bf16[768,512]{1,0:T(8,128)(2,1)}), (bf16[768,768]{1,0:T(8,128)(2,1)}, bf16[384,768]{0,1:T(8,128)(2,1)}, bf16[768,512]{1,0:T(8,128)(2,1)})) %all-reduce.12.cloned.1.call-update) | async-done | bytes 2555920 | tf_op jit(solution)/shard_map/psum | solution.py:590
  614.8 5.1 collective-permute-done.120.refs_1_
  625.2 19.8 %vocab_backward.3.refs_16_ = f32[960,768]{1,0:T(8,128)} custom-call(s32[2]{0:T(128)S(1)} %fusion.15.first_ref, bf16[256,768]{1,0:T(8,128)(2,1)S(1)} %copy-done.65, bf16[256,768]{1,0:T(8,128)(2,1)S(1)} %copy-done.31, bf16[256,768]{1,0:T(8,128)(2,1)S(1)} %copy-done.33, bf16[128,768]{1,0:T(8,128)(2,1)S(1)} %copy-done.110, ...), custom_call_target="tpu_custom_call", output_to_operand_aliasing={{}: (24, {})} | custom-call | tf_op jit(solution)/shard_map/vocab_backward/pallas_call | solution.py:546
  645.0 40.4 %collective-permute-done.126.refs_0_ = bf16[256,768]{1,0:T(8,128)(2,1)S(1)} collective-permute-done((bf16[256,768]{1,0:T(8,128)(2,1)S(1)}, bf16[256,768]{1,0:T(8,128)(2,1)S(1)}, u32[]{:S(2)}, u32[]{:S(2)}) %collective-permute-start.126) | collective-permute-done | bytes 393248 | tf_op jit(solution)/shard_map/ppermute | solution.py:64
  688.0 4.5 collective-permute-start.42
  694.1 6.6 collective-permute-done.131.refs_6_
  703.4 7.5 collective-permute-start.119
  724.3 2.9 maximum_select_fusion
  727.2 5.0 collective-permute-done.137.refs_13_
  732.3 7.4 embed_backward.6.refs_6_
  739.7 3.6 embed_backward.7
  746.9 2.9 maximum_select_fusion.1
  749.8 7.4 embed_backward.4.refs_6_
  757.2 3.5 embed_backward.5
  772.2 3.3 convert_add_fusion
  778.3 4.3 fusion
  (966 shorter events, 288.7 us)
Async XLA Ops:
  7.2 599.3 %all-reduce.12.cloned.1.call-start = ((), (), s32[]{:S(2)}) async-start(), calls=%async_computation | async-start | bytes 5111808 | tf_op jit(solution)/shard_map/psum | solution.py:590
  12.7 46.8 %collective-permute-start.10 = (f32[3,512,512]{2,1,0:T(8,128)}, f32[3,512,512]{2,1,0:T(8,128)}, u32[]{:S(2)}, u32[]{:S(2)}) collective-permute-start(f32[3,512,512]{2,1,0:T(8,128)} %bitcast.10), channel_id=1, source_target_pairs={{0,16},{16,0},{1,17},{17,1},{2,18},{18,2},{3,19},{19,3},{4,20},{20... | collective-permute-start | bytes 9437192 | tf_op jit(solution)/shard_map/ppermute | solution.py:64
  29.6 22.0 %collective-permute-start.8 = (bf16[768,576]{0,1:T(8,128)(2,1)S(1)}, bf16[768,576]{0,1:T(8,128)(2,1)}, u32[]{:S(2)}, u32[]{:S(2)}) collective-permute-start(bf16[768,576]{0,1:T(8,128)(2,1)S(1)} %bitcast.122), channel_id=1, source_target_pairs={{0,16},{16,0},{1,17},{17,1},{2,18},{18,2},{3,19},{19,3},{4,20},{20... | collective-permute-start | bytes 2654216 | tf_op jit(solution)/shard_map/ppermute | solution.py:64
  33.8 16.0 %collective-permute-start.11 = (bf16[192,768]{1,0:T(8,128)(2,1)}, bf16[192,768]{1,0:T(8,128)(2,1)S(1)}, u32[]{:S(2)}, u32[]{:S(2)}) collective-permute-start(bf16[192,768]{1,0:T(8,128)(2,1)} %bitcast.11), channel_id=1, source_target_pairs={{0,16},{16,0},{1,17},{17,1},{2,18},{18,2},{3,19},{19,3},{4,20},{20... | collective-permute-start | bytes 884744 | tf_op jit(solution)/shard_map/ppermute | solution.py:64
  79.9 20.1 %collective-permute-start.20 = (bf16[768,768]{1,0:T(8,128)(2,1)S(1)}, bf16[768,768]{1,0:T(8,128)(2,1)S(1)}, u32[]{:S(2)}, u32[]{:S(2)}) collective-permute-start(bf16[768,768]{1,0:T(8,128)(2,1)S(1)} %bitcast.114), channel_id=1, source_target_pairs={{0,16},{16,0},{1,17},{17,1},{2,18},{18,2},{3,19},{19,3},{4,20},{20... | collective-permute-start | bytes 3538952 | tf_op jit(solution)/shard_map/ppermute | solution.py:64
  83.1 24.5 %collective-permute-start.21 = (bf16[768,768]{1,0:T(8,128)(2,1)S(1)}, bf16[768,768]{1,0:T(8,128)(2,1)S(1)}, u32[]{:S(2)}, u32[]{:S(2)}) collective-permute-start(bf16[768,768]{1,0:T(8,128)(2,1)S(1)} %bitcast.115), channel_id=1, source_target_pairs={{0,16},{16,0},{1,17},{17,1},{2,18},{18,2},{3,19},{19,3},{4,20},{20... | collective-permute-start | bytes 3538952 | tf_op jit(solution)/shard_map/ppermute | solution.py:64
  83.7 14.0 %collective-permute-start.13 = (bf16[256,768]{1,0:T(8,128)(2,1)S(1)}, bf16[256,768]{1,0:T(8,128)(2,1)S(1)}, u32[]{:S(2)}, u32[]{:S(2)}) collective-permute-start(bf16[256,768]{1,0:T(8,128)(2,1)S(1)} %pad_maximum_fusion.4), channel_id=1, source_target_pairs={{0,1},{1,0},{2,3},{3,2},{4,5},{5,4},{6,7},{7,6},{8,9},{9,8},{10,11... | collective-permute-start | bytes 1179656 | tf_op jit(solution)/shard_map/ppermute | solution.py:64
  188.3 13.9 %collective-permute-start.34 = (bf16[256,768]{1,0:T(8,128)(2,1)}, bf16[256,768]{1,0:T(8,128)(2,1)}, u32[]{:S(2)}, u32[]{:S(2)}) collective-permute-start(bf16[256,768]{1,0:T(8,128)(2,1)} %get-tuple-element.203.refs_0_), channel_id=1, source_target_pairs={{0,1},{1,0},{2,3},{3,2},{4,5},{5,4},{6,7},{7,6},{8,9},{9,8},{10,11... | collective-permute-start | bytes 1179656 | tf_op jit(solution)/shard_map/ppermute | solution.py:64
  189.8 15.5 %collective-permute-start.35 = (bf16[256,768]{1,0:T(8,128)(2,1)}, bf16[256,768]{1,0:T(8,128)(2,1)}, u32[]{:S(2)}, u32[]{:S(2)}) collective-permute-start(bf16[256,768]{1,0:T(8,128)(2,1)} %get-tuple-element.203.refs_0_), channel_id=1, source_target_pairs={{0,2},{1,3},{2,0},{3,1},{4,6},{5,7},{6,4},{7,5},{8,10},{9,11},{10,... | collective-permute-start | bytes 1179656 | tf_op jit(solution)/shard_map/ppermute | solution.py:64
  244.6 59.1 %collective-permute-start.58 = (bf16[256,768]{1,0:T(8,128)(2,1)}, bf16[256,768]{1,0:T(8,128)(2,1)}, u32[]{:S(2)}, u32[]{:S(2)}) collective-permute-start(bf16[256,768]{1,0:T(8,128)(2,1)} %pad_maximum_fusion.13), channel_id=1, source_target_pairs={{0,2},{1,3},{2,0},{3,1},{4,6},{5,7},{6,4},{7,5},{8,10},{9,11},{10,... | collective-permute-start | bytes 1179656 | tf_op jit(solution)/shard_map/ppermute | solution.py:64
  249.3 17.8 %collective-permute-start.45 = (bf16[128,768]{1,0:T(8,128)(2,1)S(1)}, bf16[128,768]{1,0:T(8,128)(2,1)S(1)}, u32[]{:S(2)}, u32[]{:S(2)}) collective-permute-start(bf16[128,768]{1,0:T(8,128)(2,1)S(1)} %slice.620), channel_id=1, source_target_pairs={{0,2},{1,3},{2,0},{3,1},{4,6},{5,7},{6,4},{7,5},{8,10},{9,11},{10,... | collective-permute-start | bytes 589832 | tf_op jit(solution)/shard_map/ppermute | solution.py:64
  251.2 17.3 %collective-permute-start.46 = (bf16[128,768]{1,0:T(8,128)(2,1)S(1)}, bf16[128,768]{1,0:T(8,128)(2,1)S(1)}, u32[]{:S(2)}, u32[]{:S(2)}) collective-permute-start(bf16[128,768]{1,0:T(8,128)(2,1)S(1)} %slice.621), channel_id=1, source_target_pairs={{0,1},{1,0},{2,3},{3,2},{4,5},{5,4},{6,7},{7,6},{8,9},{9,8},{10,11... | collective-permute-start | bytes 589832 | tf_op jit(solution)/shard_map/ppermute | solution.py:64
  251.3 17.2 %collective-permute-start.48 = (bf16[256,768]{1,0:T(8,128)(2,1)S(1)}, bf16[256,768]{1,0:T(8,128)(2,1)S(1)}, u32[]{:S(2)}, u32[]{:S(2)}) collective-permute-start(bf16[256,768]{1,0:T(8,128)(2,1)S(1)} %collective-permute-done.47.refs_5_), channel_id=1, source_target_pairs={{0,1},{1,0},{2,3},{3,2},{4,5},{5,4},{6,7},{7,6},{8,9},{9,8},{10,11... | collective-permute-start | bytes 1179656 | tf_op jit(solution)/shard_map/ppermute | solution.py:64
  252.7 15.9 %collective-permute-start.49 = (bf16[256,768]{1,0:T(8,128)(2,1)S(1)}, bf16[256,768]{1,0:T(8,128)(2,1)S(1)}, u32[]{:S(2)}, u32[]{:S(2)}) collective-permute-start(bf16[256,768]{1,0:T(8,128)(2,1)S(1)} %collective-permute-done.47.refs_5_), channel_id=1, source_target_pairs={{0,2},{1,3},{2,0},{3,1},{4,6},{5,7},{6,4},{7,5},{8,10},{9,11},{10,... | collective-permute-start | bytes 1179656 | tf_op jit(solution)/shard_map/ppermute | solution.py:64
  267.1 36.9 %collective-permute-start.56 = (bf16[256,768]{1,0:T(8,128)(2,1)}, bf16[256,768]{1,0:T(8,128)(2,1)}, u32[]{:S(2)}, u32[]{:S(2)}) collective-permute-start(bf16[256,768]{1,0:T(8,128)(2,1)} %pad_maximum_fusion.12), channel_id=1, source_target_pairs={{0,1},{1,0},{2,3},{3,2},{4,5},{5,4},{6,7},{7,6},{8,9},{9,8},{10,11... | collective-permute-start | bytes 1179656 | tf_op jit(solution)/shard_map/ppermute | solution.py:64
  268.5 26.5 %collective-permute-start.50 = (bf16[128,768]{1,0:T(8,128)(2,1)S(1)}, bf16[128,768]{1,0:T(8,128)(2,1)S(1)}, u32[]{:S(2)}, u32[]{:S(2)}) collective-permute-start(bf16[128,768]{1,0:T(8,128)(2,1)S(1)} %slice.622), channel_id=1, source_target_pairs={{0,2},{1,3},{2,0},{3,1},{4,6},{5,7},{6,4},{7,5},{8,10},{9,11},{10,... | collective-permute-start | bytes 589832 | tf_op jit(solution)/shard_map/ppermute | solution.py:64
  268.7 27.0 %collective-permute-start.51 = (bf16[128,768]{1,0:T(8,128)(2,1)S(1)}, bf16[128,768]{1,0:T(8,128)(2,1)S(1)}, u32[]{:S(2)}, u32[]{:S(2)}) collective-permute-start(bf16[128,768]{1,0:T(8,128)(2,1)S(1)} %slice.623), channel_id=1, source_target_pairs={{0,1},{1,0},{2,3},{3,2},{4,5},{5,4},{6,7},{7,6},{8,9},{9,8},{10,11... | collective-permute-start | bytes 589832 | tf_op jit(solution)/shard_map/ppermute | solution.py:64
  296.4 12.1 %collective-permute-start.52 = (bf16[256,896]{1,0:T(8,128)(2,1)}, bf16[256,896]{1,0:T(8,128)(2,1)}, u32[]{:S(2)}, u32[]{:S(2)}) collective-permute-start(bf16[256,896]{1,0:T(8,128)(2,1)} %get-tuple-element.220), channel_id=1, source_target_pairs={{0,1},{1,0},{2,3},{3,2},{4,5},{5,4},{6,7},{7,6},{8,9},{9,8},{10,11... | collective-permute-start | bytes 1376264 | tf_op jit(solution)/shard_map/ppermute | solution.py:64
  296.5 12.6 %collective-permute-start.53 = (bf16[256,896]{1,0:T(8,128)(2,1)}, bf16[256,896]{1,0:T(8,128)(2,1)}, u32[]{:S(2)}, u32[]{:S(2)}) collective-permute-start(bf16[256,896]{1,0:T(8,128)(2,1)} %get-tuple-element.221), channel_id=1, source_target_pairs={{0,2},{1,3},{2,0},{3,1},{4,6},{5,7},{6,4},{7,5},{8,10},{9,11},{10,... | collective-permute-start | bytes 1376264 | tf_op jit(solution)/shard_map/ppermute | solution.py:64
  313.9 13.2 %collective-permute-start.82 = (bf16[256,768]{1,0:T(8,128)(2,1)S(1)}, bf16[256,768]{1,0:T(8,128)(2,1)S(1)}, u32[]{:S(2)}, u32[]{:S(2)}) collective-permute-start(bf16[256,768]{1,0:T(8,128)(2,1)S(1)} %copy-done.63), channel_id=1, source_target_pairs={{0,8},{4,12},{8,0},{12,4},{1,9},{5,13},{9,1},{13,5},{2,10},{6,14},... | collective-permute-start | bytes 1179656 | tf_op jit(solution)/shard_map/ppermute | solution.py:64
  313.9 20.9 %collective-permute-start.87 = (bf16[256,768]{1,0:T(8,128)(2,1)S(1)}, bf16[256,768]{1,0:T(8,128)(2,1)S(1)}, u32[]{:S(2)}, u32[]{:S(2)}) collective-permute-start(bf16[256,768]{1,0:T(8,128)(2,1)S(1)} %copy-done.63), channel_id=1, source_target_pairs={{0,12},{4,8},{8,4},{12,0},{1,13},{5,9},{9,5},{13,1},{2,14},{6,10},... | collective-permute-start | bytes 1179656 | tf_op jit(solution)/shard_map/ppermute | solution.py:64
  318.4 17.8 %collective-permute-start.61 = (bf16[128,768]{1,0:T(8,128)(2,1)S(1)}, bf16[128,768]{1,0:T(8,128)(2,1)S(1)}, u32[]{:S(2)}, u32[]{:S(2)}) collective-permute-start(bf16[128,768]{1,0:T(8,128)(2,1)S(1)} %slice.631), channel_id=1, source_target_pairs={{0,2},{1,3},{2,0},{3,1},{4,6},{5,7},{6,4},{7,5},{8,10},{9,11},{10,... | collective-permute-start | bytes 589832 | tf_op jit(solution)/shard_map/ppermute | solution.py:64
  319.9 16.3 %collective-permute-start.62 = (bf16[128,768]{1,0:T(8,128)(2,1)S(1)}, bf16[128,768]{1,0:T(8,128)(2,1)S(1)}, u32[]{:S(2)}, u32[]{:S(2)}) collective-permute-start(bf16[128,768]{1,0:T(8,128)(2,1)S(1)} %slice.632), channel_id=1, source_target_pairs={{0,1},{1,0},{2,3},{3,2},{4,5},{5,4},{6,7},{7,6},{8,9},{9,8},{10,11... | collective-permute-start | bytes 589832 | tf_op jit(solution)/shard_map/ppermute | solution.py:64
  327.0 51.5 %collective-permute-start.83 = (bf16[256,768]{1,0:T(8,128)(2,1)S(1)}, bf16[256,768]{1,0:T(8,128)(2,1)S(1)}, u32[]{:S(2)}, u32[]{:S(2)}) collective-permute-start(bf16[256,768]{1,0:T(8,128)(2,1)S(1)} %collective-permute-done.82.refs_10_), channel_id=1, source_target_pairs={{0,1},{1,0},{2,3},{3,2},{4,5},{5,4},{6,7},{7,6},{8,9},{9,8},{10,11... | collective-permute-start | bytes 1179656 | tf_op jit(solution)/shard_map/ppermute | solution.py:64
  328.4 51.2 %collective-permute-start.84 = (bf16[256,768]{1,0:T(8,128)(2,1)S(1)}, bf16[256,768]{1,0:T(8,128)(2,1)S(1)}, u32[]{:S(2)}, u32[]{:S(2)}) collective-permute-start(bf16[256,768]{1,0:T(8,128)(2,1)S(1)} %collective-permute-done.82.refs_10_), channel_id=1, source_target_pairs={{0,2},{1,3},{2,0},{3,1},{4,6},{5,7},{6,4},{7,5},{8,10},{9,11},{10,... | collective-permute-start | bytes 1179656 | tf_op jit(solution)/shard_map/ppermute | solution.py:64
  334.8 46.0 %collective-permute-start.88 = (bf16[256,768]{1,0:T(8,128)(2,1)S(1)}, bf16[256,768]{1,0:T(8,128)(2,1)S(1)}, u32[]{:S(2)}, u32[]{:S(2)}) collective-permute-start(bf16[256,768]{1,0:T(8,128)(2,1)S(1)} %collective-permute-done.87.refs_15_), channel_id=1, source_target_pairs={{0,1},{1,0},{2,3},{3,2},{4,5},{5,4},{6,7},{7,6},{8,9},{9,8},{10,11... | collective-permute-start | bytes 1179656 | tf_op jit(solution)/shard_map/ppermute | solution.py:64
  336.2 45.4 %collective-permute-start.89 = (bf16[256,768]{1,0:T(8,128)(2,1)S(1)}, bf16[256,768]{1,0:T(8,128)(2,1)S(1)}, u32[]{:S(2)}, u32[]{:S(2)}) collective-permute-start(bf16[256,768]{1,0:T(8,128)(2,1)S(1)} %collective-permute-done.87.refs_15_), channel_id=1, source_target_pairs={{0,2},{1,3},{2,0},{3,1},{4,6},{5,7},{6,4},{7,5},{8,10},{9,11},{10,... | collective-permute-start | bytes 1179656 | tf_op jit(solution)/shard_map/ppermute | solution.py:64
  350.6 51.5 %collective-permute-start.71 = (bf16[768,768]{1,0:T(8,128)(2,1)S(1)}, bf16[768,768]{1,0:T(8,128)(2,1)S(1)}, u32[]{:S(2)}, u32[]{:S(2)}) collective-permute-start(bf16[768,768]{1,0:T(8,128)(2,1)S(1)} %get-tuple-element.452), channel_id=1, source_target_pairs={{0,16},{16,0},{1,17},{17,1},{2,18},{18,2},{3,19},{19,3},{4,20},{20... | collective-permute-start | bytes 3538952 | tf_op jit(solution)/shard_map/ppermute | solution.py:64
  382.3 60.4 %collective-permute-start.107 = (f32[8,256]{1,0:T(8,128)S(1)}, f32[8,256]{1,0:T(8,128)S(1)}, u32[]{:S(2)}, u32[]{:S(2)}) collective-permute-start(f32[8,256]{1,0:T(8,128)S(1)} %get-tuple-element.311), channel_id=1, source_target_pairs={{0,3},{1,2},{2,1},{3,0},{4,7},{5,6},{6,5},{7,4},{8,11},{9,10},{10,... | collective-permute-start | bytes 24584 | tf_op jit(solution)/shard_map/ppermute | solution.py:64
  392.6 45.8 %collective-permute-start.106 = (f32[8,256]{1,0:T(8,128)S(1)}, f32[8,256]{1,0:T(8,128)S(1)}, u32[]{:S(2)}, u32[]{:S(2)}) collective-permute-start(f32[8,256]{1,0:T(8,128)S(1)} %get-tuple-element.311), channel_id=1, source_target_pairs={{0,2},{1,3},{2,0},{3,1},{4,6},{5,7},{6,4},{7,5},{8,10},{9,11},{10,... | collective-permute-start | bytes 24584 | tf_op jit(solution)/shard_map/ppermute | solution.py:64
  431.5 12.0 %collective-permute-start.80 = (bf16[384,768]{0,1:T(8,128)(2,1)S(1)}, bf16[384,768]{0,1:T(8,128)(2,1)S(1)}, u32[]{:S(2)}, u32[]{:S(2)}) collective-permute-start(bf16[384,768]{0,1:T(8,128)(2,1)S(1)} %fusion.3), channel_id=1, source_target_pairs={{0,16},{16,0},{1,17},{17,1},{2,18},{18,2},{3,19},{19,3},{4,20},{20... | collective-permute-start | bytes 1769480 | tf_op jit(solution)/shard_map/ppermute | solution.py:64
  438.5 19.5 %collective-permute-start.81 = (bf16[768,512]{1,0:T(8,128)(2,1)S(1)}, bf16[768,512]{1,0:T(8,128)(2,1)S(1)}, u32[]{:S(2)}, u32[]{:S(2)}) collective-permute-start(bf16[768,512]{1,0:T(8,128)(2,1)S(1)} %constant_dynamic-slice_fusion.4), channel_id=1, source_target_pairs={{0,16},{16,0},{1,17},{17,1},{2,18},{18,2},{3,19},{19,3},{4,20},{20... | collective-permute-start | bytes 2359304 | tf_op jit(solution)/shard_map/ppermute | solution.py:64
  440.3 15.4 %collective-permute-start.85 = (bf16[128,768]{1,0:T(8,128)(2,1)S(1)}, bf16[128,768]{1,0:T(8,128)(2,1)S(1)}, u32[]{:S(2)}, u32[]{:S(2)}) collective-permute-start(bf16[128,768]{1,0:T(8,128)(2,1)S(1)} %slice.639), channel_id=1, source_target_pairs={{0,2},{1,3},{2,0},{3,1},{4,6},{5,7},{6,4},{7,5},{8,10},{9,11},{10,... | collective-permute-start | bytes 589832 | tf_op jit(solution)/shard_map/ppermute | solution.py:64
  442.7 12.3 %collective-permute-start.77 = (bf16[256,768]{1,0:T(8,128)(2,1)S(1)}, bf16[256,768]{1,0:T(8,128)(2,1)S(1)}, u32[]{:S(2)}, u32[]{:S(2)}) collective-permute-start(bf16[256,768]{1,0:T(8,128)(2,1)S(1)} %get-tuple-element.266.refs_0_), channel_id=1, source_target_pairs={{0,2},{1,3},{2,0},{3,1},{4,6},{5,7},{6,4},{7,5},{8,10},{9,11},{10,... | collective-permute-start | bytes 1179656 | tf_op jit(solution)/shard_map/ppermute | solution.py:64
  443.5 15.7 %collective-permute-start.86 = (bf16[128,768]{1,0:T(8,128)(2,1)}, bf16[128,768]{1,0:T(8,128)(2,1)}, u32[]{:S(2)}, u32[]{:S(2)}) collective-permute-start(bf16[128,768]{1,0:T(8,128)(2,1)} %slice.640), channel_id=1, source_target_pairs={{0,1},{1,0},{2,3},{3,2},{4,5},{5,4},{6,7},{7,6},{8,9},{9,8},{10,11... | collective-permute-start | bytes 589832 | tf_op jit(solution)/shard_map/ppermute | solution.py:64
  448.4 12.2 %collective-permute-start.90 = (bf16[128,768]{1,0:T(8,128)(2,1)}, bf16[128,768]{1,0:T(8,128)(2,1)}, u32[]{:S(2)}, u32[]{:S(2)}) collective-permute-start(bf16[128,768]{1,0:T(8,128)(2,1)} %slice.641), channel_id=1, source_target_pairs={{0,2},{1,3},{2,0},{3,1},{4,6},{5,7},{6,4},{7,5},{8,10},{9,11},{10,... | collective-permute-start | bytes 589832 | tf_op jit(solution)/shard_map/ppermute | solution.py:64
  459.1 28.9 %collective-permute-start.108 = (f32[1,1024]{1,0:T(1,128)}, f32[1,1024]{1,0:T(1,128)S(1)}, u32[]{:S(2)}, u32[]{:S(2)}) collective-permute-start(f32[1,1024]{1,0:T(1,128)} %pad_maximum_fusion.23), channel_id=1, source_target_pairs={{0,4},{4,0},{8,12},{12,8},{1,5},{5,1},{9,13},{13,9},{2,6},{6,2},{1... | collective-permute-start | bytes 12296 | tf_op jit(solution)/shard_map/ppermute | solution.py:64
  460.7 28.6 %collective-permute-start.109 = (f32[1,1024]{1,0:T(1,128)}, f32[1,1024]{1,0:T(1,128)S(1)}, u32[]{:S(2)}, u32[]{:S(2)}) collective-permute-start(f32[1,1024]{1,0:T(1,128)} %pad_maximum_fusion.23), channel_id=1, source_target_pairs={{0,8},{4,12},{8,0},{12,4},{1,9},{5,13},{9,1},{13,5},{2,10},{6,14},... | collective-permute-start | bytes 12296 | tf_op jit(solution)/shard_map/ppermute | solution.py:64
  461.8 102.1 %collective-permute-start.110 = (f32[1,1024]{1,0:T(1,128)}, f32[1,1024]{1,0:T(1,128)}, u32[]{:S(2)}, u32[]{:S(2)}) collective-permute-start(f32[1,1024]{1,0:T(1,128)} %pad_maximum_fusion.23), channel_id=1, source_target_pairs={{0,12},{4,8},{8,4},{12,0},{1,13},{5,9},{9,5},{13,1},{2,14},{6,10},... | collective-permute-start | bytes 12296 | tf_op jit(solution)/shard_map/ppermute | solution.py:64
  475.6 11.9 %collective-permute-start.94 = (bf16[128,768]{1,0:T(8,128)(2,1)S(1)}, bf16[128,768]{1,0:T(8,128)(2,1)S(1)}, u32[]{:S(2)}, u32[]{:S(2)}) collective-permute-start(bf16[128,768]{1,0:T(8,128)(2,1)S(1)} %get-tuple-element.276), channel_id=1, source_target_pairs={{0,1},{1,0},{2,3},{3,2},{4,5},{5,4},{6,7},{7,6},{8,9},{9,8},{10,11... | collective-permute-start | bytes 589832 | tf_op jit(solution)/shard_map/ppermute | solution.py:64
  481.3 32.5 %collective-permute-start.100 = (bf16[768,768]{1,0:T(8,128)(2,1)}, bf16[768,768]{1,0:T(8,128)(2,1)}, u32[]{:S(2)}, u32[]{:S(2)}) collective-permute-start(bf16[768,768]{1,0:T(8,128)(2,1)} %get-tuple-element.454), channel_id=1, source_target_pairs={{0,16},{16,0},{1,17},{17,1},{2,18},{18,2},{3,19},{19,3},{4,20},{20... | collective-permute-start | bytes 3538952 | tf_op jit(solution)/shard_map/ppermute | solution.py:64
  502.7 258.0 %all-reduce.14.cloned.1.call-start = ((), (), s32[]{:S(2)}) async-start(), calls=%async_computation.1 | async-start | bytes 5505024 | tf_op jit(solution)/shard_map/psum | solution.py:590
  538.1 20.0 %collective-permute-start.101 = (bf16[128,768]{1,0:T(8,128)(2,1)}, bf16[128,768]{1,0:T(8,128)(2,1)}, u32[]{:S(2)}, u32[]{:S(2)}) collective-permute-start(bf16[128,768]{1,0:T(8,128)(2,1)} %get-tuple-element.293), channel_id=1, source_target_pairs={{0,2},{1,3},{2,0},{3,1},{4,6},{5,7},{6,4},{7,5},{8,10},{9,11},{10,... | collective-permute-start | bytes 589832 | tf_op jit(solution)/shard_map/ppermute | solution.py:64
  538.2 22.1 %collective-permute-start.103 = (bf16[128,768]{1,0:T(8,128)(2,1)}, bf16[128,768]{1,0:T(8,128)(2,1)}, u32[]{:S(2)}, u32[]{:S(2)}) collective-permute-start(bf16[128,768]{1,0:T(8,128)(2,1)} %get-tuple-element.295), channel_id=1, source_target_pairs={{0,1},{1,0},{2,3},{3,2},{4,5},{5,4},{6,7},{7,6},{8,9},{9,8},{10,11... | collective-permute-start | bytes 589832 | tf_op jit(solution)/shard_map/ppermute | solution.py:64
  543.8 43.7 %collective-permute-start.114 = (bf16[384,768]{0,1:T(8,128)(2,1)}, bf16[384,768]{0,1:T(8,128)(2,1)}, u32[]{:S(2)}, u32[]{:S(2)}) collective-permute-start(bf16[384,768]{0,1:T(8,128)(2,1)} %fusion.1), channel_id=1, source_target_pairs={{0,16},{16,0},{1,17},{17,1},{2,18},{18,2},{3,19},{19,3},{4,20},{20... | collective-permute-start | bytes 1769480 | tf_op jit(solution)/shard_map/ppermute | solution.py:64
  557.3 31.7 %collective-permute-start.115 = (bf16[768,512]{1,0:T(8,128)(2,1)}, bf16[768,512]{1,0:T(8,128)(2,1)}, u32[]{:S(2)}, u32[]{:S(2)}) collective-permute-start(bf16[768,512]{1,0:T(8,128)(2,1)} %constant_dynamic-slice_fusion.1), channel_id=1, source_target_pairs={{0,16},{16,0},{1,17},{17,1},{2,18},{18,2},{3,19},{19,3},{4,20},{20... | collective-permute-start | bytes 2359304 | tf_op jit(solution)/shard_map/ppermute | solution.py:64
  560.3 27.2 %collective-permute-start.102 = (bf16[256,768]{1,0:T(8,128)(2,1)}, bf16[256,768]{1,0:T(8,128)(2,1)}, u32[]{:S(2)}, u32[]{:S(2)}) collective-permute-start(bf16[256,768]{1,0:T(8,128)(2,1)} %pad_maximum_fusion.20), channel_id=1, source_target_pairs={{0,1},{1,0},{2,3},{3,2},{4,5},{5,4},{6,7},{7,6},{8,9},{9,8},{10,11... | collective-permute-start | bytes 1179656 | tf_op jit(solution)/shard_map/ppermute | solution.py:64
  563.8 23.7 %collective-permute-start.104 = (bf16[256,768]{1,0:T(8,128)(2,1)}, bf16[256,768]{1,0:T(8,128)(2,1)}, u32[]{:S(2)}, u32[]{:S(2)}) collective-permute-start(bf16[256,768]{1,0:T(8,128)(2,1)} %pad_maximum_fusion.21), channel_id=1, source_target_pairs={{0,2},{1,3},{2,0},{3,1},{4,6},{5,7},{6,4},{7,5},{8,10},{9,11},{10,... | collective-permute-start | bytes 1179656 | tf_op jit(solution)/shard_map/ppermute | solution.py:64
  563.9 23.5 %collective-permute-start.118 = (f32[2,18,768]{2,1,0:T(8,128)S(1)}, f32[2,18,768]{2,1,0:T(8,128)S(1)}, u32[]{:S(2)}, u32[]{:S(2)}) collective-permute-start(f32[2,18,768]{2,1,0:T(8,128)S(1)} %fusion.55), channel_id=1, source_target_pairs={{0,16},{16,0},{1,17},{17,1},{2,18},{18,2},{3,19},{19,3},{4,20},{20... | collective-permute-start | bytes 331784 | tf_op jit(solution)/shard_map/ppermute | solution.py:64
  612.1 32.9 %collective-permute-start.124 = (bf16[256,768]{1,0:T(8,128)(2,1)S(1)}, bf16[256,768]{1,0:T(8,128)(2,1)S(1)}, u32[]{:S(2)}, u32[]{:S(2)}) collective-permute-start(bf16[256,768]{1,0:T(8,128)(2,1)S(1)} %get-tuple-element.340.refs_0_), channel_id=1, source_target_pairs={{0,4},{4,0},{8,12},{12,8},{1,5},{5,1},{9,13},{13,9},{2,6},{6,2},{1... | collective-permute-start | bytes 1179656 | tf_op jit(solution)/shard_map/ppermute | solution.py:64
  612.5 32.5 %collective-permute-start.125 = (bf16[256,768]{1,0:T(8,128)(2,1)S(1)}, bf16[256,768]{1,0:T(8,128)(2,1)}, u32[]{:S(2)}, u32[]{:S(2)}) collective-permute-start(bf16[256,768]{1,0:T(8,128)(2,1)S(1)} %get-tuple-element.340.refs_0_), channel_id=1, source_target_pairs={{0,8},{4,12},{8,0},{12,4},{1,9},{5,13},{9,1},{13,5},{2,10},{6,14},... | collective-permute-start | bytes 1179656 | tf_op jit(solution)/shard_map/ppermute | solution.py:64
  613.3 72.2 %collective-permute-start.126 = (bf16[256,768]{1,0:T(8,128)(2,1)S(1)}, bf16[256,768]{1,0:T(8,128)(2,1)S(1)}, u32[]{:S(2)}, u32[]{:S(2)}) collective-permute-start(bf16[256,768]{1,0:T(8,128)(2,1)S(1)} %get-tuple-element.340.refs_0_), channel_id=1, source_target_pairs={{0,12},{4,8},{8,4},{12,0},{1,13},{5,9},{9,5},{13,1},{2,14},{6,10},... | collective-permute-start | bytes 1179656 | tf_op jit(solution)/shard_map/ppermute | solution.py:64
  619.9 65.6 %collective-permute-start.122 = (bf16[128,768]{1,0:T(8,128)(2,1)S(1)}, bf16[128,768]{1,0:T(8,128)(2,1)S(1)}, u32[]{:S(2)}, u32[]{:S(2)}) collective-permute-start(bf16[128,768]{1,0:T(8,128)(2,1)S(1)} %slice.653), channel_id=1, source_target_pairs={{0,2},{1,3},{2,0},{3,1},{4,6},{5,7},{6,4},{7,5},{8,10},{9,11},{10,... | collective-permute-start | bytes 589832 | tf_op jit(solution)/shard_map/ppermute | solution.py:64
  622.0 63.5 %collective-permute-start.123 = (bf16[128,768]{1,0:T(8,128)(2,1)S(1)}, bf16[128,768]{1,0:T(8,128)(2,1)S(1)}, u32[]{:S(2)}, u32[]{:S(2)}) collective-permute-start(bf16[128,768]{1,0:T(8,128)(2,1)S(1)} %slice.654), channel_id=1, source_target_pairs={{0,1},{1,0},{2,3},{3,2},{4,5},{5,4},{6,7},{7,6},{8,9},{9,8},{10,11... | collective-permute-start | bytes 589832 | tf_op jit(solution)/shard_map/ppermute | solution.py:64
  685.6 15.2 %collective-permute-start.131 = (bf16[256,768]{1,0:T(8,128)(2,1)S(1)}, bf16[256,768]{1,0:T(8,128)(2,1)S(1)}, u32[]{:S(2)}, u32[]{:S(2)}) collective-permute-start(bf16[256,768]{1,0:T(8,128)(2,1)S(1)} %collective-permute-done.124.refs_5_), channel_id=1, source_target_pairs={{0,1},{1,0},{2,3},{3,2},{4,5},{5,4},{6,7},{7,6},{8,9},{9,8},{10,11... | collective-permute-start | bytes 1179656 | tf_op jit(solution)/shard_map/ppermute | solution.py:64
  688.0 33.0 %collective-permute-start.42 = (f32[256,768]{1,0:T(8,128)}, f32[256,768]{1,0:T(8,128)}, u32[]{:S(2)}, u32[]{:S(2)}) collective-permute-start(f32[256,768]{1,0:T(8,128)} %broadcast_select_fusion.20), channel_id=1, source_target_pairs={{0,16},{16,0},{1,17},{17,1},{2,18},{18,2},{3,19},{19,3},{4,20},{20... | collective-permute-start | bytes 2359304 | tf_op jit(solution)/shard_map/ppermute | solution.py:64
  692.6 19.7 %collective-permute-start.128 = (bf16[256,768]{1,0:T(8,128)(2,1)S(1)}, bf16[256,768]{1,0:T(8,128)(2,1)}, u32[]{:S(2)}, u32[]{:S(2)}) collective-permute-start(bf16[256,768]{1,0:T(8,128)(2,1)S(1)} %collective-permute-done.126.refs_0_), channel_id=1, source_target_pairs={{0,2},{1,3},{2,0},{3,1},{4,6},{5,7},{6,4},{7,5},{8,10},{9,11},{10,... | collective-permute-start | bytes 1179656 | tf_op jit(solution)/shard_map/ppermute | solution.py:64
  694.0 20.1 %collective-permute-start.135 = (bf16[256,768]{1,0:T(8,128)(2,1)}, bf16[256,768]{1,0:T(8,128)(2,1)}, u32[]{:S(2)}, u32[]{:S(2)}) collective-permute-start(bf16[256,768]{1,0:T(8,128)(2,1)} %collective-permute-done.125.refs_10_), channel_id=1, source_target_pairs={{0,1},{1,0},{2,3},{3,2},{4,5},{5,4},{6,7},{7,6},{8,9},{9,8},{10,11... | collective-permute-start | bytes 1179656 | tf_op jit(solution)/shard_map/ppermute | solution.py:64
  700.8 18.8 %collective-permute-start.136 = (bf16[256,768]{1,0:T(8,128)(2,1)}, bf16[256,768]{1,0:T(8,128)(2,1)}, u32[]{:S(2)}, u32[]{:S(2)}) collective-permute-start(bf16[256,768]{1,0:T(8,128)(2,1)} %collective-permute-done.125.refs_10_), channel_id=1, source_target_pairs={{0,2},{1,3},{2,0},{3,1},{4,6},{5,7},{6,4},{7,5},{8,10},{9,11},{10,... | collective-permute-start | bytes 1179656 | tf_op jit(solution)/shard_map/ppermute | solution.py:64
  703.4 42.6 %collective-permute-start.119 = (f32[256,768]{1,0:T(8,128)}, f32[256,768]{1,0:T(8,128)S(1)}, u32[]{:S(2)}, u32[]{:S(2)}) collective-permute-start(f32[256,768]{1,0:T(8,128)} %broadcast_select_fusion.19), channel_id=1, source_target_pairs={{0,16},{16,0},{1,17},{17,1},{2,18},{18,2},{3,19},{19,3},{4,20},{20... | collective-permute-start | bytes 2359304 | tf_op jit(solution)/shard_map/ppermute | solution.py:64
  719.6 20.1 %collective-permute-start.129 = (bf16[128,768]{1,0:T(8,128)(2,1)S(1)}, bf16[128,768]{1,0:T(8,128)(2,1)S(1)}, u32[]{:S(2)}, u32[]{:S(2)}) collective-permute-start(bf16[128,768]{1,0:T(8,128)(2,1)S(1)} %slice.655), channel_id=1, source_target_pairs={{0,2},{1,3},{2,0},{3,1},{4,6},{5,7},{6,4},{7,5},{8,10},{9,11},{10,... | collective-permute-start | bytes 589832 | tf_op jit(solution)/shard_map/ppermute | solution.py:64
  721.0 18.7 %collective-permute-start.130 = (bf16[128,768]{1,0:T(8,128)(2,1)S(1)}, bf16[128,768]{1,0:T(8,128)(2,1)S(1)}, u32[]{:S(2)}, u32[]{:S(2)}) collective-permute-start(bf16[128,768]{1,0:T(8,128)(2,1)S(1)} %slice.656), channel_id=1, source_target_pairs={{0,1},{1,0},{2,3},{3,2},{4,5},{5,4},{6,7},{7,6},{8,9},{9,8},{10,11... | collective-permute-start | bytes 589832 | tf_op jit(solution)/shard_map/ppermute | solution.py:64
  744.6 27.6 %collective-permute-start.139 = (bf16[960,768]{1,0:T(8,128)(2,1)}, bf16[960,768]{1,0:T(8,128)(2,1)}, u32[]{:S(2)}, u32[]{:S(2)}) collective-permute-start(bf16[960,768]{1,0:T(8,128)(2,1)} %convert_element_type.405), channel_id=1, source_target_pairs={{0,16},{16,0},{1,17},{17,1},{2,18},{18,2},{3,19},{19,3},{4,20},{20... | collective-permute-start | bytes 4423688 | tf_op jit(solution)/shard_map/ppermute | solution.py:64
  770.3 12.3 %collective-permute-start.141 = (bf16[768,768]{1,0:T(8,128)(2,1)S(1)}, bf16[768,768]{1,0:T(8,128)(2,1)S(1)}, u32[]{:S(2)}, u32[]{:S(2)}) collective-permute-start(bf16[768,768]{1,0:T(8,128)(2,1)S(1)} %broadcast_select_fusion.6), channel_id=1, source_target_pairs={{0,16},{16,0},{1,17},{17,1},{2,18},{18,2},{3,19},{19,3},{4,20},{20... | collective-permute-start | bytes 3538952 | tf_op jit(solution)/shard_map/ppermute | solution.py:64
  (322 other events, 3767.0 us)
Sparse Core Ops, SparseCore 0:
  502.8 103.6 all-reduce.11
  609.9 138.8 all-reduce.13

commit v3 on v2

--- a/solution.py
+++ b/solution.py
@@ -55,7 +55,7 @@
         out_specs=whole_specs(len(outs)),
         scratch_shapes=list(scratch),
         compiler_params=pltpu.CompilerParams(vmem_limit_bytes=vmem * MIB),
-        cost_estimate=pl.CostEstimate(flops=flops, bytes_accessed=moved, transcendentals=0),
+        cost_estimate=pl.CostEstimate(flops=0, bytes_accessed=0, transcendentals=0),
     )(*scalars, *arrays)
 
 
@@ -531,9 +531,7 @@
             pltpu.VMEM((tokens, 1), F32),
         ],
         compiler_params=pltpu.CompilerParams(vmem_limit_bytes=44 * MIB),
-        cost_estimate=pl.CostEstimate(
-            flops=4 * tokens * vocab * width, bytes_accessed=2 * vocab * width, transcendentals=vocab * tokens
-        ),
+        cost_estimate=pl.CostEstimate(flops=0, bytes_accessed=0, transcendentals=0),
     )(*pieces, embedding)
 
 
@@ -555,9 +553,7 @@
         out_shape=sds((count, width), F32),
         input_output_aliases={1 + len(pieces) + len(columns) + len(given): 0},
         compiler_params=pltpu.CompilerParams(vmem_limit_bytes=44 * MIB),
-        cost_estimate=pl.CostEstimate(
-            flops=0, bytes_accessed=0, transcendentals=0
-        ),
+        cost_estimate=pl.CostEstimate(flops=0, bytes_accessed=0, transcendentals=0),
     )(firsts, *pieces, *columns, *given, so_far)
 
 

time: 801 us -> 799 us (level)
    unnamed x488 -> x448, local copies, waits for them, and re-layouts: 39.8 us -> 35.7 us
  transfers between devices with their start and end apart: 145 -> 145, of which waited for: 52 -> 54; matrix products, arithmetic and copies ran while one was open for 20% -> 20% of each run, Pallas kernels for 19% -> 19%
where the time goes in v3:
time: 799 us; the launch traced here: 790 us
  waiting for transfers between devices  222 us (28%)
  Pallas kernels  186 us (23%)
  starting transfers between devices  164 us (21%)
  local copies, waits for them, and re-layouts  110 us (14%)
  other arithmetic  79.2 us (10%)
  between operations  17.3 us (2%)
  matrix products  11.7 us (1%)
    ppermute x143, waiting for transfers between devices, swap(): return lax.ppermute(array, axis, [(i, i ^ bit) for i in range(count)])  208 us
    ppermute x143, starting transfers between devices, swap(): return lax.ppermute(array, axis, [(i, i ^ bit) for i in range(count)])  164 us
    pallas_call x16, Pallas kernels, kernel_call(): pl.pallas_call(kernel, name=name, out_shape=outs, in_specs=scalar_specs(l...  85.5 us
    pallas_call x6, Pallas kernels, owned_rows(): pl.pallas_call(kernel, name=name, grid=(steps,), in_specs=scalar_specs(1)...  62.4 us
    pallas_call x2, Pallas kernels, head_blocks(): pl.pallas_call(functools.partial(head_forward, len(pieces)), name='head_f...  38.3 us
    unnamed x448, local copies, waits for them, and re-layouts  35.7 us
    gather x2, local copies, waits for them, and re-layouts, lookup_rows(): embedding[jnp.clip(ids, 0, rows - 1)]  22 us
  transfers between devices with their start and end apart: 145, of which 54 were waited for; matrix products, arithmetic and copies ran while one was open for 20% of the time, Pallas kernels for 19%

profile of v3, /device:TPU:17, one launch (start us, length us, event | category | flops | bytes accessed | tf_op | source)
XLA Modules:
  0.0 789.9 jit_solution(490639969580493752)
XLA Ops:
  7.3 5.4 add_divide_fusion
  16.4 10.3 %gather_fusion.1 = bf16[1024,768]{1,0:T(8,128)(2,1)S(1)} fusion(bf16[7680,768]{1,0:T(8,128)(2,1)} %refs_4_.1, s32[1024]{0:T(1024)S(1)} %broadcast_clamp_fusion.1), kind=kCustom, calls=%fused_computation.1 | custom fusion | bytes 3149824 | tf_op jit(solution)/shard_map/gather | solution.py:569
  39.6 5.7 collective-permute-done.3
  59.4 5.7 broadcast_select_fusion.2
  65.2 12.3 %attention_forward.2 = (f32[256,768]{1,0:T(8,128)S(1)}, bf16[256,768]{1,0:T(8,128)(2,1)S(1)}, bf16[256,768]{1,0:T(8,128)(2,1)S(1)}, bf16[128,768]{1,0:T(8,128)(2...) custom-call(s32[4]{0:T(128)S(1)} %fusion.14.len_ref, ...), custom_call_target="tpu_custom_call" | custom-call | tf_op jit(solution)/shard_map/attention_forward/pallas_call | solution.py:50
  79.9 3.2 collective-permute-start.20
  84.9 4.4 collective-permute-done.14
  90.8 6.9 collective-permute-done.13.near
  101.1 4.9 collective-permute-done.16.refs_1_
  108.8 3.0 collective-permute-done.18.refs_3_
  111.8 3.3 feed_forward.2
  119.0 3.0 collective-permute-done.22
  123.7 6.4 collective-permute-done.23.near
  136.4 6.2 collective-permute-done.26.refs_1_
  148.1 2.8 copy.51.refs_5_
  150.9 3.2 collective-permute-done.29.refs_4_
  158.3 13.0 %attention_forward.3 = (f32[256,768]{1,0:T(8,128)S(1)}, bf16[256,768]{1,0:T(8,128)(2,1)S(1)}, bf16[256,768]{1,0:T(8,128)(2,1)S(1)}, bf16[128,768]{1,0:T(8,128)(2...) custom-call(s32[4]{0:T(128)S(1)} %fusion.14.len_ref, ...), custom_call_target="tpu_custom_call" | custom-call | tf_op jit(solution)/shard_map/attention_forward/pallas_call | solution.py:50
  173.7 2.9 collective-permute-done.30
  179.5 3.9 collective-permute-done.31.near
  187.1 9.5 %collective-permute-done.34.refs_1_ = bf16[256,768]{1,0:T(8,128)(2,1)S(1)} collective-permute-done((bf16[256,768]{1,0:T(8,128)(2,1)S(1)}, bf16[256,768]{1,0:T(8,128)(2,1)S(1)}, u32[]{:S(2)}, u32[]{:S(2)}) %collective-permute-start.34) | collective-permute-done | bytes 393248 | tf_op jit(solution)/shard_map/ppermute | solution.py:64
  198.3 4.2 collective-permute-done.36.refs_3_
  202.5 3.2 feed_forward.3
  218.2 11.7 %gather_fusion.3 = bf16[1024,768]{1,0:T(8,128)(2,1)} fusion(bf16[7680,768]{1,0:T(8,128)(2,1)} %refs_4_.1, s32[1024]{0:T(1024)} %broadcast_clamp_fusion), kind=kCustom, calls=%fused_computation.3 | custom fusion | bytes 3149824 | tf_op jit(solution)/shard_map/gather | solution.py:569
  257.3 13.3 %head_forward.2.own = f32[256,896]{1,0:T(8,128)S(1)} custom-call(bf16[256,768]{1,0:T(8,128)(2,1)} %get-tuple-element.211.refs_0_, bf16[7680,768]{1,0:T(8,128)(2,1)} %refs_4_.1), custom_call_target="tpu_custom_call" | custom-call | tf_op jit(solution)/shard_map/head_forward/pallas_call | solution.py:519
  271.6 25.0 %head_forward.3 = (bf16[256,896]{1,0:T(8,128)(2,1)}, bf16[256,896]{1,0:T(8,128)(2,1)}, bf16[256,896]{1,0:T(8,128)(2,1)}) custom-call(bf16[256,768]{1,0:T(8,128)(2,1)S(1)} %collective-permute-done.43.refs_0_.refs_1_, bf16[256,768]{1,0:T(8,128)(2,1)} %collective-permute-done.44.refs_1_.refs_2_, bf16[128,768]{1,0:T(8,128)(2,1)S(1)} %collective-permute-done.45.refs_2_.refs_3_, ...), custom_call_target="tpu_custom_call" | custom-call | tf_op jit(solution)/shard_map/head_forward/pallas_call | solution.py:519
  303.0 3.7 constant_dynamic-slice_fusion
  306.9 3.3 collective-permute-start.112
  323.2 7.4 collective-permute-done.82.refs_10_
  332.2 5.3 collective-permute-done.87.refs_15_
  339.0 2.8 feed_backward.2
  345.4 3.0 collective-permute-done.63
  348.5 4.7 collective-permute-done.65
  353.2 29.0 %collective-permute-start.71 = (bf16[768,768]{1,0:T(8,128)(2,1)S(1)}, bf16[768,768]{1,0:T(8,128)(2,1)S(1)}, u32[]{:S(2)}, u32[]{:S(2)}) collective-permute-start(bf16[768,768]{1,0:T(8,128)(2,1)S(1)} %get-tuple-element.452), channel_id=1, source_target_pairs={{0,16},{16,0},{1,17},{17,1},{2,18},{18,2},{3,19},{19,3},{4,20},{20... | collective-permute-start | bytes 3538952 | tf_op jit(solution)/shard_map/ppermute | solution.py:64
  398.0 6.2 collective-permute-done.67.refs_1_
  409.4 18.7 %attention_backward.2 = (f32[256,768]{1,0:T(8,128)S(1)}, bf16[256,768]{1,0:T(8,128)(2,1)S(1)}, bf16[256,768]{1,0:T(8,128)(2,1)S(1)}, bf16[128,768]{1,0:T(8,128)(...) custom-call(s32[4]{0:T(128)S(1)} %copy-done.147, ...), custom_call_target="tpu_custom_call" | custom-call | tf_op jit(solution)/shard_map/attention_backward/pallas_call | solution.py:50
  435.0 6.4 collective-permute-start.80
  454.3 4.3 collective-permute-done.77.refs_2_
  472.5 3.9 feed_backward.3
  479.4 3.0 broadcast_select_fusion.7
  482.6 6.1 collective-permute-start.100
  493.1 6.5 collective-permute-done.93.near
  505.3 5.7 collective-permute-done.96.refs_1_
  512.7 3.3 add_convert_fusion
  517.5 19.0 %attention_backward.3 = (f32[256,768]{1,0:T(8,128)S(1)}, bf16[256,768]{1,0:T(8,128)(2,1)S(1)}, bf16[256,768]{1,0:T(8,128)(2,1)S(1)}, bf16[128,768]{1,0:T(8,128)(...) custom-call(s32[4]{0:T(128)S(1)} %copy-done.148, ...), custom_call_target="tpu_custom_call" | custom-call | tf_op jit(solution)/shard_map/attention_backward/pallas_call | solution.py:50
  542.1 3.6 collective-permute-start.114
  554.9 3.2 collective-permute-done.116
  569.5 20.4 %vocab_backward.2.refs_16_ = f32[960,768]{1,0:T(8,128)} custom-call(s32[2]{0:T(128)S(1)} %copy-done.151, bf16[256,768]{1,0:T(8,128)(2,1)} %get-tuple-element.211.refs_0_, bf16[256,768]{1,0:T(8,128)(2,1)S(1)} %collective-permute-done.43.refs_0_.refs_1_, bf16[256,768]{1,0:T(8,128)(2,1)} %collective-permute-done.44.refs_1_.refs_2_, ...), custom_call_target="tpu_custom_call", output_to_operand_aliasing={{}: (24, {})} | custom-call | tf_op jit(solution)/shard_map/vocab_backward/pallas_call | solution.py:544
  594.6 13.8 %all-reduce.12.cloned.1.call-done = (bf16[768,768]{1,0:T(8,128)(2,1)}, bf16[384,768]{0,1:T(8,128)(2,1)}, bf16[768,512]{1,0:T(8,128)(2,1)}) async-done(((bf16[768,768]{1,0:T(8,128)(2,1)}, bf16[384,768]{0,1:T(8,128)(2,1)}, bf16[768,512]{1,0:T(8,128)(2,1)}), (bf16[768,768]{1,0:T(8,128)(2,1)}, bf16[384,768]{0,1:T(8,128)(2,1)}, bf16[768,512]{1,0:T(8,128)(2,1)})) %all-reduce.12.cloned.1.call-update) | async-done | bytes 2555920 | tf_op jit(solution)/shard_map/psum | solution.py:586
  617.4 5.0 collective-permute-done.120.refs_1_
  627.7 20.5 %vocab_backward.3.refs_16_ = f32[960,768]{1,0:T(8,128)} custom-call(s32[2]{0:T(128)S(1)} %fusion.15.first_ref, bf16[256,768]{1,0:T(8,128)(2,1)} %get-tuple-element.211.refs_0_, bf16[256,768]{1,0:T(8,128)(2,1)S(1)} %collective-permute-done.43.refs_0_.refs_1_, ...), custom_call_target="tpu_custom_call", output_to_operand_aliasing={{}: (24, {})} | custom-call | tf_op jit(solution)/shard_map/vocab_backward/pallas_call | solution.py:544
  648.2 40.8 %collective-permute-done.126.refs_0_ = bf16[256,768]{1,0:T(8,128)(2,1)S(1)} collective-permute-done((bf16[256,768]{1,0:T(8,128)(2,1)S(1)}, bf16[256,768]{1,0:T(8,128)(2,1)S(1)}, u32[]{:S(2)}, u32[]{:S(2)}) %collective-permute-start.126) | collective-permute-done | bytes 393248 | tf_op jit(solution)/shard_map/ppermute | solution.py:64
  691.5 3.7 collective-permute-start.42
  696.8 8.3 %collective-permute-done.131.refs_6_ = bf16[256,768]{1,0:T(8,128)(2,1)S(1)} collective-permute-done((bf16[256,768]{1,0:T(8,128)(2,1)S(1)}, bf16[256,768]{1,0:T(8,128)(2,1)S(1)}, u32[]{:S(2)}, u32[]{:S(2)}) %collective-permute-start.131) | collective-permute-done | bytes 393248 | tf_op jit(solution)/shard_map/ppermute | solution.py:64
  706.1 7.8 collective-permute-start.119
  718.5 3.5 collective-permute-done.136.refs_12_
  726.6 2.9 maximum_select_fusion
  729.4 5.1 collective-permute-done.137.refs_13_
  734.6 7.4 embed_backward.6.refs_6_
  742.0 3.5 embed_backward.7
  748.6 2.9 maximum_select_fusion.1
  751.5 7.4 embed_backward.4.refs_6_
  758.9 3.3 embed_backward.5
  770.0 3.4 convert_add_fusion
  776.1 4.3 fusion
  (926 shorter events, 286.5 us)
Async XLA Ops:
  7.2 601.2 %all-reduce.12.cloned.1.call-start = ((), (), s32[]{:S(2)}) async-start(), calls=%async_computation | async-start | bytes 5111808 | tf_op jit(solution)/shard_map/psum | solution.py:586
  12.7 46.8 %collective-permute-start.10 = (f32[3,512,512]{2,1,0:T(8,128)}, f32[3,512,512]{2,1,0:T(8,128)}, u32[]{:S(2)}, u32[]{:S(2)}) collective-permute-start(f32[3,512,512]{2,1,0:T(8,128)} %bitcast.10), channel_id=1, source_target_pairs={{0,16},{16,0},{1,17},{17,1},{2,18},{18,2},{3,19},{19,3},{4,20},{20... | collective-permute-start | bytes 9437192 | tf_op jit(solution)/shard_map/ppermute | solution.py:64
  29.6 22.0 %collective-permute-start.8 = (bf16[768,576]{0,1:T(8,128)(2,1)S(1)}, bf16[768,576]{0,1:T(8,128)(2,1)}, u32[]{:S(2)}, u32[]{:S(2)}) collective-permute-start(bf16[768,576]{0,1:T(8,128)(2,1)S(1)} %bitcast.122), channel_id=1, source_target_pairs={{0,16},{16,0},{1,17},{17,1},{2,18},{18,2},{3,19},{19,3},{4,20},{20... | collective-permute-start | bytes 2654216 | tf_op jit(solution)/shard_map/ppermute | solution.py:64
  33.8 16.0 %collective-permute-start.11 = (bf16[192,768]{1,0:T(8,128)(2,1)}, bf16[192,768]{1,0:T(8,128)(2,1)S(1)}, u32[]{:S(2)}, u32[]{:S(2)}) collective-permute-start(bf16[192,768]{1,0:T(8,128)(2,1)} %bitcast.11), channel_id=1, source_target_pairs={{0,16},{16,0},{1,17},{17,1},{2,18},{18,2},{3,19},{19,3},{4,20},{20... | collective-permute-start | bytes 884744 | tf_op jit(solution)/shard_map/ppermute | solution.py:64
  79.9 20.1 %collective-permute-start.20 = (bf16[768,768]{1,0:T(8,128)(2,1)S(1)}, bf16[768,768]{1,0:T(8,128)(2,1)S(1)}, u32[]{:S(2)}, u32[]{:S(2)}) collective-permute-start(bf16[768,768]{1,0:T(8,128)(2,1)S(1)} %bitcast.114), channel_id=1, source_target_pairs={{0,16},{16,0},{1,17},{17,1},{2,18},{18,2},{3,19},{19,3},{4,20},{20... | collective-permute-start | bytes 3538952 | tf_op jit(solution)/shard_map/ppermute | solution.py:64
  83.1 24.5 %collective-permute-start.21 = (bf16[768,768]{1,0:T(8,128)(2,1)S(1)}, bf16[768,768]{1,0:T(8,128)(2,1)S(1)}, u32[]{:S(2)}, u32[]{:S(2)}) collective-permute-start(bf16[768,768]{1,0:T(8,128)(2,1)S(1)} %bitcast.115), channel_id=1, source_target_pairs={{0,16},{16,0},{1,17},{17,1},{2,18},{18,2},{3,19},{19,3},{4,20},{20... | collective-permute-start | bytes 3538952 | tf_op jit(solution)/shard_map/ppermute | solution.py:64
  83.7 14.0 %collective-permute-start.13 = (bf16[256,768]{1,0:T(8,128)(2,1)S(1)}, bf16[256,768]{1,0:T(8,128)(2,1)S(1)}, u32[]{:S(2)}, u32[]{:S(2)}) collective-permute-start(bf16[256,768]{1,0:T(8,128)(2,1)S(1)} %pad_maximum_fusion.4), channel_id=1, source_target_pairs={{0,1},{1,0},{2,3},{3,2},{4,5},{5,4},{6,7},{7,6},{8,9},{9,8},{10,11... | collective-permute-start | bytes 1179656 | tf_op jit(solution)/shard_map/ppermute | solution.py:64
  214.4 17.9 %collective-permute-start.39 = (bf16[256,768]{1,0:T(8,128)(2,1)}, bf16[256,768]{1,0:T(8,128)(2,1)S(1)}, u32[]{:S(2)}, u32[]{:S(2)}) collective-permute-start(bf16[256,768]{1,0:T(8,128)(2,1)} %pad_maximum_fusion.10), channel_id=1, source_target_pairs={{0,1},{1,0},{2,3},{3,2},{4,5},{5,4},{6,7},{7,6},{8,9},{9,8},{10,11... | collective-permute-start | bytes 1179656 | tf_op jit(solution)/shard_map/ppermute | solution.py:64
  217.7 14.7 %collective-permute-start.41 = (bf16[256,768]{1,0:T(8,128)(2,1)}, bf16[256,768]{1,0:T(8,128)(2,1)}, u32[]{:S(2)}, u32[]{:S(2)}) collective-permute-start(bf16[256,768]{1,0:T(8,128)(2,1)} %pad_maximum_fusion.11), channel_id=1, source_target_pairs={{0,2},{1,3},{2,0},{3,1},{4,6},{5,7},{6,4},{7,5},{8,10},{9,11},{10,... | collective-permute-start | bytes 1179656 | tf_op jit(solution)/shard_map/ppermute | solution.py:64
  249.4 57.3 %collective-permute-start.58 = (bf16[256,768]{1,0:T(8,128)(2,1)}, bf16[256,768]{1,0:T(8,128)(2,1)}, u32[]{:S(2)}, u32[]{:S(2)}) collective-permute-start(bf16[256,768]{1,0:T(8,128)(2,1)} %pad_maximum_fusion.13), channel_id=1, source_target_pairs={{0,2},{1,3},{2,0},{3,1},{4,6},{5,7},{6,4},{7,5},{8,10},{9,11},{10,... | collective-permute-start | bytes 1179656 | tf_op jit(solution)/shard_map/ppermute | solution.py:64
  251.5 20.0 %collective-permute-start.46 = (bf16[128,768]{1,0:T(8,128)(2,1)S(1)}, bf16[128,768]{1,0:T(8,128)(2,1)S(1)}, u32[]{:S(2)}, u32[]{:S(2)}) collective-permute-start(bf16[128,768]{1,0:T(8,128)(2,1)S(1)} %slice.621), channel_id=1, source_target_pairs={{0,1},{1,0},{2,3},{3,2},{4,5},{5,4},{6,7},{7,6},{8,9},{9,8},{10,11... | collective-permute-start | bytes 589832 | tf_op jit(solution)/shard_map/ppermute | solution.py:64
  253.5 43.0 %collective-permute-start.50 = (bf16[128,768]{1,0:T(8,128)(2,1)S(1)}, bf16[128,768]{1,0:T(8,128)(2,1)S(1)}, u32[]{:S(2)}, u32[]{:S(2)}) collective-permute-start(bf16[128,768]{1,0:T(8,128)(2,1)S(1)} %slice.622), channel_id=1, source_target_pairs={{0,2},{1,3},{2,0},{3,1},{4,6},{5,7},{6,4},{7,5},{8,10},{9,11},{10,... | collective-permute-start | bytes 589832 | tf_op jit(solution)/shard_map/ppermute | solution.py:64
  255.0 42.2 %collective-permute-start.51 = (bf16[128,768]{1,0:T(8,128)(2,1)S(1)}, bf16[128,768]{1,0:T(8,128)(2,1)S(1)}, u32[]{:S(2)}, u32[]{:S(2)}) collective-permute-start(bf16[128,768]{1,0:T(8,128)(2,1)S(1)} %slice.623), channel_id=1, source_target_pairs={{0,1},{1,0},{2,3},{3,2},{4,5},{5,4},{6,7},{7,6},{8,9},{9,8},{10,11... | collective-permute-start | bytes 589832 | tf_op jit(solution)/shard_map/ppermute | solution.py:64
  256.6 50.2 %collective-permute-start.56 = (bf16[256,768]{1,0:T(8,128)(2,1)}, bf16[256,768]{1,0:T(8,128)(2,1)}, u32[]{:S(2)}, u32[]{:S(2)}) collective-permute-start(bf16[256,768]{1,0:T(8,128)(2,1)} %pad_maximum_fusion.12), channel_id=1, source_target_pairs={{0,1},{1,0},{2,3},{3,2},{4,5},{5,4},{6,7},{7,6},{8,9},{9,8},{10,11... | collective-permute-start | bytes 1179656 | tf_op jit(solution)/shard_map/ppermute | solution.py:64
  297.9 13.6 %collective-permute-start.52 = (bf16[256,896]{1,0:T(8,128)(2,1)}, bf16[256,896]{1,0:T(8,128)(2,1)}, u32[]{:S(2)}, u32[]{:S(2)}) collective-permute-start(bf16[256,896]{1,0:T(8,128)(2,1)} %get-tuple-element.220), channel_id=1, source_target_pairs={{0,1},{1,0},{2,3},{3,2},{4,5},{5,4},{6,7},{7,6},{8,9},{9,8},{10,11... | collective-permute-start | bytes 1376264 | tf_op jit(solution)/shard_map/ppermute | solution.py:64
  298.7 12.9 %collective-permute-start.53 = (bf16[256,896]{1,0:T(8,128)(2,1)}, bf16[256,896]{1,0:T(8,128)(2,1)}, u32[]{:S(2)}, u32[]{:S(2)}) collective-permute-start(bf16[256,896]{1,0:T(8,128)(2,1)} %get-tuple-element.221), channel_id=1, source_target_pairs={{0,2},{1,3},{2,0},{3,1},{4,6},{5,7},{6,4},{7,5},{8,10},{9,11},{10,... | collective-permute-start | bytes 1376264 | tf_op jit(solution)/shard_map/ppermute | solution.py:64
  299.4 12.2 %collective-permute-start.54 = (bf16[256,896]{1,0:T(8,128)(2,1)}, bf16[256,896]{1,0:T(8,128)(2,1)}, u32[]{:S(2)}, u32[]{:S(2)}) collective-permute-start(bf16[256,896]{1,0:T(8,128)(2,1)} %get-tuple-element.222), channel_id=1, source_target_pairs={{0,3},{1,2},{2,1},{3,0},{4,7},{5,6},{6,5},{7,4},{8,11},{9,10},{10,... | collective-permute-start | bytes 1376264 | tf_op jit(solution)/shard_map/ppermute | solution.py:64
  311.5 11.1 %collective-permute-start.111 = (s32[2,1024]{1,0:T(2,128)S(1)}, s32[2,1024]{1,0:T(2,128)S(1)}, u32[]{:S(2)}, u32[]{:S(2)}) collective-permute-start(s32[2,1024]{1,0:T(2,128)S(1)} %pad_add_fusion.2), channel_id=1, source_target_pairs={{0,4},{4,0},{8,12},{12,8},{1,5},{5,1},{9,13},{13,9},{2,6},{6,2},{1... | collective-permute-start | bytes 24584 | tf_op jit(solution)/shard_map/ppermute | solution.py:64
  316.4 14.2 %collective-permute-start.82 = (bf16[256,768]{1,0:T(8,128)(2,1)}, bf16[256,768]{1,0:T(8,128)(2,1)S(1)}, u32[]{:S(2)}, u32[]{:S(2)}) collective-permute-start(bf16[256,768]{1,0:T(8,128)(2,1)} %get-tuple-element.211.refs_0_), channel_id=1, source_target_pairs={{0,8},{4,12},{8,0},{12,4},{1,9},{5,13},{9,1},{13,5},{2,10},{6,14},... | collective-permute-start | bytes 1179656 | tf_op jit(solution)/shard_map/ppermute | solution.py:64
  317.2 20.4 %collective-permute-start.87 = (bf16[256,768]{1,0:T(8,128)(2,1)}, bf16[256,768]{1,0:T(8,128)(2,1)S(1)}, u32[]{:S(2)}, u32[]{:S(2)}) collective-permute-start(bf16[256,768]{1,0:T(8,128)(2,1)} %get-tuple-element.211.refs_0_), channel_id=1, source_target_pairs={{0,12},{4,8},{8,4},{12,0},{1,13},{5,9},{9,5},{13,1},{2,14},{6,10},... | collective-permute-start | bytes 1179656 | tf_op jit(solution)/shard_map/ppermute | solution.py:64
  321.0 17.0 %collective-permute-start.61 = (bf16[128,768]{1,0:T(8,128)(2,1)S(1)}, bf16[128,768]{1,0:T(8,128)(2,1)S(1)}, u32[]{:S(2)}, u32[]{:S(2)}) collective-permute-start(bf16[128,768]{1,0:T(8,128)(2,1)S(1)} %slice.631), channel_id=1, source_target_pairs={{0,2},{1,3},{2,0},{3,1},{4,6},{5,7},{6,4},{7,5},{8,10},{9,11},{10,... | collective-permute-start | bytes 589832 | tf_op jit(solution)/shard_map/ppermute | solution.py:64
  321.5 17.5 %collective-permute-start.62 = (bf16[128,768]{1,0:T(8,128)(2,1)S(1)}, bf16[128,768]{1,0:T(8,128)(2,1)S(1)}, u32[]{:S(2)}, u32[]{:S(2)}) collective-permute-start(bf16[128,768]{1,0:T(8,128)(2,1)S(1)} %slice.632), channel_id=1, source_target_pairs={{0,1},{1,0},{2,3},{3,2},{4,5},{5,4},{6,7},{7,6},{8,9},{9,8},{10,11... | collective-permute-start | bytes 589832 | tf_op jit(solution)/shard_map/ppermute | solution.py:64
  330.6 51.7 %collective-permute-start.83 = (bf16[256,768]{1,0:T(8,128)(2,1)S(1)}, bf16[256,768]{1,0:T(8,128)(2,1)S(1)}, u32[]{:S(2)}, u32[]{:S(2)}) collective-permute-start(bf16[256,768]{1,0:T(8,128)(2,1)S(1)} %collective-permute-done.82.refs_10_), channel_id=1, source_target_pairs={{0,1},{1,0},{2,3},{3,2},{4,5},{5,4},{6,7},{7,6},{8,9},{9,8},{10,11... | collective-permute-start | bytes 1179656 | tf_op jit(solution)/shard_map/ppermute | solution.py:64
  331.1 52.2 %collective-permute-start.84 = (bf16[256,768]{1,0:T(8,128)(2,1)S(1)}, bf16[256,768]{1,0:T(8,128)(2,1)S(1)}, u32[]{:S(2)}, u32[]{:S(2)}) collective-permute-start(bf16[256,768]{1,0:T(8,128)(2,1)S(1)} %collective-permute-done.82.refs_10_), channel_id=1, source_target_pairs={{0,2},{1,3},{2,0},{3,1},{4,6},{5,7},{6,4},{7,5},{8,10},{9,11},{10,... | collective-permute-start | bytes 1179656 | tf_op jit(solution)/shard_map/ppermute | solution.py:64
  337.5 48.0 %collective-permute-start.88 = (bf16[256,768]{1,0:T(8,128)(2,1)S(1)}, bf16[256,768]{1,0:T(8,128)(2,1)S(1)}, u32[]{:S(2)}, u32[]{:S(2)}) collective-permute-start(bf16[256,768]{1,0:T(8,128)(2,1)S(1)} %collective-permute-done.87.refs_15_), channel_id=1, source_target_pairs={{0,1},{1,0},{2,3},{3,2},{4,5},{5,4},{6,7},{7,6},{8,9},{9,8},{10,11... | collective-permute-start | bytes 1179656 | tf_op jit(solution)/shard_map/ppermute | solution.py:64
  338.0 49.0 %collective-permute-start.89 = (bf16[256,768]{1,0:T(8,128)(2,1)S(1)}, bf16[256,768]{1,0:T(8,128)(2,1)S(1)}, u32[]{:S(2)}, u32[]{:S(2)}) collective-permute-start(bf16[256,768]{1,0:T(8,128)(2,1)S(1)} %collective-permute-done.87.refs_15_), channel_id=1, source_target_pairs={{0,2},{1,3},{2,0},{3,1},{4,6},{5,7},{6,4},{7,5},{8,10},{9,11},{10,... | collective-permute-start | bytes 1179656 | tf_op jit(solution)/shard_map/ppermute | solution.py:64
  353.2 52.8 %collective-permute-start.71 = (bf16[768,768]{1,0:T(8,128)(2,1)S(1)}, bf16[768,768]{1,0:T(8,128)(2,1)S(1)}, u32[]{:S(2)}, u32[]{:S(2)}) collective-permute-start(bf16[768,768]{1,0:T(8,128)(2,1)S(1)} %get-tuple-element.452), channel_id=1, source_target_pairs={{0,16},{16,0},{1,17},{17,1},{2,18},{18,2},{3,19},{19,3},{4,20},{20... | collective-permute-start | bytes 3538952 | tf_op jit(solution)/shard_map/ppermute | solution.py:64
  388.4 57.6 %collective-permute-start.107 = (f32[8,256]{1,0:T(8,128)S(1)}, f32[8,256]{1,0:T(8,128)S(1)}, u32[]{:S(2)}, u32[]{:S(2)}) collective-permute-start(f32[8,256]{1,0:T(8,128)S(1)} %get-tuple-element.311), channel_id=1, source_target_pairs={{0,3},{1,2},{2,1},{3,0},{4,7},{5,6},{6,5},{7,4},{8,11},{9,10},{10,... | collective-permute-start | bytes 24584 | tf_op jit(solution)/shard_map/ppermute | solution.py:64
  397.0 44.8 %collective-permute-start.106 = (f32[8,256]{1,0:T(8,128)S(1)}, f32[8,256]{1,0:T(8,128)S(1)}, u32[]{:S(2)}, u32[]{:S(2)}) collective-permute-start(f32[8,256]{1,0:T(8,128)S(1)} %get-tuple-element.311), channel_id=1, source_target_pairs={{0,2},{1,3},{2,0},{3,1},{4,6},{5,7},{6,4},{7,5},{8,10},{9,11},{10,... | collective-permute-start | bytes 24584 | tf_op jit(solution)/shard_map/ppermute | solution.py:64
  435.0 12.9 %collective-permute-start.80 = (bf16[384,768]{0,1:T(8,128)(2,1)S(1)}, bf16[384,768]{0,1:T(8,128)(2,1)S(1)}, u32[]{:S(2)}, u32[]{:S(2)}) collective-permute-start(bf16[384,768]{0,1:T(8,128)(2,1)S(1)} %fusion.3), channel_id=1, source_target_pairs={{0,16},{16,0},{1,17},{17,1},{2,18},{18,2},{3,19},{19,3},{4,20},{20... | collective-permute-start | bytes 1769480 | tf_op jit(solution)/shard_map/ppermute | solution.py:64
  441.8 20.0 %collective-permute-start.81 = (bf16[768,512]{1,0:T(8,128)(2,1)S(1)}, bf16[768,512]{1,0:T(8,128)(2,1)S(1)}, u32[]{:S(2)}, u32[]{:S(2)}) collective-permute-start(bf16[768,512]{1,0:T(8,128)(2,1)S(1)} %constant_dynamic-slice_fusion.4), channel_id=1, source_target_pairs={{0,16},{16,0},{1,17},{17,1},{2,18},{18,2},{3,19},{19,3},{4,20},{20... | collective-permute-start | bytes 2359304 | tf_op jit(solution)/shard_map/ppermute | solution.py:64
  444.4 15.0 %collective-permute-start.85 = (bf16[128,768]{1,0:T(8,128)(2,1)S(1)}, bf16[128,768]{1,0:T(8,128)(2,1)S(1)}, u32[]{:S(2)}, u32[]{:S(2)}) collective-permute-start(bf16[128,768]{1,0:T(8,128)(2,1)S(1)} %slice.639), channel_id=1, source_target_pairs={{0,2},{1,3},{2,0},{3,1},{4,6},{5,7},{6,4},{7,5},{8,10},{9,11},{10,... | collective-permute-start | bytes 589832 | tf_op jit(solution)/shard_map/ppermute | solution.py:64
  446.0 12.7 %collective-permute-start.77 = (bf16[256,768]{1,0:T(8,128)(2,1)S(1)}, bf16[256,768]{1,0:T(8,128)(2,1)S(1)}, u32[]{:S(2)}, u32[]{:S(2)}) collective-permute-start(bf16[256,768]{1,0:T(8,128)(2,1)S(1)} %get-tuple-element.266.refs_0_), channel_id=1, source_target_pairs={{0,2},{1,3},{2,0},{3,1},{4,6},{5,7},{6,4},{7,5},{8,10},{9,11},{10,... | collective-permute-start | bytes 1179656 | tf_op jit(solution)/shard_map/ppermute | solution.py:64
  447.9 14.9 %collective-permute-start.86 = (bf16[128,768]{1,0:T(8,128)(2,1)}, bf16[128,768]{1,0:T(8,128)(2,1)}, u32[]{:S(2)}, u32[]{:S(2)}) collective-permute-start(bf16[128,768]{1,0:T(8,128)(2,1)} %slice.640), channel_id=1, source_target_pairs={{0,1},{1,0},{2,3},{3,2},{4,5},{5,4},{6,7},{7,6},{8,9},{9,8},{10,11... | collective-permute-start | bytes 589832 | tf_op jit(solution)/shard_map/ppermute | solution.py:64
  452.2 12.2 %collective-permute-start.90 = (bf16[128,768]{1,0:T(8,128)(2,1)}, bf16[128,768]{1,0:T(8,128)(2,1)}, u32[]{:S(2)}, u32[]{:S(2)}) collective-permute-start(bf16[128,768]{1,0:T(8,128)(2,1)} %slice.641), channel_id=1, source_target_pairs={{0,2},{1,3},{2,0},{3,1},{4,6},{5,7},{6,4},{7,5},{8,10},{9,11},{10,... | collective-permute-start | bytes 589832 | tf_op jit(solution)/shard_map/ppermute | solution.py:64
  462.9 26.5 %collective-permute-start.108 = (f32[1,1024]{1,0:T(1,128)}, f32[1,1024]{1,0:T(1,128)S(1)}, u32[]{:S(2)}, u32[]{:S(2)}) collective-permute-start(f32[1,1024]{1,0:T(1,128)} %pad_maximum_fusion.23), channel_id=1, source_target_pairs={{0,4},{4,0},{8,12},{12,8},{1,5},{5,1},{9,13},{13,9},{2,6},{6,2},{1... | collective-permute-start | bytes 12296 | tf_op jit(solution)/shard_map/ppermute | solution.py:64
  464.3 26.8 %collective-permute-start.109 = (f32[1,1024]{1,0:T(1,128)}, f32[1,1024]{1,0:T(1,128)S(1)}, u32[]{:S(2)}, u32[]{:S(2)}) collective-permute-start(f32[1,1024]{1,0:T(1,128)} %pad_maximum_fusion.23), channel_id=1, source_target_pairs={{0,8},{4,12},{8,0},{12,4},{1,9},{5,13},{9,1},{13,5},{2,10},{6,14},... | collective-permute-start | bytes 12296 | tf_op jit(solution)/shard_map/ppermute | solution.py:64
  465.1 100.7 %collective-permute-start.110 = (f32[1,1024]{1,0:T(1,128)}, f32[1,1024]{1,0:T(1,128)}, u32[]{:S(2)}, u32[]{:S(2)}) collective-permute-start(f32[1,1024]{1,0:T(1,128)} %pad_maximum_fusion.23), channel_id=1, source_target_pairs={{0,12},{4,8},{8,4},{12,0},{1,13},{5,9},{9,5},{13,1},{2,14},{6,10},... | collective-permute-start | bytes 12296 | tf_op jit(solution)/shard_map/ppermute | solution.py:64
  476.9 11.9 %collective-permute-start.94 = (bf16[128,768]{1,0:T(8,128)(2,1)S(1)}, bf16[128,768]{1,0:T(8,128)(2,1)S(1)}, u32[]{:S(2)}, u32[]{:S(2)}) collective-permute-start(bf16[128,768]{1,0:T(8,128)(2,1)S(1)} %get-tuple-element.276), channel_id=1, source_target_pairs={{0,1},{1,0},{2,3},{3,2},{4,5},{5,4},{6,7},{7,6},{8,9},{9,8},{10,11... | collective-permute-start | bytes 589832 | tf_op jit(solution)/shard_map/ppermute | solution.py:64
  482.6 30.1 %collective-permute-start.100 = (bf16[768,768]{1,0:T(8,128)(2,1)}, bf16[768,768]{1,0:T(8,128)(2,1)}, u32[]{:S(2)}, u32[]{:S(2)}) collective-permute-start(bf16[768,768]{1,0:T(8,128)(2,1)} %get-tuple-element.454), channel_id=1, source_target_pairs={{0,16},{16,0},{1,17},{17,1},{2,18},{18,2},{3,19},{19,3},{4,20},{20... | collective-permute-start | bytes 3538952 | tf_op jit(solution)/shard_map/ppermute | solution.py:64
  504.6 257.7 %all-reduce.14.cloned.1.call-start = ((), (), s32[]{:S(2)}) async-start(), calls=%async_computation.1 | async-start | bytes 5505024 | tf_op jit(solution)/shard_map/psum | solution.py:586
  536.5 22.3 %collective-permute-start.101 = (bf16[128,768]{1,0:T(8,128)(2,1)}, bf16[128,768]{1,0:T(8,128)(2,1)}, u32[]{:S(2)}, u32[]{:S(2)}) collective-permute-start(bf16[128,768]{1,0:T(8,128)(2,1)} %get-tuple-element.293), channel_id=1, source_target_pairs={{0,2},{1,3},{2,0},{3,1},{4,6},{5,7},{6,4},{7,5},{8,10},{9,11},{10,... | collective-permute-start | bytes 589832 | tf_op jit(solution)/shard_map/ppermute | solution.py:64
  536.5 24.5 %collective-permute-start.103 = (bf16[128,768]{1,0:T(8,128)(2,1)S(1)}, bf16[128,768]{1,0:T(8,128)(2,1)}, u32[]{:S(2)}, u32[]{:S(2)}) collective-permute-start(bf16[128,768]{1,0:T(8,128)(2,1)S(1)} %get-tuple-element.295), channel_id=1, source_target_pairs={{0,1},{1,0},{2,3},{3,2},{4,5},{5,4},{6,7},{7,6},{8,9},{9,8},{10,11... | collective-permute-start | bytes 589832 | tf_op jit(solution)/shard_map/ppermute | solution.py:64
  542.1 47.9 %collective-permute-start.114 = (bf16[384,768]{0,1:T(8,128)(2,1)}, bf16[384,768]{0,1:T(8,128)(2,1)}, u32[]{:S(2)}, u32[]{:S(2)}) collective-permute-start(bf16[384,768]{0,1:T(8,128)(2,1)} %fusion.1), channel_id=1, source_target_pairs={{0,16},{16,0},{1,17},{17,1},{2,18},{18,2},{3,19},{19,3},{4,20},{20... | collective-permute-start | bytes 1769480 | tf_op jit(solution)/shard_map/ppermute | solution.py:64
  558.0 34.1 %collective-permute-start.115 = (bf16[768,512]{1,0:T(8,128)(2,1)}, bf16[768,512]{1,0:T(8,128)(2,1)}, u32[]{:S(2)}, u32[]{:S(2)}) collective-permute-start(bf16[768,512]{1,0:T(8,128)(2,1)} %constant_dynamic-slice_fusion.1), channel_id=1, source_target_pairs={{0,16},{16,0},{1,17},{17,1},{2,18},{18,2},{3,19},{19,3},{4,20},{20... | collective-permute-start | bytes 2359304 | tf_op jit(solution)/shard_map/ppermute | solution.py:64
  561.0 29.0 %collective-permute-start.102 = (bf16[256,768]{1,0:T(8,128)(2,1)}, bf16[256,768]{1,0:T(8,128)(2,1)}, u32[]{:S(2)}, u32[]{:S(2)}) collective-permute-start(bf16[256,768]{1,0:T(8,128)(2,1)} %pad_maximum_fusion.20), channel_id=1, source_target_pairs={{0,1},{1,0},{2,3},{3,2},{4,5},{5,4},{6,7},{7,6},{8,9},{9,8},{10,11... | collective-permute-start | bytes 1179656 | tf_op jit(solution)/shard_map/ppermute | solution.py:64
  564.4 25.6 %collective-permute-start.104 = (bf16[256,768]{1,0:T(8,128)(2,1)}, bf16[256,768]{1,0:T(8,128)(2,1)}, u32[]{:S(2)}, u32[]{:S(2)}) collective-permute-start(bf16[256,768]{1,0:T(8,128)(2,1)} %pad_maximum_fusion.21), channel_id=1, source_target_pairs={{0,2},{1,3},{2,0},{3,1},{4,6},{5,7},{6,4},{7,5},{8,10},{9,11},{10,... | collective-permute-start | bytes 1179656 | tf_op jit(solution)/shard_map/ppermute | solution.py:64
  565.8 24.1 %collective-permute-start.118 = (f32[2,18,768]{2,1,0:T(8,128)S(1)}, f32[2,18,768]{2,1,0:T(8,128)S(1)}, u32[]{:S(2)}, u32[]{:S(2)}) collective-permute-start(f32[2,18,768]{2,1,0:T(8,128)S(1)} %fusion.55), channel_id=1, source_target_pairs={{0,16},{16,0},{1,17},{17,1},{2,18},{18,2},{3,19},{19,3},{4,20},{20... | collective-permute-start | bytes 331784 | tf_op jit(solution)/shard_map/ppermute | solution.py:64
  614.7 33.4 %collective-permute-start.124 = (bf16[256,768]{1,0:T(8,128)(2,1)S(1)}, bf16[256,768]{1,0:T(8,128)(2,1)S(1)}, u32[]{:S(2)}, u32[]{:S(2)}) collective-permute-start(bf16[256,768]{1,0:T(8,128)(2,1)S(1)} %get-tuple-element.340.refs_0_), channel_id=1, source_target_pairs={{0,4},{4,0},{8,12},{12,8},{1,5},{5,1},{9,13},{13,9},{2,6},{6,2},{1... | collective-permute-start | bytes 1179656 | tf_op jit(solution)/shard_map/ppermute | solution.py:64
  615.1 33.1 %collective-permute-start.125 = (bf16[256,768]{1,0:T(8,128)(2,1)S(1)}, bf16[256,768]{1,0:T(8,128)(2,1)}, u32[]{:S(2)}, u32[]{:S(2)}) collective-permute-start(bf16[256,768]{1,0:T(8,128)(2,1)S(1)} %get-tuple-element.340.refs_0_), channel_id=1, source_target_pairs={{0,8},{4,12},{8,0},{12,4},{1,9},{5,13},{9,1},{13,5},{2,10},{6,14},... | collective-permute-start | bytes 1179656 | tf_op jit(solution)/shard_map/ppermute | solution.py:64
  615.9 73.1 %collective-permute-start.126 = (bf16[256,768]{1,0:T(8,128)(2,1)S(1)}, bf16[256,768]{1,0:T(8,128)(2,1)S(1)}, u32[]{:S(2)}, u32[]{:S(2)}) collective-permute-start(bf16[256,768]{1,0:T(8,128)(2,1)S(1)} %get-tuple-element.340.refs_0_), channel_id=1, source_target_pairs={{0,12},{4,8},{8,4},{12,0},{1,13},{5,9},{9,5},{13,1},{2,14},{6,10},... | collective-permute-start | bytes 1179656 | tf_op jit(solution)/shard_map/ppermute | solution.py:64
  622.3 66.7 %collective-permute-start.122 = (bf16[128,768]{1,0:T(8,128)(2,1)S(1)}, bf16[128,768]{1,0:T(8,128)(2,1)S(1)}, u32[]{:S(2)}, u32[]{:S(2)}) collective-permute-start(bf16[128,768]{1,0:T(8,128)(2,1)S(1)} %slice.653), channel_id=1, source_target_pairs={{0,2},{1,3},{2,0},{3,1},{4,6},{5,7},{6,4},{7,5},{8,10},{9,11},{10,... | collective-permute-start | bytes 589832 | tf_op jit(solution)/shard_map/ppermute | solution.py:64
  624.4 64.6 %collective-permute-start.123 = (bf16[128,768]{1,0:T(8,128)(2,1)S(1)}, bf16[128,768]{1,0:T(8,128)(2,1)S(1)}, u32[]{:S(2)}, u32[]{:S(2)}) collective-permute-start(bf16[128,768]{1,0:T(8,128)(2,1)S(1)} %slice.654), channel_id=1, source_target_pairs={{0,1},{1,0},{2,3},{3,2},{4,5},{5,4},{6,7},{7,6},{8,9},{9,8},{10,11... | collective-permute-start | bytes 589832 | tf_op jit(solution)/shard_map/ppermute | solution.py:64
  689.1 15.9 %collective-permute-start.131 = (bf16[256,768]{1,0:T(8,128)(2,1)S(1)}, bf16[256,768]{1,0:T(8,128)(2,1)S(1)}, u32[]{:S(2)}, u32[]{:S(2)}) collective-permute-start(bf16[256,768]{1,0:T(8,128)(2,1)S(1)} %collective-permute-done.124.refs_5_), channel_id=1, source_target_pairs={{0,1},{1,0},{2,3},{3,2},{4,5},{5,4},{6,7},{7,6},{8,9},{9,8},{10,11... | collective-permute-start | bytes 1179656 | tf_op jit(solution)/shard_map/ppermute | solution.py:64
  691.5 31.7 %collective-permute-start.42 = (f32[256,768]{1,0:T(8,128)}, f32[256,768]{1,0:T(8,128)}, u32[]{:S(2)}, u32[]{:S(2)}) collective-permute-start(f32[256,768]{1,0:T(8,128)} %broadcast_select_fusion.20), channel_id=1, source_target_pairs={{0,16},{16,0},{1,17},{17,1},{2,18},{18,2},{3,19},{19,3},{4,20},{20... | collective-permute-start | bytes 2359304 | tf_op jit(solution)/shard_map/ppermute | solution.py:64
  695.2 19.3 %collective-permute-start.128 = (bf16[256,768]{1,0:T(8,128)(2,1)S(1)}, bf16[256,768]{1,0:T(8,128)(2,1)}, u32[]{:S(2)}, u32[]{:S(2)}) collective-permute-start(bf16[256,768]{1,0:T(8,128)(2,1)S(1)} %collective-permute-done.126.refs_0_), channel_id=1, source_target_pairs={{0,2},{1,3},{2,0},{3,1},{4,6},{5,7},{6,4},{7,5},{8,10},{9,11},{10,... | collective-permute-start | bytes 1179656 | tf_op jit(solution)/shard_map/ppermute | solution.py:64
  696.7 19.7 %collective-permute-start.135 = (bf16[256,768]{1,0:T(8,128)(2,1)}, bf16[256,768]{1,0:T(8,128)(2,1)}, u32[]{:S(2)}, u32[]{:S(2)}) collective-permute-start(bf16[256,768]{1,0:T(8,128)(2,1)} %collective-permute-done.125.refs_10_), channel_id=1, source_target_pairs={{0,1},{1,0},{2,3},{3,2},{4,5},{5,4},{6,7},{7,6},{8,9},{9,8},{10,11... | collective-permute-start | bytes 1179656 | tf_op jit(solution)/shard_map/ppermute | solution.py:64
  705.0 17.0 %collective-permute-start.136 = (bf16[256,768]{1,0:T(8,128)(2,1)}, bf16[256,768]{1,0:T(8,128)(2,1)}, u32[]{:S(2)}, u32[]{:S(2)}) collective-permute-start(bf16[256,768]{1,0:T(8,128)(2,1)} %collective-permute-done.125.refs_10_), channel_id=1, source_target_pairs={{0,2},{1,3},{2,0},{3,1},{4,6},{5,7},{6,4},{7,5},{8,10},{9,11},{10,... | collective-permute-start | bytes 1179656 | tf_op jit(solution)/shard_map/ppermute | solution.py:64
  706.1 42.5 %collective-permute-start.119 = (f32[256,768]{1,0:T(8,128)}, f32[256,768]{1,0:T(8,128)}, u32[]{:S(2)}, u32[]{:S(2)}) collective-permute-start(f32[256,768]{1,0:T(8,128)} %broadcast_select_fusion.19), channel_id=1, source_target_pairs={{0,16},{16,0},{1,17},{17,1},{2,18},{18,2},{3,19},{19,3},{4,20},{20... | collective-permute-start | bytes 2359304 | tf_op jit(solution)/shard_map/ppermute | solution.py:64
  714.6 11.5 %collective-permute-start.133 = (bf16[128,768]{1,0:T(8,128)(2,1)}, bf16[128,768]{1,0:T(8,128)(2,1)S(1)}, u32[]{:S(2)}, u32[]{:S(2)}) collective-permute-start(bf16[128,768]{1,0:T(8,128)(2,1)} %slice.658), channel_id=1, source_target_pairs={{0,2},{1,3},{2,0},{3,1},{4,6},{5,7},{6,4},{7,5},{8,10},{9,11},{10,... | collective-permute-start | bytes 589832 | tf_op jit(solution)/shard_map/ppermute | solution.py:64
  722.0 20.0 %collective-permute-start.129 = (bf16[128,768]{1,0:T(8,128)(2,1)S(1)}, bf16[128,768]{1,0:T(8,128)(2,1)S(1)}, u32[]{:S(2)}, u32[]{:S(2)}) collective-permute-start(bf16[128,768]{1,0:T(8,128)(2,1)S(1)} %slice.655), channel_id=1, source_target_pairs={{0,2},{1,3},{2,0},{3,1},{4,6},{5,7},{6,4},{7,5},{8,10},{9,11},{10,... | collective-permute-start | bytes 589832 | tf_op jit(solution)/shard_map/ppermute | solution.py:64
  723.3 18.7 %collective-permute-start.130 = (bf16[128,768]{1,0:T(8,128)(2,1)S(1)}, bf16[128,768]{1,0:T(8,128)(2,1)S(1)}, u32[]{:S(2)}, u32[]{:S(2)}) collective-permute-start(bf16[128,768]{1,0:T(8,128)(2,1)S(1)} %slice.656), channel_id=1, source_target_pairs={{0,1},{1,0},{2,3},{3,2},{4,5},{5,4},{6,7},{7,6},{8,9},{9,8},{10,11... | collective-permute-start | bytes 589832 | tf_op jit(solution)/shard_map/ppermute | solution.py:64
  746.8 23.2 %collective-permute-start.139 = (bf16[960,768]{1,0:T(8,128)(2,1)}, bf16[960,768]{1,0:T(8,128)(2,1)}, u32[]{:S(2)}, u32[]{:S(2)}) collective-permute-start(bf16[960,768]{1,0:T(8,128)(2,1)} %convert_element_type.405), channel_id=1, source_target_pairs={{0,16},{16,0},{1,17},{17,1},{2,18},{18,2},{3,19},{19,3},{4,20},{20... | collective-permute-start | bytes 4423688 | tf_op jit(solution)/shard_map/ppermute | solution.py:64
  768.1 12.3 %collective-permute-start.141 = (bf16[768,768]{1,0:T(8,128)(2,1)S(1)}, bf16[768,768]{1,0:T(8,128)(2,1)S(1)}, u32[]{:S(2)}, u32[]{:S(2)}) collective-permute-start(bf16[768,768]{1,0:T(8,128)(2,1)S(1)} %broadcast_select_fusion.6), channel_id=1, source_target_pairs={{0,16},{16,0},{1,17},{17,1},{2,18},{18,2},{3,19},{19,3},{4,20},{20... | collective-permute-start | bytes 3538952 | tf_op jit(solution)/shard_map/ppermute | solution.py:64
  (302 other events, 2920.8 us)
Sparse Core Ops, SparseCore 0:
  504.7 103.5 all-reduce.11
  611.7 139.5 all-reduce.13
